TPU v7x, 128 devices: a whole 4x4x4 slice. The times are simulated.
128 devices in a mesh: expert: 32 (over z, y, core), tensor: 4 (over x).
Axes of the slice: x: 4, y: 4, z: 4, core: 2. Of those that a mesh axis runs over, the one named last changes fastest.
Arguments:
- inputs: bfloat16 [16384, 2048], P(('expert', 'tensor')), may hold values from -6 to 6
- attn_gain: float32 [2048], replicated, may hold values from 0.25 to 1.75
- w_query: bfloat16 [2048, 4096], P(None, 'tensor'), may hold values from -0.125 to 0.125
- w_key: bfloat16 [2048, 512], P(None, 'tensor'), may hold values from -0.125 to 0.125
- w_value: bfloat16 [2048, 512], P(None, 'tensor'), may hold values from -0.125 to 0.125
- q_gain: float32 [128], replicated, may hold values from 0.25 to 1.75
- k_gain: float32 [128], replicated, may hold values from 0.25 to 1.75
- w_out: bfloat16 [4096, 2048], P('tensor'), may hold values from -0.75 to 0.75
- mlp_gain: float32 [2048], replicated, may hold values from 0.25 to 1.75
- w_router: bfloat16 [2048, 64], replicated, may hold values from -0.0625 to 0.0625
- w_gate: bfloat16 [64, 2048, 768], P('expert', None, 'tensor'), may hold values from -0.125 to 0.125
- w_up: bfloat16 [64, 2048, 768], P('expert', None, 'tensor'), may hold values from -0.125 to 0.125
- w_down: bfloat16 [64, 768, 2048], P('expert', 'tensor'), may hold values from -0.875 to 0.875
- routes: int32 [16384, 8], P(('expert', 'tensor')), may hold values from 0 to 63, all different within a row; in each aligned block of 128 rows (0 to 127, 128 to 255, ...) at most 20 rows name the same one
- grad_out: bfloat16 [16384, 2048], P(('expert', 'tensor')), may hold values from -6 to 6
Outputs:
- output: bfloat16 [16384, 2048], P(('expert', 'tensor'))
- grad_inputs: bfloat16 [16384, 2048], P(('expert', 'tensor'))
- grad_attn_gain: float32 [2048], replicated
- grad_w_query: float32 [2048, 4096], P(None, 'tensor')
- grad_w_key: float32 [2048, 512], P(None, 'tensor')
- grad_w_value: float32 [2048, 512], P(None, 'tensor')
- grad_q_gain: float32 [128], replicated
- grad_k_gain: float32 [128], replicated
- grad_w_out: float32 [4096, 2048], P('tensor')
- grad_mlp_gain: float32 [2048], replicated
- grad_w_router: float32 [2048, 64], replicated
- grad_w_gate: float32 [64, 2048, 768], P('expert', None, 'tensor')
- grad_w_up: float32 [64, 2048, 768], P('expert', None, 'tensor')
- grad_w_down: float32 [64, 768, 2048], P('expert', 'tensor')
Inputs may be any that keep to these rules, and one draw needn't show every extreme that they name: `routes`: each row names 8 different experts. Among the 128 rows of one device no expert is named more than 20 times, and in every draw some expert is named exactly 20 times by the rows of some device.
All inputs are finite; a program needn't handle non-finite values.
Results may differ from a plain program's by a relative error of at most 0.025.
Values may be sent and summed in bfloat16 or wider, within the bound.
A program may use at most 384 MiB of HBM per device.

v0:
```python
import jax
import jax.numpy as jnp
from jax import lax
from jax.sharding import PartitionSpec as P

EPSILON = 1e-06
ROPE_BASE = 1000000.0
MASK_VALUE = -1e30


def laid_out(parts, dim):
    dims = list(parts.shape[1:])
    dims[dim] *= parts.shape[0]
    return jnp.moveaxis(parts, 0, dim).reshape(dims)


def sent_to_all(x, axis):
    peers = lax.axis_size(axis)
    return lax.all_to_all(jnp.broadcast_to(x[None], (peers, *x.shape)), axis, 0, 0, tiled=True)


def gather_directly(x, axis, dim):
    return laid_out(sent_to_all(x, axis), dim)


def in_blocks(x, dim, peers):
    before, after = (x.shape[:dim], x.shape[dim + 1 :])
    return jnp.moveaxis(x.reshape(*before, peers, -1, *after), dim, 0)


def sent_and_summed(x, axis, dim):
    peers = lax.axis_size(axis)
    parts = lax.all_to_all(in_blocks(x, dim, peers), axis, 0, 0, tiled=True)
    return jnp.sum(parts.astype(jnp.float32), axis=0)


def turned_gather(arrays, axis, dims):
    turned = [jnp.moveaxis(a, dim, 0) for a, dim in zip(arrays, dims)]
    both = jnp.concatenate([t.reshape(len(t), -1) for t in turned], axis=1)
    filled, at, done = (lax.all_gather(both, axis, axis=0, tiled=True), 0, [])
    for t, dim in zip(turned, dims):
        section = filled[:, at : at + t[0].size].reshape(-1, *t.shape[1:])
        done.append(jnp.moveaxis(section, 0, dim))
        at += t[0].size
    return tuple(done)


def angles(length, head_size):
    position = jnp.arange(length, dtype=jnp.float32)[:, None]
    index_half = jnp.arange(head_size // 2, dtype=jnp.float32)[None, :]
    frequency = jnp.exp(index_half * (-2.0 / head_size) * jnp.log(ROPE_BASE))
    turned = position * frequency
    turned = jnp.concatenate([turned, turned], axis=1)
    return (jnp.cos(turned)[:, None, :], jnp.sin(turned)[:, None, :])


def rotate(values, cosine, sine):
    halfway = values.shape[-1] // 2
    turned = jnp.concatenate([-values[..., halfway:], values[..., :halfway]], axis=-1)
    return values * cosine + turned * sine


def rotate_back(grads, cosine, sine):
    halfway = grads.shape[-1] // 2
    along = grads * sine
    return grads * cosine + jnp.concatenate([along[..., halfway:], -along[..., :halfway]], axis=-1)


def inverse_rms(values):
    return lax.rsqrt(jnp.mean(values * values, axis=-1, keepdims=True) + EPSILON)


def norm_back(values, scales, gain, grads):
    weighted = grads * gain
    return scales * weighted - values * scales * scales * scales * jnp.mean(
        weighted * values, axis=-1, keepdims=True
    )


def per_device(
    inputs,
    attn_gain,
    w_query,
    w_key,
    w_value,
    q_gain,
    k_gain,
    w_out,
    mlp_gain,
    w_router,
    w_gate,
    w_up,
    w_down,
    routes,
    grad_out,
):
    f32 = jnp.float32
    bf16 = jnp.bfloat16
    row_count = inputs.shape[0]
    model_width = inputs.shape[1]
    head_size = q_gain.shape[0]
    expert_count = w_router.shape[1]
    local_experts = w_gate.shape[0]
    top_count = routes.shape[1]
    group_count = lax.axis_size("expert")
    capacity = 5 * row_count * top_count // (4 * expert_count)
    query_heads = w_query.shape[1] // head_size
    key_heads = w_key.shape[1] // head_size
    group_size = query_heads // key_heads
    scale_factor = head_size ** (-0.5)
    float_in = inputs.astype(f32)
    first_scale = inverse_rms(float_in)
    normed = (float_in * first_scale * attn_gain).astype(bf16)
    seq_rows = gather_directly(normed, "tensor", 0)
    length = seq_rows.shape[0]
    queries = jnp.dot(seq_rows, w_query, preferred_element_type=f32).reshape(
        length, query_heads, head_size
    )
    keys_raw = jnp.dot(seq_rows, w_key, preferred_element_type=f32).reshape(
        length, key_heads, head_size
    )
    values_low = (
        jnp.dot(seq_rows, w_value, preferred_element_type=f32)
        .astype(bf16)
        .reshape(length, key_heads, head_size)
    )
    cosine, sine = angles(length, head_size)
    query_scale = inverse_rms(queries)
    key_scale = inverse_rms(keys_raw)
    query_rot = rotate(queries * query_scale * q_gain, cosine, sine).astype(bf16)
    key_rot = rotate(keys_raw * key_scale * k_gain, cosine, sine).astype(bf16)
    query_group = query_rot.reshape(length, key_heads, group_size, head_size)
    causal = jnp.arange(length)[:, None] >= jnp.arange(length)[None, :]
    scores = (
        jnp.einsum("skgd,tkd->kgst", query_group, key_rot, preferred_element_type=f32)
        * scale_factor
    )
    scores = jnp.where(causal, scores, MASK_VALUE)
    row_peak = jnp.max(scores, axis=-1, keepdims=True)
    exp_scores = jnp.exp(scores - row_peak)
    denominator = jnp.sum(exp_scores, axis=-1, keepdims=True)
    attn_probs = exp_scores / denominator
    log_norm = row_peak + jnp.log(denominator)
    context = jnp.einsum(
        "kgst,tkd->skgd", attn_probs.astype(bf16), values_low, preferred_element_type=f32
    )
    context = context.reshape(length, query_heads * head_size).astype(bf16)
    attended = sent_and_summed(
        jnp.dot(context, w_out, preferred_element_type=f32).astype(jnp.bfloat16), "tensor", 0
    )
    hidden = float_in + attended
    second_scale = inverse_rms(hidden)
    mixed_in = (hidden * second_scale * mlp_gain).astype(bf16)
    logits = jnp.dot(mixed_in, w_router, preferred_element_type=f32)
    router_peak = jnp.max(logits, axis=-1, keepdims=True)
    router_exp = jnp.exp(logits - router_peak)
    router_probs = router_exp / jnp.sum(router_exp, axis=-1, keepdims=True)
    chosen = routes[:, :, None] == jnp.arange(expert_count, dtype=jnp.int32)[None, None, :]
    chosen_float = chosen.astype(f32)
    picked = jnp.sum(chosen_float * router_probs[:, None, :], axis=-1)
    picked_total = jnp.sum(picked, axis=-1, keepdims=True)
    gate_values = picked / picked_total
    flat_onehot = chosen.reshape(row_count * top_count, expert_count).astype(jnp.int32)
    slot_index = jnp.sum(flat_onehot * (jnp.cumsum(flat_onehot, axis=0) - 1), axis=1)
    target = routes.reshape(-1) * capacity + slot_index
    repeated = jnp.repeat(mixed_in, top_count, axis=0)
    send_buffer = jnp.zeros((expert_count * capacity, model_width), bf16).at[target].set(repeated)
    send_buffer = send_buffer.reshape(group_count, local_experts, capacity, model_width)
    arrived = lax.all_to_all(send_buffer, "expert", split_axis=0, concat_axis=0, tiled=True)
    full_gate, full_up, full_down = turned_gather((w_gate, w_up, w_down), "tensor", (2, 2, 1))
    gate_pre = jnp.einsum("sxcd,xdf->sxcf", arrived, full_gate, preferred_element_type=f32)
    up_pre = jnp.einsum("sxcd,xdf->sxcf", arrived, full_up, preferred_element_type=f32)
    sigmoid = 1.0 / (1.0 + jnp.exp(-gate_pre))
    activated = gate_pre * sigmoid
    middle = (activated * up_pre).astype(bf16)
    produced = jnp.einsum("sxcf,xfd->sxcd", middle, full_down, preferred_element_type=f32)
    expert_out = produced.astype(bf16)
    returned = lax.all_to_all(
        expert_out, "expert", split_axis=0, concat_axis=0, tiled=True
    ).reshape(expert_count * capacity, model_width)
    row_out = returned[target].reshape(row_count, top_count, model_width).astype(f32)
    expert_mix = jnp.sum(gate_values[:, :, None] * row_out, axis=1)
    output = (hidden + expert_mix).astype(bf16)
    dout = grad_out.astype(f32)
    gate_grad = jnp.sum(dout[:, None, :] * row_out, axis=-1)
    row_grad = (
        (gate_values[:, :, None] * dout[:, None, :])
        .astype(bf16)
        .reshape(row_count * top_count, model_width)
    )
    grad_buffer = jnp.zeros((expert_count * capacity, model_width), bf16).at[target].set(row_grad)
    grad_buffer = grad_buffer.reshape(group_count, local_experts, capacity, model_width)
    grad_arrived = lax.all_to_all(grad_buffer, "expert", split_axis=0, concat_axis=0, tiled=True)
    grad_mid = jnp.einsum("sxcd,xfd->sxcf", grad_arrived, full_down, preferred_element_type=f32)
    grad_gate_pre = (grad_mid * up_pre * sigmoid * (1.0 + gate_pre * (1.0 - sigmoid))).astype(bf16)
    grad_up_pre = (grad_mid * activated).astype(bf16)
    grad_down_w = jnp.einsum("sxcf,sxcd->xfd", middle, grad_arrived, preferred_element_type=f32)
    grad_gate_w = jnp.einsum("sxcd,sxcf->xdf", arrived, grad_gate_pre, preferred_element_type=f32)
    grad_up_w = jnp.einsum("sxcd,sxcf->xdf", arrived, grad_up_pre, preferred_element_type=f32)
    row_back = jnp.einsum("sxcf,xdf->sxcd", grad_gate_pre, full_gate, preferred_element_type=f32)
    row_back = row_back + jnp.einsum(
        "sxcf,xdf->sxcd", grad_up_pre, full_up, preferred_element_type=f32
    )
    grad_gate_w, grad_up_w, grad_down_w = (
        lax.psum_scatter(
            grad_gate_w.astype(jnp.bfloat16), "tensor", scatter_dimension=2, tiled=True
        ).astype(jnp.float32),
        lax.psum_scatter(
            grad_up_w.astype(jnp.bfloat16), "tensor", scatter_dimension=2, tiled=True
        ).astype(jnp.float32),
        lax.psum_scatter(
            grad_down_w.astype(jnp.bfloat16), "tensor", scatter_dimension=1, tiled=True
        ).astype(jnp.float32),
    )
    row_back = row_back.astype(bf16)
    grad_returned = lax.all_to_all(
        row_back, "expert", split_axis=0, concat_axis=0, tiled=True
    ).reshape(expert_count * capacity, model_width)
    grad_mixed = jnp.sum(
        grad_returned[target].reshape(row_count, top_count, model_width).astype(f32), axis=1
    )
    picked_grad = (
        gate_grad - jnp.sum(gate_grad * gate_values, axis=-1, keepdims=True)
    ) / picked_total
    prob_grad = jnp.sum(chosen_float * picked_grad[:, :, None], axis=1)
    logit_grad = (
        router_probs * (prob_grad - jnp.sum(prob_grad * router_probs, axis=-1, keepdims=True))
    ).astype(bf16)
    grad_router = jnp.dot(mixed_in.T, logit_grad, preferred_element_type=f32)
    grad_mixed = grad_mixed + jnp.dot(logit_grad, w_router.T, preferred_element_type=f32)
    grad_hidden = dout + norm_back(hidden, second_scale, mlp_gain, grad_mixed)
    mlp_gain_grad = jnp.sum(grad_mixed * hidden * second_scale, axis=0)
    grad_att = grad_hidden.astype(bf16)
    grad_seq_rows = gather_directly(grad_att, "tensor", 0)
    grad_out_w = jnp.dot(context.T, grad_seq_rows, preferred_element_type=f32)
    grad_context = jnp.dot(grad_seq_rows, w_out.T, preferred_element_type=f32).astype(bf16)
    grad_context = grad_context.reshape(length, key_heads, group_size, head_size)
    again = (
        jnp.einsum("skgd,tkd->kgst", query_group, key_rot, preferred_element_type=f32)
        * scale_factor
    )
    again = jnp.where(causal, again, MASK_VALUE)
    probs_again = jnp.exp(again - log_norm)
    grad_probs = jnp.einsum("skgd,tkd->kgst", grad_context, values_low, preferred_element_type=f32)
    grad_values = jnp.einsum(
        "kgst,skgd->tkd", probs_again.astype(bf16), grad_context, preferred_element_type=f32
    )
    grad_values = grad_values.astype(bf16).reshape(length, key_heads * head_size)
    grad_scores = probs_again * (
        grad_probs - jnp.sum(grad_probs * probs_again, axis=-1, keepdims=True)
    )
    grad_scores = grad_scores.astype(bf16)
    grad_query_rot = (
        jnp.einsum("kgst,tkd->skgd", grad_scores, key_rot, preferred_element_type=f32)
        * scale_factor
    )
    grad_key_rot = (
        jnp.einsum("kgst,skgd->tkd", grad_scores, query_group, preferred_element_type=f32)
        * scale_factor
    )
    grad_q_norm = rotate_back(grad_query_rot.reshape(length, query_heads, head_size), cosine, sine)
    grad_k_norm = rotate_back(grad_key_rot, cosine, sine)
    q_gain_grad = jnp.sum(grad_q_norm * queries * query_scale, axis=(0, 1))
    k_gain_grad = jnp.sum(grad_k_norm * keys_raw * key_scale, axis=(0, 1))
    grad_queries = (
        norm_back(queries, query_scale, q_gain, grad_q_norm)
        .astype(bf16)
        .reshape(length, query_heads * head_size)
    )
    grad_keys = (
        norm_back(keys_raw, key_scale, k_gain, grad_k_norm)
        .astype(bf16)
        .reshape(length, key_heads * head_size)
    )
    grad_query_w = jnp.dot(seq_rows.T, grad_queries, preferred_element_type=f32)
    grad_key_w = jnp.dot(seq_rows.T, grad_keys, preferred_element_type=f32)
    grad_value_w = jnp.dot(seq_rows.T, grad_values, preferred_element_type=f32)
    summed = jnp.dot(grad_queries, w_query.T, preferred_element_type=f32)
    summed = summed + jnp.dot(grad_keys, w_key.T, preferred_element_type=f32)
    grad_normed = sent_and_summed(
        (summed + jnp.dot(grad_values, w_value.T, preferred_element_type=f32)).astype(jnp.bfloat16),
        "tensor",
        0,
    )
    grad_inputs = (grad_hidden + norm_back(float_in, first_scale, attn_gain, grad_normed)).astype(
        bf16
    )
    attn_gain_grad = jnp.sum(grad_normed * float_in * first_scale, axis=0)
    weight_totals = (
        lax.psum(grad_query_w.astype(jnp.bfloat16), "expert").astype(jnp.float32),
        lax.psum(grad_key_w.astype(jnp.bfloat16), "expert").astype(jnp.float32),
        lax.psum(grad_value_w.astype(jnp.bfloat16), "expert").astype(jnp.float32),
        lax.psum(grad_out_w.astype(jnp.bfloat16), "expert").astype(jnp.float32),
    )
    small_totals = lax.psum(
        (grad_router, attn_gain_grad, q_gain_grad, k_gain_grad, mlp_gain_grad), ("expert", "tensor")
    )
    return (
        output,
        grad_inputs,
        small_totals[1],
        weight_totals[0],
        weight_totals[1],
        weight_totals[2],
        small_totals[2],
        small_totals[3],
        weight_totals[3],
        small_totals[4],
        small_totals[0],
        grad_gate_w,
        grad_up_w,
        grad_down_w,
    )


def solution(mesh):
    placed = (
        P(("expert", "tensor"), None),
        P(),
        P(None, "tensor"),
        P(None, "tensor"),
        P(None, "tensor"),
        P(),
        P(),
        P("tensor", None),
        P(),
        P(),
        P("expert", None, "tensor"),
        P("expert", None, "tensor"),
        P("expert", "tensor", None),
        P(("expert", "tensor"), None),
        P(("expert", "tensor"), None),
    )
    return jax.shard_map(
        per_device,
        mesh=mesh,
        in_specs=placed,
        out_specs=(
            P(("expert", "tensor"), None),
            P(("expert", "tensor"), None),
            P(),
            P(None, "tensor"),
            P(None, "tensor"),
            P(None, "tensor"),
            P(),
            P(),
            P("tensor", None),
            P(),
            P(),
            P("expert", None, "tensor"),
            P("expert", None, "tensor"),
            P("expert", "tensor", None),
        ),
        check_vma=False,
    )
```

profile of v0, /device:TPU:1, one launch (start us, length us, event | category | flops | bytes accessed | tf_op | source)
XLA Modules:
  0.0 1090.9 jit_solution(11070851148304388479)
XLA Ops:
  19.9 6.5 copy.223
  27.3 26.9 %all-to-all-done = bf16[4,128,2048]{2,1,0:T(8,128)(2,1)S(1)} async-done(((bf16[4,128,2048]{2,1,0:T(8,128)(2,1)}), bf16[4,128,2048]{2,1,0:T(8,128)(2,1)S(1)}, u32[]{:S(2)}, u32[]{:S(2)}) %all-to-all-start) | async-done | bytes 2097184 | tf_op jit(solution)/shard_map/all_to_all | solution.py:19
  79.7 31.1 %reduce-window.6 = s32[64,8,128]{2,1,0:T(8,128)S(1)} reduce-window(s32[64,8,128]{2,1,0:T(8,128)} %fusion.85, s32[]{:T(128)} %constant.47.clone.1), window={size=1x1x128 pad=0_0x0_0x127_0}, to_apply=%region_11.12 | reduce-window | flops 8323072 | bytes 524292 | tf_op jit(solution)/shard_map/reduce-window
  113.1 12.8 %all-to-all-done.1 = bf16[4,128,2048]{2,1,0:T(8,128)(2,1)S(1)} async-done(((bf16[4,128,2048]{2,1,0:T(8,128)(2,1)}), bf16[4,128,2048]{2,1,0:T(8,128)(2,1)S(1)}, u32[]{:S(2)}, u32[]{:S(2)}) %all-to-all-start.1) | async-done | bytes 2097184 | tf_op jit(solution)/shard_map/all_to_all | solution.py:33
  127.7 9.6 scatter_custom_fusion
  137.3 9.0 reshape.480
  146.3 11.1 %copy.189 = bf16[32,2,20,2048]{3,1,2,0:T(2,128)(2,1)} copy(bf16[32,2,20,2048]{3,2,1,0:T(8,128)(2,1)} %reshape.480) | data formatting | bytes 10485760 | tf_op jit(solution)/shard_map/reshape | solution.py:168
  157.4 16.0 %all-to-all-start.2 = ((bf16[32,2,20,2048]{3,1,2,0:T(2,128)(2,1)}), bf16[32,2,20,2048]{3,1,2,0:T(2,128)(2,1)}, u32[]{:S(2)}, u32[]{:S(2)}) async-start(bf16[32,2,20,2048]{3,1,2,0:T(2,128)(2,1)} %copy.189), calls=%async_computation.2 | async-start | bytes 10485760 | tf_op jit(solution)/shard_map/all_to_all | solution.py:169
  174.2 10.0 scatter_custom_fusion.1
  184.2 8.9 reshape.483
  193.1 11.1 %copy.196 = bf16[32,2,20,2048]{3,1,2,0:T(2,128)(2,1)} copy(bf16[32,2,20,2048]{3,2,1,0:T(8,128)(2,1)} %reshape.483) | data formatting | bytes 10485760 | tf_op jit(solution)/shard_map/reshape | solution.py:192
  204.3 30.5 %all-to-all-done.2 = bf16[32,2,20,2048]{3,1,2,0:T(2,128)(2,1)} async-done(((bf16[32,2,20,2048]{3,1,2,0:T(2,128)(2,1)}), bf16[32,2,20,2048]{3,1,2,0:T(2,128)(2,1)}, u32[]{:S(2)}, u32[]{:S(2)}) %all-to-all-start.2) | async-done | bytes 5242912 | tf_op jit(solution)/shard_map/all_to_all | solution.py:169
  234.7 8.9 all-to-all-start.4
  243.7 13.9 %fusion.94 = (bf16[768,4096]{1,0:T(8,128)(2,1)}, bf16[768,4096]{1,0:T(8,128)(2,1)}, bf16[768,4096]{1,0:T(8,128)(2,1)}) fusion(bf16[768,12288]{1,0:T(8,128)(2,1)} %all-gather.2.cloned.1.call-done), kind=kLoop, calls=%fused_computation.189 | loop fusion | bytes 37748736 | tf_op jit(solution)/shard_map/slice | solution.py:42
  257.6 8.6 copy.181
  266.3 8.7 copy.182
  275.0 8.6 copy.191
  283.6 8.8 copy.183
  292.4 12.5 %fusion.38 = f32[2,768,32,20]{1,2,3,0:T(8,128)} fusion(bf16[2,2048,768,1]{2,1,3,0:T(8,128)(2,1)} %bitcast.295, bf16[32,2,20,2048]{3,1,2,0:T(2,128)(2,1)} %all-to-all-done.2), kind=kOutput, calls=%fused_computation.66 | convolution fusion | flops 4026531840 | bytes 15466496 | tf_op jit(solution)/shard_map/sxcd,xdf->sxcf/dot_general | solution.py:172
  304.9 11.0 %fusion.40 = f32[2,768,32,20]{1,2,3,0:T(8,128)} fusion(bf16[2,2048,768,1]{2,1,3,0:T(8,128)(2,1)S(1)} %bitcast.298, bf16[32,2,20,2048]{3,1,2,0:T(2,128)(2,1)} %all-to-all-done.2), kind=kOutput, calls=%fused_computation.68 | convolution fusion | flops 4026531840 | bytes 15466496 | tf_op jit(solution)/shard_map/sxcd,xdf->sxcf/dot_general | solution.py:171
  316.0 18.3 %fusion.30 = (bf16[32,2,20,768]{3,0,2,1:T(8,128)(2,1)}, bf16[32,2,20,768]{3,0,2,1:T(8,128)(2,1)}, bf16[32,2,20,768]{3,0,2,1:T(8,128)(2,1)}) fusion(f32[2,768,32,20]{1,2,3,0:T(8,128)} %fusion.40, f32[2,768,32,20]{1,2,3,0:T(8,128)} %fusion.38, bf16[32,2,20,2048]{3,1,2,0:T(2,128)(2,1)} %all-to-all-done.4, bf16[768,2,2048]{2,0,1:T(8,128)(2,1)} %copy.182), kind=kOutput, calls=%fused_computation.52 | convolution fusion | flops 4041277440 | bytes 25296896 | tf_op jit(solution)/shard_map/sxcd,xfd->sxcf/dot_general | solution.py:194
  334.3 10.3 convert_bitcast_fusion
  344.6 10.3 copy.193
  354.9 7.9 all-to-all-start.3
  362.8 11.6 %fusion.99 = f32[2,2048,32,20]{1,2,3,0:T(8,128)} fusion(bf16[2,2048,768,1]{2,1,3,0:T(8,128)(2,1)} %bitcast.297, bf16[32,2,20,768]{3,0,2,1:T(8,128)(2,1)} %get-tuple-element.44), kind=kOutput, calls=%fused_computation.194 | convolution fusion | flops 4026531840 | bytes 18743296 | tf_op jit(solution)/shard_map/sxcf,xdf->sxcd/dot_general | solution.py:200
  374.4 13.0 %fusion.12 = bf16[32,2,20,2048]{3,0,2,1:T(8,128)(2,1)} fusion(f32[2,2048,32,20]{1,2,3,0:T(8,128)} %fusion.99, bf16[2,2048,768,1]{2,1,3,0:T(8,128)(2,1)} %bitcast.296, bf16[32,2,20,768]{3,0,2,1:T(8,128)(2,1)} %get-tuple-element.43), kind=kOutput, calls=%fused_computation.30 | convolution fusion | flops 4031774720 | bytes 23986176 | tf_op jit(solution)/shard_map/sxcf,xdf->sxcd/dot_general | solution.py:201
  387.4 10.2 copy.198
  397.7 26.5 %all-to-all-done.3 = bf16[32,2,20,2048]{3,1,2,0:T(2,128)(2,1)} async-done(((bf16[32,2,20,2048]{3,1,2,0:T(2,128)(2,1)}), bf16[32,2,20,2048]{3,1,2,0:T(2,128)(2,1)}, u32[]{:S(2)}, u32[]{:S(2)}) %all-to-all-start.3) | async-done | bytes 5242912 | tf_op jit(solution)/shard_map/all_to_all | solution.py:178
  424.1 9.5 all-to-all-start.5
  433.7 7.8 copy.194
  441.5 9.0 reshape.482
  450.6 12.0 %gather_fusion = bf16[1024,2048]{1,0:T(8,128)(2,1)} fusion(bf16[1280,2048]{1,0:T(8,128)(2,1)} %reshape.482, s32[1024]{0:T(1024)S(1)} %broadcast_clamp_fusion), kind=kCustom, calls=%fused_computation | custom fusion | bytes 8392704 | tf_op jit(solution)/shard_map/gather | solution.py:181
  462.5 5.8 fusion.1
  468.6 26.5 %all-to-all-done.5 = bf16[32,2,20,2048]{3,1,2,0:T(2,128)(2,1)} async-done(((bf16[32,2,20,2048]{3,1,2,0:T(2,128)(2,1)}), bf16[32,2,20,2048]{3,1,2,0:T(2,128)(2,1)}, u32[]{:S(2)}, u32[]{:S(2)}) %all-to-all-start.5) | async-done | bytes 5242912 | tf_op jit(solution)/shard_map/all_to_all | solution.py:216
  495.0 7.8 copy.199
  502.9 9.0 reshape.484
  511.9 12.1 %gather_fusion.1 = bf16[1024,2048]{1,0:T(8,128)(2,1)} fusion(bf16[1280,2048]{1,0:T(8,128)(2,1)} %reshape.484, s32[1024]{0:T(1024)S(1)} %broadcast_clamp_fusion), kind=kCustom, calls=%fused_computation.1 | custom fusion | bytes 8392704 | tf_op jit(solution)/shard_map/gather | solution.py:220
  537.1 21.7 %all-to-all-done.6 = bf16[4,128,2048]{2,1,0:T(8,128)(2,1)S(1)} async-done(((bf16[4,128,2048]{2,1,0:T(8,128)(2,1)}), bf16[4,128,2048]{2,1,0:T(8,128)(2,1)S(1)}, u32[]{:S(2)}, u32[]{:S(2)}) %all-to-all-start.6) | async-done | bytes 2097184 | tf_op jit(solution)/shard_map/all_to_all | solution.py:19
  580.1 8.3 copy.205
  605.7 18.0 %bitcast_convert_fusion = bf16[2,768,2048]{2,1,0:T(8,128)(2,1)} fusion(bf16[32,2,20,768]{3,0,2,1:T(8,128)(2,1)S(1)} %copy-done.76, bf16[32,2,20,2048]{3,1,2,0:T(2,128)(2,1)} %all-to-all-done.4), kind=kOutput, calls=%fused_computation.4 | convolution fusion | flops 4029677568 | bytes 13500416 | tf_op jit(solution)/shard_map/sxcf,sxcd->xfd/dot_general | solution.py:197
  625.3 21.3 %bitcast_convert_fusion.1 = bf16[2,2048,768]{1,2,0:T(8,128)(2,1)} fusion(bf16[32,2,20,768]{3,0,2,1:T(8,128)(2,1)S(1)} %copy-done.74, bf16[32,2,20,2048]{3,1,2,0:T(2,128)(2,1)} %all-to-all-done.2), kind=kOutput, calls=%fused_computation.5 | convolution fusion | flops 4029677568 | bytes 13500416 | tf_op jit(solution)/shard_map/sxcd,sxcf->xdf/dot_general | solution.py:199
  648.2 21.5 %bitcast_convert_fusion.2 = bf16[2,2048,768]{1,2,0:T(8,128)(2,1)} fusion(bf16[32,2,20,768]{3,0,2,1:T(8,128)(2,1)S(1)} %copy-done.75, bf16[32,2,20,2048]{3,1,2,0:T(2,128)(2,1)} %all-to-all-done.2), kind=kOutput, calls=%fused_computation.6 | convolution fusion | flops 4029677568 | bytes 13500416 | tf_op jit(solution)/shard_map/sxcd,sxcf->xdf/dot_general | solution.py:198
  683.6 18.5 %all-to-all-done.7 = bf16[4,128,2048]{2,1,0:T(8,128)(2,1)} async-done(((bf16[4,128,2048]{2,1,0:T(8,128)(2,1)}), bf16[4,128,2048]{2,1,0:T(8,128)(2,1)}, u32[]{:S(2)}, u32[]{:S(2)}) %all-to-all-start.7) | async-done | bytes 2097184 | tf_op jit(solution)/shard_map/all_to_all | solution.py:33
  706.8 77.1 %all-reduce = (f32[2048]{0:T(1024)}, f32[128]{0:T(128)}, f32[128]{0:T(128)}, f32[2048]{0:T(1024)}) all-reduce(f32[2048]{0:T(1024)S(1)} %get-tuple-element.20, f32[128]{0:T(128)S(1)} %get-tuple-element.14, f32[128]{0:T(128)S(1)} %copy-done.70, f32[2048]{0:T(1024)S(1)} %copy-done.59), channel_id=1, replica_groups=mesh['expert'=32,'tensor'=4] {'expert','tensor'}, use_global_device_ids=true, to_apply=%region_29.30 | all-reduce | flops 4352 | bytes 34816 | tf_op jit(solution)/shard_map/psum | solution.py:295
  788.0 6.8 convert_element_type.219
  803.2 62.3 %reduce-scatter.6.cloned.1.call-done = bf16[2,2048,192]{1,2,0:T(8,128)(2,1)} async-done(((bf16[2,2048,768]{1,2,0:T(8,128)(2,1)}), bf16[2,2048,192]{1,2,0:T(8,128)(2,1)}) %reduce-scatter.6.cloned.1.call-update) | async-done | bytes 1572880 | tf_op jit(solution)/shard_map/reduce_scatter | solution.py:208
  868.9 62.6 %reduce-scatter.4.cloned.1.call-done = bf16[2,2048,192]{1,2,0:T(8,128)(2,1)} async-done(((bf16[2,2048,768]{1,2,0:T(8,128)(2,1)}), bf16[2,2048,192]{1,2,0:T(8,128)(2,1)}) %reduce-scatter.4.cloned.1.call-update) | async-done | bytes 1572880 | tf_op jit(solution)/shard_map/reduce_scatter | solution.py:205
  935.0 146.9 %all-reduce.5.cloned.1.call-done = f32[2048,64]{0,1:T(8,128)} async-done(((f32[2048,64]{0,1:T(8,128)}), f32[2048,64]{0,1:T(8,128)}) %all-reduce.5.cloned.1.call-update) | async-done | bytes 524304 | tf_op jit(solution)/shard_map/psum | solution.py:295
  (279 shorter events, 137.8 us)
Async XLA Ops:
  7.2 47.0 %copy-start = (bf16[2048,128]{1,0:T(8,128)(2,1)S(1)}, bf16[2048,128]{1,0:T(8,128)(2,1)}, u32[]{:S(2)}) copy-start(bf16[2048,128]{1,0:T(8,128)(2,1)} %param.18) | copy-start | bytes 1572868
  7.2 236.5 %all-gather.2.cloned.1.call-start = ((), (), s32[]{:S(2)}) async-start(), calls=%async_computation.11 | async-start | bytes 23592960 | tf_op jit(solution)/shard_map/all_gather | solution.py:40
  15.1 39.1 %all-to-all-start = ((bf16[4,128,2048]{2,1,0:T(8,128)(2,1)}), bf16[4,128,2048]{2,1,0:T(8,128)(2,1)S(1)}, u32[]{:S(2)}, u32[]{:S(2)}) async-start(bf16[4,128,2048]{2,1,0:T(8,128)(2,1)} %broadcast_in_dim.14), calls=%async_computation | async-start | bytes 4194304 | tf_op jit(solution)/shard_map/all_to_all | solution.py:19
  54.2 7.1 copy-start.2
  55.0 4.9 copy-start.19
  55.1 4.9 copy-start.55
  55.1 6.2 copy-start.33
  74.5 51.4 %all-to-all-start.1 = ((bf16[4,128,2048]{2,1,0:T(8,128)(2,1)}), bf16[4,128,2048]{2,1,0:T(8,128)(2,1)S(1)}, u32[]{:S(2)}, u32[]{:S(2)}) async-start(bf16[4,128,2048]{2,1,0:T(8,128)(2,1)} %bitcast.306), calls=%async_computation.1 | async-start | bytes 4194304 | tf_op jit(solution)/shard_map/all_to_all | solution.py:33
  78.8 48.8 %copy-start.50 = (f32[2048]{0:T(1024)S(1)}, f32[2048]{0:T(1024)}, u32[]{:S(2)}) copy-start(f32[2048]{0:T(1024)} %param.23) | copy-start | bytes 24580
  126.6 19.7 %copy-start.60 = (f32[128]{0:T(128)}, f32[128]{0:T(128)S(1)}, u32[]{:S(2)}) copy-start(f32[128]{0:T(128)S(1)} %add_rsqrt_fusion.2) | copy-start | bytes 1540
  127.7 45.8 %copy-start.16 = (bf16[128,2048]{1,0:T(8,128)(2,1)}, bf16[128,2048]{1,0:T(8,128)(2,1)S(1)}, u32[]{:S(2)}) copy-start(bf16[128,2048]{1,0:T(8,128)(2,1)S(1)} %multiply_convert_fusion) | copy-start | bytes 1572868
  157.4 16.0 %copy-start.22 = (bf16[128,2048]{1,0:T(8,128)(2,1)S(1)}, bf16[128,2048]{1,0:T(8,128)(2,1)}, u32[]{:S(2)}) copy-start(bf16[128,2048]{1,0:T(8,128)(2,1)} %param.29) | copy-start | bytes 1572868
  157.4 16.1 %copy-start.40 = (bf16[2048,64]{0,1:T(8,128)(2,1)S(1)}, bf16[2048,64]{0,1:T(8,128)(2,1)}, u32[]{:S(2)}) copy-start(bf16[2048,64]{0,1:T(8,128)(2,1)} %param.24) | copy-start | bytes 786436
  157.4 77.3 %all-to-all-start.2 = ((bf16[32,2,20,2048]{3,1,2,0:T(2,128)(2,1)}), bf16[32,2,20,2048]{3,1,2,0:T(2,128)(2,1)}, u32[]{:S(2)}, u32[]{:S(2)}) async-start(bf16[32,2,20,2048]{3,1,2,0:T(2,128)(2,1)} %copy.189), calls=%async_computation.2 | async-start | bytes 10485760 | tf_op jit(solution)/shard_map/all_to_all | solution.py:169
  234.7 81.3 %all-to-all-start.4 = ((bf16[32,2,20,2048]{3,1,2,0:T(2,128)(2,1)}), bf16[32,2,20,2048]{3,1,2,0:T(2,128)(2,1)}, u32[]{:S(2)}, u32[]{:S(2)}) async-start(bf16[32,2,20,2048]{3,1,2,0:T(2,128)(2,1)} %copy.196), calls=%async_computation.4 | async-start | bytes 10485760 | tf_op jit(solution)/shard_map/all_to_all | solution.py:193
  292.4 12.6 %copy-start.21 = (bf16[768,4096]{0,1:T(8,128)(2,1)S(1)}, bf16[768,4096]{0,1:T(8,128)(2,1)}, u32[]{:S(2)}) copy-start(bf16[768,4096]{0,1:T(8,128)(2,1)} %copy.183) | copy-start | bytes 18874372
  354.9 69.2 %all-to-all-start.3 = ((bf16[32,2,20,2048]{3,1,2,0:T(2,128)(2,1)}), bf16[32,2,20,2048]{3,1,2,0:T(2,128)(2,1)}, u32[]{:S(2)}, u32[]{:S(2)}) async-start(bf16[32,2,20,2048]{3,1,2,0:T(2,128)(2,1)} %copy.193), calls=%async_computation.3 | async-start | bytes 10485760 | tf_op jit(solution)/shard_map/all_to_all | solution.py:178
  424.1 70.9 %all-to-all-start.5 = ((bf16[32,2,20,2048]{3,1,2,0:T(2,128)(2,1)}), bf16[32,2,20,2048]{3,1,2,0:T(2,128)(2,1)}, u32[]{:S(2)}, u32[]{:S(2)}) async-start(bf16[32,2,20,2048]{3,1,2,0:T(2,128)(2,1)} %copy.198), calls=%async_computation.5 | async-start | bytes 10485760 | tf_op jit(solution)/shard_map/all_to_all | solution.py:216
  524.0 5.2 copy-start.7
  524.0 5.2 copy-start.41
  524.0 5.2 copy-start.51
  524.0 5.2 copy-start.61
  524.0 7.3 copy-start.23
  531.8 5.3 copy-start.49
  531.8 5.3 copy-start.57
  533.4 25.4 %all-to-all-start.6 = ((bf16[4,128,2048]{2,1,0:T(8,128)(2,1)}), bf16[4,128,2048]{2,1,0:T(8,128)(2,1)S(1)}, u32[]{:S(2)}, u32[]{:S(2)}) async-start(bf16[4,128,2048]{2,1,0:T(8,128)(2,1)} %broadcast_in_dim.20), calls=%async_computation.6 | async-start | bytes 4194304 | tf_op jit(solution)/shard_map/all_to_all | solution.py:19
  537.0 246.8 %all-reduce.7.cloned.1.call-start = ((), (), s32[]{:S(2)}) async-start(), calls=%async_computation.16 | async-start | bytes 18874368 | tf_op jit(solution)/shard_map/psum | solution.py:290
  558.8 10.3 slice-start
  558.8 10.3 slice-start.1
  563.5 5.6 copy-start.45
  580.1 8.4 copy-start.20
  580.1 11.6 %copy-start.3 = (bf16[4,128,2048]{2,1,0:T(8,128)(2,1)S(1)}, bf16[4,128,2048]{2,1,0:T(8,128)(2,1)}, u32[]{:S(2)}) copy-start(bf16[4,128,2048]{2,1,0:T(8,128)(2,1)} %copy-done.2) | copy-start | bytes 6291460
  588.5 4.8 copy-start.9
  588.5 4.8 copy-start.28
  604.2 195.6 %reduce-scatter.8.cloned.1.call-start = ((), (), s32[]{:S(2)}) async-start(), calls=%async_computation.15 | async-start | bytes 7864320 | tf_op jit(solution)/shard_map/reduce_scatter | solution.py:211
  623.7 241.8 %reduce-scatter.6.cloned.1.call-start = ((), (), s32[]{:S(2)}) async-start(), calls=%async_computation.14 | async-start | bytes 7864320 | tf_op jit(solution)/shard_map/reduce_scatter | solution.py:208
  646.6 285.0 %reduce-scatter.4.cloned.1.call-start = ((), (), s32[]{:S(2)}) async-start(), calls=%async_computation.13 | async-start | bytes 7864320 | tf_op jit(solution)/shard_map/reduce_scatter | solution.py:205
  676.6 28.0 %copy-start.11 = (bf16[128,2048]{1,0:T(8,128)(2,1)S(1)}, bf16[128,2048]{1,0:T(8,128)(2,1)}, u32[]{:S(2)}) copy-start(bf16[128,2048]{1,0:T(8,128)(2,1)} %param.15) | copy-start | bytes 1572868
  676.6 28.0 %copy-start.54 = (f32[2048]{0:T(1024)S(1)}, f32[2048]{0:T(1024)}, u32[]{:S(2)}) copy-start(f32[2048]{0:T(1024)} %param.16) | copy-start | bytes 24580
  676.6 28.0 %copy-start.67 = (f32[128]{0:T(128)S(1)}, f32[128]{0:T(128)}, u32[]{:S(2)}) copy-start(f32[128]{0:T(128)} %copy-done.66) | copy-start | bytes 1540
  676.6 25.5 %all-to-all-start.7 = ((bf16[4,128,2048]{2,1,0:T(8,128)(2,1)}), bf16[4,128,2048]{2,1,0:T(8,128)(2,1)}, u32[]{:S(2)}, u32[]{:S(2)}) async-start(bf16[4,128,2048]{2,1,0:T(8,128)(2,1)} %bitcast.294), calls=%async_computation.7 | async-start | bytes 4194304 | tf_op jit(solution)/shard_map/all_to_all | solution.py:33
  681.3 23.7 %copy-start.8 = (f32[128,2048]{1,0:T(8,128)S(1)}, f32[128,2048]{1,0:T(8,128)}, u32[]{:S(2)}) copy-start(f32[128,2048]{1,0:T(8,128)} %copy-done.6) | copy-start | bytes 3145732
  681.3 23.7 %copy-start.15 = (f32[128,2048]{1,0:T(8,128)S(1)}, f32[128,2048]{1,0:T(8,128)}, u32[]{:S(2)}) copy-start(f32[128,2048]{1,0:T(8,128)} %copy-done.14) | copy-start | bytes 3145732
  681.3 23.7 %copy-start.52 = (f32[2048]{0:T(1024)S(1)}, f32[2048]{0:T(1024)}, u32[]{:S(2)}) copy-start(f32[2048]{0:T(1024)} %param.23) | copy-start | bytes 24580
  681.3 23.7 %copy-start.62 = (f32[128]{0:T(128)S(1)}, f32[128]{0:T(128)}, u32[]{:S(2)}) copy-start(f32[128]{0:T(128)} %copy-done.60) | copy-start | bytes 1540
  681.3 23.7 %copy-start.69 = (f32[128]{0:T(128)S(1)}, f32[128]{0:T(128)}, u32[]{:S(2)}) copy-start(f32[128]{0:T(128)} %copy-done.68) | copy-start | bytes 1540
  681.3 400.6 %all-reduce.5.cloned.1.call-start = ((), (), s32[]{:S(2)}) async-start(), calls=%async_computation.12 | async-start | bytes 1048576 | tf_op jit(solution)/shard_map/psum | solution.py:295
  788.0 6.8 copy-start.25
  (45 other events, 109.7 us)
Sparse Core Ops, SparseCore 0:
  12.2 208.7 all-gather.1
  604.3 127.8 all-reduce.6
  734.8 64.9 reduce-scatter.7
  802.1 63.3 reduce-scatter.5
  867.9 63.6 reduce-scatter.3
  936.9 144.9 all-reduce.4
where the time goes:
time: 1100 us; the launch traced here: 1090 us
  waiting for transfers between devices  436 us (40%)
  local copies, waits for them, and re-layouts  217 us (20%)
  matrix products  184 us (17%)
  other arithmetic  102 us (9%)
  blocking collectives  77.1 us (7%)
  starting transfers between devices  59.6 us (5%)
  between operations  15.6 us (1%)
    psum x1, waiting for transfers between devices, per_device(): lax.psum((grad_router, attn_gain_grad, q_gain_grad, k_gain_grad, mlp_gain...  147 us
    psum x1, blocking collectives, per_device(): lax.psum((grad_router, attn_gain_grad, q_gain_grad, k_gain_grad, mlp_gain...  77.1 us
    reduce_scatter x1, waiting for transfers between devices, per_device(): lax.psum_scatter(grad_gate_w.astype(jnp.bfloat16), 'tensor', scatter_dime...  62.6 us
    reduce_scatter x1, waiting for transfers between devices, per_device(): lax.psum_scatter(grad_up_w.astype(jnp.bfloat16), 'tensor', scatter_dimens...  62.3 us
    all_to_all x2, waiting for transfers between devices, sent_to_all(): lax.all_to_all(jnp.broadcast_to(x[None], (peers, *x.shape)), axis, 0, 0,...  48.6 us
    slice x4, local copies, waits for them, and re-layouts, turned_gather(): section = filled[:, at:at + t[0].size].reshape(-1, *t.shape[1:])  39.9 us
    another operation x3, other arithmetic  35.2 us
    all_to_all x2, waiting for transfers between devices, sent_and_summed(): parts = lax.all_to_all(in_blocks(x, dim, peers), axis, 0, 0, tiled=True)  31.3 us
  transfers between devices with their start and end apart: 14, of which 11 were waited for; matrix products, arithmetic and copies ran while one was open for 33% of the time, Pallas kernels for 0%

commit v1 on v0

v1 whole, which is shorter than its diff:
```python
import functools

import jax
import jax.numpy as jnp
from jax import lax
from jax.experimental import pallas as pl
from jax.experimental.pallas import tpu as pltpu
from jax.sharding import PartitionSpec as P

MESH = pl.DeviceIdType.MESH


class Place:
    def __init__(self):
        e = lax.axis_index("expert")
        self.x = lax.axis_index("tensor")
        self.z = e // 8
        self.y = (e // 2) % 4
        self.core = e % 2

    def block(self, axis="z", a=0, b=0, other=0):
        dz, dy = (a, b) if axis == "z" else (b, a)
        core = (self.core + other) % 2
        return ((self.z + dz) % 4) * 8 + ((self.y + dy) % 4) * 2 + core

    def device(self, axis="z", a=0, b=0, other=0):
        return (self.block(axis, a, b, other), self.x)


def greet(devices):
    barrier = pltpu.get_barrier_semaphore()
    for device in devices:
        pl.semaphore_signal(barrier, inc=1, device_id=device, device_id_type=MESH)
    pl.semaphore_wait(barrier, len(devices))


def plane_neighbours(place):
    return [
        place.device("z", 1),
        place.device("z", -1),
        place.device("y", 1),
        place.device("y", -1),
        place.device(other=1),
    ]


OTHER = {"z": "y", "y": "z"}


def gather_plan():
    stages = [[], [], [], []]
    for half, first in ((0, "y"), (1, "z")):
        for side in (-1, 1):
            stages[0].append((first, half, side, 0, None, ("f", side)))
            stages[0].append((first, half, 0, side, None, ("s", side)))
    for half, first in ((0, "y"), (1, "z")):
        for quarter, side in ((0, -1), (1, 1)):
            stages[1].append((first, half, 2, 0, quarter, ("f", side)))
        for f in (-1, 1):
            for side in (-1, 1):
                stages[1].append((first, half, f, side, None, ("s", side)))
        for quarter, side in ((0, -1), (1, 1)):
            stages[1].append((first, half, 0, 2, quarter, ("s", side)))
    for half, first in ((0, "y"), (1, "z")):
        for quarter in (0, 1):
            for side in (-1, 1):
                stages[2].append((first, half, 2, side, quarter, ("s", side)))
        for f in (-1, 1):
            for quarter, side in ((0, -1), (1, 1)):
                stages[2].append((first, half, f, 2, quarter, ("s", side)))
    for half, first in ((0, "y"), (1, "z")):
        for quarter, side in ((0, -1), (1, 1)):
            stages[3].append((first, half, 2, 2, quarter, ("s", side)))
    return [piece for stage in stages for piece in stage]


PIECES = gather_plan()
PIECE_AT = {piece: at for at, piece in enumerate(PIECES)}


def gather_kernel(x_ref, out_ref, own_sem, send_sems, recv_sems, core_send, core_recv):
    place = Place()
    rows = x_ref.shape[0]
    greet(plane_neighbours(place))

    def span(half, quarter):
        if quarter is None:
            return pl.ds(half * (rows // 2), rows // 2)
        return pl.ds(half * (rows // 2) + quarter * (rows // 4), rows // 4)

    def view(piece):
        first, half, f, s, quarter, _ = piece
        return out_ref.at[place.block(first, f, s), span(half, quarter)]

    def sent(source, piece):
        first, half, f, s, quarter, (leg, side) = piece
        axis = first if leg == "f" else OTHER[first]
        f_here, s_here = (f - side, s) if leg == "f" else (f, s - side)
        at = PIECE_AT[piece]
        return pltpu.make_async_remote_copy(
            src_ref=source,
            dst_ref=out_ref.at[place.block(first, f_here, s_here), span(half, quarter)],
            send_sem=send_sems.at[at],
            recv_sem=recv_sems.at[at],
            device_id=place.device(axis, -side),
            device_id_type=MESH,
        )

    def to_core(at, block, where, source):
        return pltpu.make_async_remote_copy(
            src_ref=source,
            dst_ref=out_ref.at[block, where],
            send_sem=core_send.at[at],
            recv_sem=core_recv.at[at],
            device_id=place.device(other=1),
            device_id_type=MESH,
        )

    own = pltpu.make_async_copy(x_ref, out_ref.at[place.block()], own_sem)
    own.start()
    started = []

    def forward(piece_here, targets):
        for target in targets:
            first, half, f, s, quarter, (leg, side) = target
            if piece_here is None:
                source = x_ref.at[span(half, quarter)]
            else:
                f_here, s_here = (f - side, s) if leg == "f" else (f, s - side)
                source = out_ref.at[place.block(first, f_here, s_here), span(half, quarter)]
            copy = sent(source, target)
            copy.start()
            started.append(copy)

    for piece in PIECES[:8]:
        forward(None, [piece])
    whole = to_core(len(PIECES), place.block(), pl.ds(0, rows), x_ref)
    whole.start()
    core_copies = [whole]

    for at, piece in enumerate(PIECES):
        first, half, f, s, quarter, (leg, side) = piece
        pltpu.make_async_remote_copy(
            src_ref=view(piece),
            dst_ref=view(piece),
            send_sem=send_sems.at[at],
            recv_sem=recv_sems.at[at],
            device_id=place.device(first, 1),
            device_id_type=MESH,
        ).wait_recv()
        next_pieces = []
        for target in PIECES:
            t_first, t_half, t_f, t_s, t_quarter, (t_leg, t_side) = target
            if t_half != half:
                continue
            back = (t_f - t_side, t_s) if t_leg == "f" else (t_f, t_s - t_side)
            if back == (0, 0) or back != (f, s):
                alt = None
                if t_leg == "f" and t_f == 2 and leg == "f" and f == t_side and s == 0 and t_s == 0:
                    alt = True
                if t_leg == "s" and t_s == 2 and s == t_side and f == t_f:
                    alt = True
                if alt is None:
                    continue
            if t_leg == "s" and t_s in (-1, 1) and not (s == 0 and f == t_f):
                continue
            if quarter is not None and t_quarter != quarter:
                continue
            next_pieces.append(target)
        for target in next_pieces:
            t_first, t_half, t_f, t_s, t_quarter, (t_leg, t_side) = target
            axis = t_first if t_leg == "f" else OTHER[t_first]
            here = out_ref.at[place.block(first, f, s), span(t_half, t_quarter)]
            copy = pltpu.make_async_remote_copy(
                src_ref=here,
                dst_ref=here,
                send_sem=send_sems.at[PIECE_AT[target]],
                recv_sem=recv_sems.at[PIECE_AT[target]],
                device_id=place.device(axis, -t_side),
                device_id_type=MESH,
            )
            copy.start()
            started.append(copy)
        core_copy = to_core(at, place.block(first, f, s), span(half, quarter), view(piece))
        core_copy.start()
        core_copies.append(core_copy)
    assert len(started) == len(PIECES), (len(started), len(PIECES))
    for copy in started:
        copy.wait_send()
    for at, piece in enumerate(PIECES):
        first, half, f, s, quarter, _ = piece
        there = out_ref.at[place.block(first, f, s, 1), span(half, quarter)]
        pltpu.make_async_remote_copy(
            src_ref=view(piece), dst_ref=there, send_sem=core_send.at[at],
            recv_sem=core_recv.at[at], device_id=place.device(other=1), device_id_type=MESH,
        ).wait()
    pltpu.make_async_remote_copy(
        src_ref=x_ref, dst_ref=out_ref.at[place.block(other=1)], send_sem=core_send.at[len(PIECES)],
        recv_sem=core_recv.at[len(PIECES)], device_id=place.device(other=1), device_id_type=MESH,
    ).wait()
    own.wait()


def gather_plane(x, collective_id):
    count = len(PIECES)
    return pl.pallas_call(
        gather_kernel,
        out_shape=jax.ShapeDtypeStruct((32, *x.shape), x.dtype),
        in_specs=[pl.BlockSpec(memory_space=pl.ANY)],
        out_specs=pl.BlockSpec(memory_space=pl.ANY),
        scratch_shapes=[
            pltpu.SemaphoreType.DMA,
            pltpu.SemaphoreType.DMA((count,)),
            pltpu.SemaphoreType.DMA((count,)),
            pltpu.SemaphoreType.DMA((count + 1,)),
            pltpu.SemaphoreType.DMA((count + 1,)),
        ],
        compiler_params=pltpu.CompilerParams(collective_id=collective_id, has_side_effects=True),
        name="gather_plane",
    )(x)


def scatter_kernel(
    c_ref, out_ref, held, other, in_a, in_b, in_c, in_d,
    load_sems, core_send, core_recv, send_sems, recv_sems,
):
    place = Place()
    rows = c_ref.shape[1]
    half_rows, quarter_rows = rows // 2, rows // 4
    greet(plane_neighbours(place))
    order = [(2, 2), (2, 1), (1, 2), (2, 3), (3, 2), (2, 0), (0, 2)]
    order += [(1, 1), (1, 3), (3, 1), (3, 3), (1, 0), (0, 1), (3, 0), (0, 3), (0, 0)]
    loads, cores = {}, {}
    for dz, dy in order:
        at = dz * 4 + dy
        cores[at] = pltpu.make_async_remote_copy(
            src_ref=c_ref.at[place.block("z", dz, dy, 1)],
            dst_ref=other.at[at],
            send_sem=core_send.at[at],
            recv_sem=core_recv.at[at],
            device_id=place.device(other=1),
            device_id_type=MESH,
        )
        cores[at].start()
        loads[at] = pltpu.make_async_copy(
            c_ref.at[place.block("z", dz, dy)], held.at[at], load_sems.at[at]
        )
        loads[at].start()
    ready = set()

    def slot(axis, a, b):
        dz, dy = (a, b) if axis == "z" else (b, a)
        return (dz % 4) * 4 + dy % 4

    def add_rows(into, at, start, count, source, s_at):
        @pl.loop(0, count, step=16)
        def _(row):
            here = (at, pl.ds(start + row, 16))
            there = (*s_at, pl.ds(row, 16))
            total = into[here].astype(jnp.float32) + source[there].astype(jnp.float32)
            into[here] = total.astype(jnp.bfloat16)

    def make_ready(at):
        if at in ready:
            return
        ready.add(at)
        loads[at].wait()
        cores[at].wait_recv()
        add_rows(held, at, 0, rows, other, (at,))

    sent = []

    def send(source, target, number, device):
        copy = pltpu.make_async_remote_copy(
            src_ref=source, dst_ref=target, send_sem=send_sems.at[number],
            recv_sem=recv_sems.at[number], device_id=device, device_id_type=MESH,
        )
        copy.start()
        sent.append(copy)

    def arrive(target, number):
        pltpu.make_async_remote_copy(
            src_ref=target, dst_ref=target, send_sem=send_sems.at[number],
            recv_sem=recv_sems.at[number], device_id=place.device("z", 1), device_id_type=MESH,
        ).wait_recv()

    axes = (("z", "y"), ("y", "z"))
    lines = (2, 1, 3, 0)
    for line in lines:
        for half, (first, second) in enumerate(axes):
            at = slot(first, 2, line)
            make_ready(at)
            for quarter, side in ((0, 1), (1, -1)):
                where = pl.ds(half * half_rows + quarter * quarter_rows, quarter_rows)
                send(held.at[at, where], in_a.at[half, line, quarter],
                     ((half * 4 + line) * 2 + quarter), place.device(first, side))
    for line in lines:
        for half, (first, second) in enumerate(axes):
            for quarter, side in ((0, 1), (1, -1)):
                at = slot(first, side, line)
                make_ready(at)
                number = (half * 4 + line) * 2 + quarter
                arrive(in_a.at[half, line, quarter], number)
                add_rows(held, at, half * half_rows + quarter * quarter_rows, quarter_rows,
                         in_a, (half, line, quarter))
                send(held.at[at, pl.ds(half * half_rows, half_rows)],
                     in_b.at[half, line, quarter], 16 + number, place.device(first, side))
    for line in lines:
        for half, (first, second) in enumerate(axes):
            at = slot(first, 0, line)
            make_ready(at)
            for quarter in (0, 1):
                number = (half * 4 + line) * 2 + quarter
                arrive(in_b.at[half, line, quarter], 16 + number)
                add_rows(held, at, half * half_rows, half_rows, in_b, (half, line, quarter))
            if line == 2:
                for quarter, side in ((0, 1), (1, -1)):
                    where = pl.ds(half * half_rows + quarter * quarter_rows, quarter_rows)
                    send(held.at[at, where], in_c.at[half, quarter],
                         32 + half * 2 + quarter, place.device(second, side))
            if line in (1, 3):
                quarter, side = (0, 1) if line == 1 else (1, -1)
                number = 32 + half * 2 + quarter
                arrive(in_c.at[half, quarter], number)
                add_rows(held, at, half * half_rows + quarter * quarter_rows, quarter_rows,
                         in_c, (half, quarter))
                send(held.at[at, pl.ds(half * half_rows, half_rows)], in_d.at[half, quarter],
                     36 + half * 2 + quarter, place.device(second, side))
    for half in (0, 1):
        for quarter in (0, 1):
            arrive(in_d.at[half, quarter], 36 + half * 2 + quarter)

        @pl.loop(0, half_rows, step=16)
        def _(row):
            here = pl.ds(half * half_rows + row, 16)
            total = held[0, here].astype(jnp.float32)
            for quarter in (0, 1):
                total = total + in_d[half, quarter, pl.ds(row, 16)].astype(jnp.float32)
            out_ref[here] = total
    for copy in sent:
        copy.wait_send()
    for at in cores:
        cores[at].wait_send()


def scatter_plane(c, collective_id):
    _, rows, width = c.shape
    bf16 = jnp.bfloat16
    return pl.pallas_call(
        scatter_kernel,
        out_shape=jax.ShapeDtypeStruct((rows, width), jnp.float32),
        in_specs=[pl.BlockSpec(memory_space=pl.ANY)],
        out_specs=pl.BlockSpec(memory_space=pltpu.VMEM),
        scratch_shapes=[
            pltpu.VMEM((16, rows, width), bf16),
            pltpu.VMEM((16, rows, width), bf16),
            pltpu.VMEM((2, 4, 2, rows // 4, width), bf16),
            pltpu.VMEM((2, 4, 2, rows // 2, width), bf16),
            pltpu.VMEM((2, 2, rows // 4, width), bf16),
            pltpu.VMEM((2, 2, rows // 2, width), bf16),
            pltpu.SemaphoreType.DMA((16,)),
            pltpu.SemaphoreType.DMA((16,)),
            pltpu.SemaphoreType.DMA((16,)),
            pltpu.SemaphoreType.DMA((40,)),
            pltpu.SemaphoreType.DMA((40,)),
        ],
        compiler_params=pltpu.CompilerParams(
            collective_id=collective_id, has_side_effects=True, vmem_limit_bytes=48 * 2**20
        ),
        name="scatter_plane",
    )(c)


def line_neighbours(place):
    e = place.block()
    return [(e, (place.x + 1) % 4), (e, (place.x + 3) % 4)]


def line_gather_kernel(x_ref, out_ref, own_sem, send_sems, recv_sems):
    place = Place()
    rows = x_ref.shape[0]
    after, before = line_neighbours(place)
    greet([after, before])
    own = pltpu.make_async_copy(x_ref, out_ref.at[place.x], own_sem)
    own.start()

    def copy(source, block, where, number, device):
        return pltpu.make_async_remote_copy(
            src_ref=source, dst_ref=out_ref.at[block, where], send_sem=send_sems.at[number],
            recv_sem=recv_sems.at[number], device_id=device, device_id_type=MESH,
        )

    every, low, high = pl.ds(0, rows), pl.ds(0, rows // 2), pl.ds(rows // 2, rows // 2)
    first = [copy(x_ref, place.x, every, 0, after), copy(x_ref, place.x, every, 1, before)]
    for c in first:
        c.start()
    left, right, far = (place.x + 3) % 4, (place.x + 1) % 4, (place.x + 2) % 4
    copy(x_ref, left, every, 0, after).wait_recv()
    third = copy(out_ref.at[left, low], left, low, 2, after)
    third.start()
    copy(x_ref, right, every, 1, before).wait_recv()
    fourth = copy(out_ref.at[right, high], right, high, 3, before)
    fourth.start()
    copy(out_ref.at[far, low], far, low, 2, after).wait_recv()
    copy(out_ref.at[far, high], far, high, 3, before).wait_recv()
    for c in (*first, third, fourth):
        c.wait_send()
    own.wait()


def gather_line(x, collective_id):
    return pl.pallas_call(
        line_gather_kernel,
        out_shape=jax.ShapeDtypeStruct((4, *x.shape), x.dtype),
        in_specs=[pl.BlockSpec(memory_space=pl.ANY)],
        out_specs=pl.BlockSpec(memory_space=pl.ANY),
        scratch_shapes=[
            pltpu.SemaphoreType.DMA,
            pltpu.SemaphoreType.DMA((4,)),
            pltpu.SemaphoreType.DMA((4,)),
        ],
        compiler_params=pltpu.CompilerParams(collective_id=collective_id, has_side_effects=True),
        name="gather_line",
    )(x)


def line_scatter_kernel(c_ref, out_ref, in_a, in_b, send_sems, recv_sems):
    place = Place()
    rows = c_ref.shape[1]
    after, before = line_neighbours(place)
    left, right, far = (place.x + 3) % 4, (place.x + 1) % 4, (place.x + 2) % 4
    half = rows // 2
    greet([after, before])

    def copy(source, target, number, device):
        return pltpu.make_async_remote_copy(
            src_ref=source, dst_ref=target, send_sem=send_sems.at[number],
            recv_sem=recv_sems.at[number], device_id=device, device_id_type=MESH,
        )

    copies = [
        copy(c_ref.at[far, pl.ds(0, half)], in_a.at[0], 0, after),
        copy(c_ref.at[far, pl.ds(half, half)], in_a.at[1], 1, before),
    ]
    for c in copies:
        c.start()

    def add(block, start, source):
        @pl.loop(0, half, step=16)
        def _(row):
            here = (block, pl.ds(start + row, 16))
            total = c_ref[here].astype(jnp.float32) + source[pl.ds(row, 16)].astype(jnp.float32)
            c_ref[here] = total.astype(jnp.bfloat16)

    copies[0].wait_recv()
    add(right, 0, in_a.at[0])
    copies.append(copy(c_ref.at[right], in_b.at[0], 2, after))
    copies[2].start()
    copies[1].wait_recv()
    add(left, half, in_a.at[1])
    copies.append(copy(c_ref.at[left], in_b.at[1], 3, before))
    copies[3].start()
    copies[2].wait_recv()
    copies[3].wait_recv()

    @pl.loop(0, rows, step=16)
    def _(row):
        here = pl.ds(row, 16)
        total = c_ref[place.x, here].astype(jnp.float32) + in_b[0, here].astype(jnp.float32)
        out_ref[here] = total + in_b[1, here].astype(jnp.float32)

    for c in copies:
        c.wait_send()


def line_scatter_outer(c_ref, out_ref, held, load_sem, *rest):
    load = pltpu.make_async_copy(c_ref, held, load_sem)
    load.start()
    load.wait()
    line_scatter_kernel(held, out_ref, *rest)


def scatter_line(c, collective_id):
    _, rows, width = c.shape
    return pl.pallas_call(
        line_scatter_outer,
        out_shape=jax.ShapeDtypeStruct((rows, width), jnp.float32),
        in_specs=[pl.BlockSpec(memory_space=pl.ANY)],
        out_specs=pl.BlockSpec(memory_space=pltpu.VMEM),
        scratch_shapes=[
            pltpu.VMEM((4, rows, width), jnp.bfloat16),
            pltpu.SemaphoreType.DMA,
            pltpu.VMEM((2, rows // 2, width), jnp.bfloat16),
            pltpu.VMEM((2, rows, width), jnp.bfloat16),
            pltpu.SemaphoreType.DMA((4,)),
            pltpu.SemaphoreType.DMA((4,)),
        ],
        compiler_params=pltpu.CompilerParams(
            collective_id=collective_id, has_side_effects=True, vmem_limit_bytes=16 * 2**20
        ),
        name="scatter_line",
    )(c)


SLOTS = 80
NT = (((1,), (1,)), ((), ()))
TN = (((0,), (0,)), ((), ()))
NN = (((1,), (0,)), ((), ()))


def dot(left, right, dims):
    return lax.dot_general(left, right, dims, preferred_element_type=jnp.float32)


def chosen_rows(slots, first):
    value = slots.astype(jnp.float32)
    lane = lax.broadcasted_iota(jnp.int32, value.shape, 1)
    slot = lax.broadcasted_iota(jnp.int32, (value.shape[0], 2 * SLOTS), 1).astype(jnp.float32)
    found = []
    for j in range(2):
        mine = jnp.sum(jnp.where(lane == first + j, value, 0.0), axis=1, keepdims=True)
        found.append(jnp.where(mine >= 0.0, mine + float(j * SLOTS), -1.0))
    return jnp.where((slot == found[0]) | (slot == found[1]), 1.0, 0.0).astype(jnp.bfloat16)


def select_kernel(first_ref, tokens_ref, slots_ref, a_ref, b_ref, gate_a_ref, gate_b_ref):
    first = first_ref[0]
    table = chosen_rows(slots_ref[...], first)
    width = a_ref.shape[1]
    rows = dot(table, tokens_ref[...], TN)
    a_ref[...] = rows[:SLOTS, :width].astype(jnp.bfloat16)
    b_ref[...] = rows[SLOTS:, :width].astype(jnp.bfloat16)
    tail = rows[:, width:]
    lane = lax.broadcasted_iota(jnp.int32, tail.shape, 1) % 64
    for j, ref in enumerate((gate_a_ref, gate_b_ref)):
        part = tail[j * SLOTS : (j + 1) * SLOTS]
        mine = lane[j * SLOTS : (j + 1) * SLOTS] == first + j
        gate = jnp.sum(jnp.where(mine, part, 0.0), axis=1, keepdims=True)
        ref[...] = jnp.broadcast_to(gate, ref.shape)


def select_rows(first, tokens, slot_source):
    count, full = tokens.shape
    width = full - 128
    groups = count // 512
    out = jax.ShapeDtypeStruct((groups * SLOTS, width), jnp.bfloat16)
    gate = jax.ShapeDtypeStruct((groups * SLOTS, 128), jnp.float32)
    return pl.pallas_call(
        select_kernel,
        grid=(groups,),
        out_shape=(out, out, gate, gate),
        in_specs=[
            pl.BlockSpec(memory_space=pltpu.SMEM),
            pl.BlockSpec((512, full), lambda i: (i, 0)),
            pl.BlockSpec((512, 128), lambda i: (i, width // 128)),
        ],
        out_specs=(
            pl.BlockSpec((SLOTS, width), lambda i: (i, 0)),
            pl.BlockSpec((SLOTS, width), lambda i: (i, 0)),
            pl.BlockSpec((SLOTS, 128), lambda i: (i, 0)),
            pl.BlockSpec((SLOTS, 128), lambda i: (i, 0)),
        ),
        compiler_params=pltpu.CompilerParams(vmem_limit_bytes=24 * 2**20),
        cost_estimate=pl.CostEstimate(
            flops=2 * count * 160 * full, bytes_accessed=count * full * 2 + groups * 160 * full * 2,
            transcendentals=0,
        ),
        name="select_rows",
    )(first, tokens, slot_source)


def combine_kernel(first_ref, a_ref, b_ref, slots_ref, out_ref):
    table = chosen_rows(slots_ref[...], first_ref[0])
    rows = jnp.concatenate([a_ref[...], b_ref[...]], axis=0)
    out_ref[...] = dot(table, rows, NN).astype(jnp.bfloat16)


def combine_rows(first, rows_a, rows_b, slot_source):
    width = rows_a.shape[1]
    groups = rows_a.shape[0] // SLOTS
    lanes = slot_source.shape[1] // 128 - 1
    return pl.pallas_call(
        combine_kernel,
        grid=(groups,),
        out_shape=jax.ShapeDtypeStruct((groups * 512, width), jnp.bfloat16),
        in_specs=[
            pl.BlockSpec(memory_space=pltpu.SMEM),
            pl.BlockSpec((SLOTS, width), lambda i: (i, 0)),
            pl.BlockSpec((SLOTS, width), lambda i: (i, 0)),
            pl.BlockSpec((512, 128), lambda i: (i, lanes)),
        ],
        out_specs=pl.BlockSpec((512, width), lambda i: (i, 0)),
        compiler_params=pltpu.CompilerParams(vmem_limit_bytes=24 * 2**20),
        cost_estimate=pl.CostEstimate(
            flops=2 * groups * 512 * 160 * width,
            bytes_accessed=(groups * 512 + groups * 160) * width * 2, transcendentals=0,
        ),
        name="combine_rows",
    )(first, rows_a, rows_b, slot_source)


def expert_kernel(
    expert_ref, own_ref, left_ref, right_ref, far0_ref, far1_ref, x_hbm, d_hbm, gate_hbm,
    p_hbm, rb_hbm, gw_hbm,
    w, x, d, gate, rg, middle, ggp, gup, p, rb, dots, turned, gw, in_sems, out_sems, gw_sems,
):
    f32, bf16 = jnp.float32, jnp.bfloat16
    rows, width = x.shape
    hidden = middle.shape[1]
    chunk = 256
    shard = own_ref.shape[1]
    loads = [
        pltpu.make_async_copy(x_hbm, x, in_sems.at[0]),
        pltpu.make_async_copy(d_hbm, d, in_sems.at[1]),
        pltpu.make_async_copy(gate_hbm, gate, in_sems.at[2]),
    ]
    at = 0
    for i, ref in enumerate((own_ref, left_ref, right_ref, far0_ref, far1_ref)):
        size = ref.shape[1]
        loads.append(pltpu.make_async_copy(ref, w.at[:, pl.ds(at, size)], in_sems.at[3 + i]))
        at += size
    for load in loads:
        load.start()
    for load in loads:
        load.wait()

    @pl.loop(0, rows, step=16)
    def _(r):
        here = pl.ds(r, 16)
        scaled = d[here].astype(f32) * gate[here, 0:1]
        rg[here] = scaled.astype(bf16)

    for c in range(0, hidden, chunk):
        here = pl.ds(c, chunk)
        gate_pre = dot(x[...], w[0, here], NT)
        up_pre = dot(x[...], w[1, here], NT)
        grad_mid = dot(rg[...], w[2, here], NT)
        sig = 1.0 / (1.0 + jnp.exp(-gate_pre))
        act = gate_pre * sig
        middle[:, here] = (act * up_pre).astype(bf16)
        ggp[:, here] = (grad_mid * up_pre * sig * (1.0 + gate_pre * (1.0 - sig))).astype(bf16)
        gup[:, here] = (grad_mid * act).astype(bf16)

    dots[...] = jnp.zeros_like(dots)

    for n in range(0, width, chunk):
        here = pl.ds(n, chunk)
        out = dot(middle[...], w[2, :, here], NN).astype(bf16).astype(f32)
        p[:, here] = (out * gate[:, 0:1]).astype(bf16)
        along = out * d[:, here].astype(f32)
        dots[...] += along[:, :128] + along[:, 128:]
        back = dot(ggp[...], w[0, :, here], NN) + dot(gup[...], w[1, :, here], NN)
        rb[:, here] = back.astype(bf16)

    expert = expert_ref[0]
    total = jnp.sum(dots[...], axis=1, keepdims=True)
    high = total.astype(bf16).astype(f32)
    lane = lax.broadcasted_iota(jnp.int32, (rows, 128), 1)
    tail = jnp.where(lane == expert, high, jnp.where(lane == expert + 64, total - high, 0.0))
    rb[:, pl.ds(width, 128)] = tail.astype(bf16)
    outs = [
        pltpu.make_async_copy(rb, rb_hbm, out_sems.at[0]),
        pltpu.make_async_copy(p, p_hbm, out_sems.at[1]),
    ]
    for out in outs:
        out.start()

    for i, (left, right) in enumerate(((ggp, x), (gup, x), (middle, rg))):
        turned[...] = left[...].T

        for c in range(0, hidden, chunk):
            here = pl.ds(c, chunk)
            for n in range(0, width, 512):
                there = pl.ds(n, 512)
                gw[i, here, there] = dot(turned[here], right[:, there], NN).astype(bf16)

        save = pltpu.make_async_copy(gw.at[i], gw_hbm.at[i], gw_sems.at[i])
        save.start()
        outs.append(save)
    for out in outs:
        out.wait()


def expert_layer(expert, weights, x, d, gate):
    bf16 = jnp.bfloat16
    rows, width = x.shape
    hidden = sum(part.shape[1] for part in weights)
    any_spec = pl.BlockSpec(memory_space=pl.ANY)
    return pl.pallas_call(
        expert_kernel,
        out_shape=(
            jax.ShapeDtypeStruct((rows, width), bf16),
            jax.ShapeDtypeStruct((rows, width + 128), bf16),
            jax.ShapeDtypeStruct((3, hidden, width), bf16),
        ),
        in_specs=[pl.BlockSpec(memory_space=pltpu.SMEM)] + [any_spec] * 8,
        out_specs=(any_spec, any_spec, any_spec),
        scratch_shapes=[
            pltpu.VMEM((3, hidden, width), bf16),
            pltpu.VMEM((rows, width), bf16),
            pltpu.VMEM((rows, width), bf16),
            pltpu.VMEM((rows, 128), jnp.float32),
            pltpu.VMEM((rows, width), bf16),
            pltpu.VMEM((rows, hidden), bf16),
            pltpu.VMEM((rows, hidden), bf16),
            pltpu.VMEM((rows, hidden), bf16),
            pltpu.VMEM((rows, width), bf16),
            pltpu.VMEM((rows, width + 128), bf16),
            pltpu.VMEM((rows, 128), jnp.float32),
            pltpu.VMEM((hidden, rows), bf16),
            pltpu.VMEM((3, hidden, width), bf16),
            pltpu.SemaphoreType.DMA((8,)),
            pltpu.SemaphoreType.DMA((2,)),
            pltpu.SemaphoreType.DMA((3,)),
        ],
        compiler_params=pltpu.CompilerParams(vmem_limit_bytes=56 * 2**20),
        cost_estimate=pl.CostEstimate(
            flops=18 * rows * hidden * width,
            bytes_accessed=12 * hidden * width + 10 * rows * width,
            transcendentals=rows * hidden,
        ),
        name="expert_layer",
    )(expert, *weights, x, d, gate)


EPSILON = 1e-06
ROPE_BASE = 1000000.0
MASK_VALUE = -1e30
F32 = jnp.float32
BF16 = jnp.bfloat16


def angles(length, head_size):
    position = jnp.arange(length, dtype=jnp.float32)[:, None]
    index_half = jnp.arange(head_size // 2, dtype=jnp.float32)[None, :]
    frequency = jnp.exp(index_half * (-2.0 / head_size) * jnp.log(ROPE_BASE))
    turned = position * frequency
    turned = jnp.concatenate([turned, turned], axis=1)
    return (jnp.cos(turned)[:, None, :], jnp.sin(turned)[:, None, :])


def rotate(values, cosine, sine):
    halfway = values.shape[-1] // 2
    turned = jnp.concatenate([-values[..., halfway:], values[..., :halfway]], axis=-1)
    return values * cosine + turned * sine


def rotate_back(grads, cosine, sine):
    halfway = grads.shape[-1] // 2
    along = grads * sine
    return grads * cosine + jnp.concatenate([along[..., halfway:], -along[..., :halfway]], axis=-1)


def inverse_rms(values):
    return lax.rsqrt(jnp.mean(values * values, axis=-1, keepdims=True) + EPSILON)


def norm_back(values, scales, gain, grads):
    weighted = grads * gain
    return scales * weighted - values * scales * scales * scales * jnp.mean(
        weighted * values, axis=-1, keepdims=True
    )


def along_line(value, step):
    return lax.ppermute(value, "tensor", [(i, (i + step) % 4) for i in range(4)])


def line_weights(own):
    half = own.shape[1] // 2
    left = along_line(own, 1)
    right = along_line(own, -1)
    far_low = along_line(left[:, :half], 1)
    far_high = along_line(right[:, half:], -1)
    return (own, left, right, far_low, far_high)


def line_grads(grads):
    shard = grads.shape[1] // 4
    half = shard // 2
    far = 3 * shard
    low = along_line(grads[:, far : far + half], -1)
    high = along_line(grads[:, far + half :], 1)

    def plus(a, b):
        return (a.astype(F32) + b.astype(F32)).astype(BF16)

    left = jnp.concatenate(
        [plus(grads[:, shard : shard + half], low), grads[:, shard + half : 2 * shard]], axis=1
    )
    right = jnp.concatenate(
        [grads[:, 2 * shard : 2 * shard + half], plus(grads[:, 2 * shard + half : far], high)], axis=1
    )
    from_right = along_line(left, -1)
    from_left = along_line(right, 1)
    return grads[:, :shard].astype(F32) + from_right.astype(F32) + from_left.astype(F32)


def per_device(
    inputs,
    attn_gain,
    w_query,
    w_key,
    w_value,
    q_gain,
    k_gain,
    w_out,
    mlp_gain,
    w_router,
    w_gate,
    w_up,
    w_down,
    routes,
    grad_out,
):
    f32, bf16 = F32, BF16
    row_count, model_width = inputs.shape
    head_size = q_gain.shape[0]
    expert_count = w_router.shape[1]
    query_heads = w_query.shape[1] // head_size
    key_heads = w_key.shape[1] // head_size
    group_size = query_heads // key_heads
    scale_factor = head_size ** (-0.5)
    place = lax.axis_index("expert")
    first = (2 * place).astype(jnp.int32).reshape(1)

    chosen = routes[:, :, None] == jnp.arange(expert_count, dtype=jnp.int32)[None, None, :]
    picks = jnp.sum(chosen.astype(f32), axis=1)
    before = (jnp.arange(row_count)[:, None] > jnp.arange(row_count)[None, :]).astype(bf16)
    rank = jnp.dot(before, picks.astype(bf16), preferred_element_type=f32)
    slots = jnp.where(picks > 0.0, rank + (20 * (place % 4)).astype(f32), -1.0)
    slots = jnp.concatenate([slots, jnp.full_like(slots, -1.0)], axis=1).astype(bf16)
    dout_all = lax.all_gather(
        jnp.concatenate([grad_out, slots], axis=1), "expert", axis=0, tiled=True
    )

    float_in = inputs.astype(f32)
    first_scale = inverse_rms(float_in)
    normed = (float_in * first_scale * attn_gain).astype(bf16)
    seq_rows = gather_line(normed, 0).reshape(-1, model_width)

    gate_t = jnp.swapaxes(w_gate, 1, 2)
    up_t = jnp.swapaxes(w_up, 1, 2)
    own = [jnp.stack([gate_t[j], up_t[j], w_down[j]]) for j in range(2)]
    seq_rows, own[0], own[1] = lax.optimization_barrier((seq_rows, own[0], own[1]))
    weights = [line_weights(part) for part in own]

    length = seq_rows.shape[0]
    queries = jnp.dot(seq_rows, w_query, preferred_element_type=f32).reshape(
        length, query_heads, head_size
    )
    keys_raw = jnp.dot(seq_rows, w_key, preferred_element_type=f32).reshape(
        length, key_heads, head_size
    )
    values_low = (
        jnp.dot(seq_rows, w_value, preferred_element_type=f32)
        .astype(bf16)
        .reshape(length, key_heads, head_size)
    )
    cosine, sine = angles(length, head_size)
    query_scale = inverse_rms(queries)
    key_scale = inverse_rms(keys_raw)
    query_rot = rotate(queries * query_scale * q_gain, cosine, sine).astype(bf16)
    key_rot = rotate(keys_raw * key_scale * k_gain, cosine, sine).astype(bf16)
    query_group = query_rot.reshape(length, key_heads, group_size, head_size)
    causal = jnp.arange(length)[:, None] >= jnp.arange(length)[None, :]
    scores = (
        jnp.einsum("skgd,tkd->kgst", query_group, key_rot, preferred_element_type=f32)
        * scale_factor
    )
    scores = jnp.where(causal, scores, MASK_VALUE)
    row_peak = jnp.max(scores, axis=-1, keepdims=True)
    exp_scores = jnp.exp(scores - row_peak)
    denominator = jnp.sum(exp_scores, axis=-1, keepdims=True)
    attn_probs = exp_scores / denominator
    log_norm = row_peak + jnp.log(denominator)
    context = jnp.einsum(
        "kgst,tkd->skgd", attn_probs.astype(bf16), values_low, preferred_element_type=f32
    )
    context = context.reshape(length, query_heads * head_size).astype(bf16)
    partial = jnp.dot(context, w_out, preferred_element_type=f32).astype(bf16)
    attended = scatter_line(partial.reshape(4, row_count, model_width), 1)

    hidden = float_in + attended
    second_scale = inverse_rms(hidden)
    mixed_in = (hidden * second_scale * mlp_gain).astype(bf16)
    logits = jnp.dot(mixed_in, w_router, preferred_element_type=f32)
    router_peak = jnp.max(logits, axis=-1, keepdims=True)
    router_exp = jnp.exp(logits - router_peak)
    router_probs = router_exp / jnp.sum(router_exp, axis=-1, keepdims=True)
    picked_total = jnp.sum(picks * router_probs, axis=-1, keepdims=True)
    gate_values = picks * router_probs / picked_total
    gate_high = gate_values.astype(bf16)
    gate_low = (gate_values - gate_high.astype(f32)).astype(bf16)

    mixed_all = gather_plane(jnp.concatenate([mixed_in, gate_high, gate_low], axis=1), 2)
    mixed_all = mixed_all.reshape(-1, model_width + 128)
    grad_a, grad_b, _, _ = select_rows(first, dout_all, dout_all)
    rows_a, rows_b, gate_a, gate_b = select_rows(first, mixed_all, dout_all)
    out_a, back_a, gw_a = expert_layer(first, weights[0], rows_a, grad_a, gate_a)
    out_b, back_b, gw_b = expert_layer(first + 1, weights[1], rows_b, grad_b, gate_b)
    back = combine_rows(first, back_a, back_b, dout_all)
    shares = combine_rows(first, out_a, out_b, dout_all)
    back = scatter_plane(back.reshape(-1, row_count, model_width + 128), 3)
    expert_mix = lax.psum_scatter(shares, "expert", scatter_dimension=0, tiled=True)
    output = (hidden + expert_mix.astype(f32)).astype(bf16)
    gw_a = line_grads(gw_a)
    gw_b = line_grads(gw_b)

    dout = grad_out.astype(f32)
    tail = back[:, model_width:]
    gate_grad = tail[:, :expert_count] + tail[:, expert_count:]
    prob_grad = (
        picks
        * (gate_grad - jnp.sum(gate_grad * gate_values, axis=-1, keepdims=True))
        / picked_total
    )
    logit_grad = (
        router_probs * (prob_grad - jnp.sum(prob_grad * router_probs, axis=-1, keepdims=True))
    ).astype(bf16)
    grad_router = jnp.dot(mixed_in.T, logit_grad, preferred_element_type=f32)
    grad_mixed = back[:, :model_width] + jnp.dot(
        logit_grad, w_router.T, preferred_element_type=f32
    )
    grad_hidden = dout + norm_back(hidden, second_scale, mlp_gain, grad_mixed)
    mlp_gain_grad = jnp.sum(grad_mixed * hidden * second_scale, axis=0)
    grad_router, mlp_gain_grad = lax.psum((grad_router, mlp_gain_grad), ("expert", "tensor"))

    grad_att = grad_hidden.astype(bf16)
    grad_seq_rows = gather_line(grad_att, 4).reshape(-1, model_width)
    grad_out_w = jnp.dot(context.T, grad_seq_rows, preferred_element_type=f32)
    grad_out_w = lax.psum(grad_out_w.astype(bf16), "expert").astype(f32)
    grad_context = jnp.dot(grad_seq_rows, w_out.T, preferred_element_type=f32).astype(bf16)
    grad_context = grad_context.reshape(length, key_heads, group_size, head_size)
    again = (
        jnp.einsum("skgd,tkd->kgst", query_group, key_rot, preferred_element_type=f32)
        * scale_factor
    )
    again = jnp.where(causal, again, MASK_VALUE)
    probs_again = jnp.exp(again - log_norm)
    grad_probs = jnp.einsum("skgd,tkd->kgst", grad_context, values_low, preferred_element_type=f32)
    grad_values = jnp.einsum(
        "kgst,skgd->tkd", probs_again.astype(bf16), grad_context, preferred_element_type=f32
    )
    grad_values = grad_values.astype(bf16).reshape(length, key_heads * head_size)
    grad_scores = probs_again * (
        grad_probs - jnp.sum(grad_probs * probs_again, axis=-1, keepdims=True)
    )
    grad_scores = grad_scores.astype(bf16)
    grad_query_rot = (
        jnp.einsum("kgst,tkd->skgd", grad_scores, key_rot, preferred_element_type=f32)
        * scale_factor
    )
    grad_key_rot = (
        jnp.einsum("kgst,skgd->tkd", grad_scores, query_group, preferred_element_type=f32)
        * scale_factor
    )
    grad_q_norm = rotate_back(grad_query_rot.reshape(length, query_heads, head_size), cosine, sine)
    grad_k_norm = rotate_back(grad_key_rot, cosine, sine)
    q_gain_grad = jnp.sum(grad_q_norm * queries * query_scale, axis=(0, 1))
    k_gain_grad = jnp.sum(grad_k_norm * keys_raw * key_scale, axis=(0, 1))
    grad_queries = (
        norm_back(queries, query_scale, q_gain, grad_q_norm)
        .astype(bf16)
        .reshape(length, query_heads * head_size)
    )
    grad_keys = (
        norm_back(keys_raw, key_scale, k_gain, grad_k_norm)
        .astype(bf16)
        .reshape(length, key_heads * head_size)
    )
    grad_query_w = jnp.dot(seq_rows.T, grad_queries, preferred_element_type=f32)
    grad_key_w = jnp.dot(seq_rows.T, grad_keys, preferred_element_type=f32)
    grad_value_w = jnp.dot(seq_rows.T, grad_values, preferred_element_type=f32)
    summed = jnp.dot(grad_queries, w_query.T, preferred_element_type=f32)
    summed = summed + jnp.dot(grad_keys, w_key.T, preferred_element_type=f32)
    summed = summed + jnp.dot(grad_values, w_value.T, preferred_element_type=f32)
    grad_normed = scatter_line(summed.astype(bf16).reshape(4, row_count, model_width), 5)
    grad_inputs = (grad_hidden + norm_back(float_in, first_scale, attn_gain, grad_normed)).astype(
        bf16
    )
    attn_gain_grad = jnp.sum(grad_normed * float_in * first_scale, axis=0)
    attn_gain_grad, q_gain_grad, k_gain_grad = lax.psum(
        (attn_gain_grad, q_gain_grad, k_gain_grad), ("expert", "tensor")
    )
    attn_w = jnp.concatenate(
        [grad_query_w.astype(bf16), grad_key_w.astype(bf16), grad_value_w.astype(bf16)], axis=1
    )
    query_width = w_query.shape[1]
    key_width = w_key.shape[1]
    attn_w = scatter_plane(attn_w.reshape(32, -1, attn_w.shape[1]), 6)
    attn_w = gather_plane(attn_w.astype(bf16), 7).reshape(model_width, -1).astype(f32)
    gw = [jnp.swapaxes(jnp.stack([gw_a[i], gw_b[i]]), 1, 2) for i in range(2)]
    return (
        output,
        grad_inputs,
        attn_gain_grad,
        attn_w[:, :query_width],
        attn_w[:, query_width : query_width + key_width],
        attn_w[:, query_width + key_width :],
        q_gain_grad,
        k_gain_grad,
        grad_out_w,
        mlp_gain_grad,
        grad_router,
        gw[0],
        gw[1],
        jnp.stack([gw_a[2], gw_b[2]]),
    )


def solution(mesh):
    placed = (
        P(("expert", "tensor"), None),
        P(),
        P(None, "tensor"),
        P(None, "tensor"),
        P(None, "tensor"),
        P(),
        P(),
        P("tensor", None),
        P(),
        P(),
        P("expert", None, "tensor"),
        P("expert", None, "tensor"),
        P("expert", "tensor", None),
        P(("expert", "tensor"), None),
        P(("expert", "tensor"), None),
    )
    return jax.shard_map(
        per_device,
        mesh=mesh,
        in_specs=placed,
        out_specs=(
            P(("expert", "tensor"), None),
            P(("expert", "tensor"), None),
            P(),
            P(None, "tensor"),
            P(None, "tensor"),
            P(None, "tensor"),
            P(),
            P(),
            P("tensor", None),
            P(),
            P(),
            P("expert", None, "tensor"),
            P("expert", None, "tensor"),
            P("expert", "tensor", None),
        ),
        check_vma=False,
    )
```

time: 1100 us -> 897 us (0.82)
  Pallas kernels: 0 us -> 481 us
  waiting for transfers between devices: 436 us -> 50.7 us
  matrix products: 184 us -> 49.2 us
  local copies, waits for them, and re-layouts: 217 us -> 122 us
  starting transfers between devices: 59.6 us -> 20.9 us
  other arithmetic: 102 us -> 79.5 us
  blocking collectives: 77.1 us -> 66 us
    pallas_call x0 -> x14, Pallas kernels: none -> 481 us  [the longest x2 175 us: scatter_line(): pl.pallas_call(line_scatter_outer, out_shape=jax.ShapeDtypeStruct((rows,...]
    all_to_all x8 -> x0, waiting for transfers between devices: 163 us -> none  [the longest x2 48.6 us: sent_to_all(): lax.all_to_all(jnp.broadcast_to(x[None], (peers, *x.shape)), axis, 0, 0,...]
    dot_general x10 -> x2, matrix products: 141 us -> 2.52 us  [the longest x1 2.38 us: per_device(): partial = jnp.dot(context, w_out, preferred_element_type=f32).astype(bf16)]
    reduce_scatter x3 -> x1, waiting for transfers between devices: 125 us -> 0.01 us  [per_device(): lax.psum_scatter(shares, 'expert', scatter_dimension=0, tiled=True)]
    psum x2, waiting for transfers between devices: 147 us -> 50.6 us  [the longest x1 50.5 us: per_device(): lax.psum((grad_router, mlp_gain_grad), ('expert', 'tensor'))]
    reshape x10 -> x2, local copies, waits for them, and re-layouts: 68.8 us -> 5.09 us  [the longest x1 3.1 us: per_device(): jnp.dot(seq_rows, w_query, preferred_element_type=f32)]
    all_to_all x8 -> x0, starting transfers between devices: 59.4 us -> none  [the longest x1 16 us: per_device(): lax.all_to_all(send_buffer, 'expert', split_axis=0, concat_axis=0, tiled=...]
    unnamed x161 -> x207, local copies, waits for them, and re-layouts: 17.5 us -> 56.4 us
  transfers between devices with their start and end apart: 14 -> 20, of which waited for: 11 -> 1; matrix products, arithmetic and copies ran while one was open for 33% -> 21% of each run, Pallas kernels for 0% -> 42%
where the time goes in v1:
time: 897 us; the launch traced here: 885 us
  Pallas kernels  481 us (54%)
  local copies, waits for them, and re-layouts  122 us (14%)
  other arithmetic  79.5 us (9%)
  blocking collectives  66 us (7%)
  waiting for transfers between devices  50.7 us (6%)
  matrix products  49.2 us (5%)
  starting transfers between devices  20.9 us (2%)
  between operations  15.5 us (2%)
    pallas_call x2, Pallas kernels, scatter_line(): pl.pallas_call(line_scatter_outer, out_shape=jax.ShapeDtypeStruct((rows,...  175 us
    pallas_call x2, Pallas kernels, gather_plane(): pl.pallas_call(gather_kernel, out_shape=jax.ShapeDtypeStruct((32, *x.shap...  87.8 us
    pallas_call x2, Pallas kernels, scatter_plane(): pl.pallas_call(scatter_kernel, out_shape=jax.ShapeDtypeStruct((rows, widt...  82.1 us
    psum x1, blocking collectives, per_device(): lax.psum((attn_gain_grad, q_gain_grad, k_gain_grad), ('expert', 'tensor'))  66 us
    pallas_call x2, Pallas kernels, expert_layer(): pl.pallas_call(expert_kernel, out_shape=(jax.ShapeDtypeStruct((rows, widt...  61.9 us
    unnamed x207, local copies, waits for them, and re-layouts  56.4 us
    psum x1, waiting for transfers between devices, per_device(): lax.psum((grad_router, mlp_gain_grad), ('expert', 'tensor'))  50.5 us
    pallas_call x2, Pallas kernels, gather_line(): pl.pallas_call(line_gather_kernel, out_shape=jax.ShapeDtypeStruct((4, *x....  41.8 us
  transfers between devices with their start and end apart: 20, of which 1 were waited for; matrix products, arithmetic and copies ran while one was open for 21% of the time, Pallas kernels for 42%

profile of v1, /device:TPU:1, one launch (start us, length us, event | category | flops | bytes accessed | tf_op | source)
XLA Modules:
  0.0 885.4 jit_solution(8329113201436360877)
XLA Ops:
  12.7 21.9 %gather_line.2 = bf16[4,128,2048]{2,1,0:T(8,128)(2,1)} custom-call(bf16[128,2048]{1,0:T(8,128)(2,1)} %fusion.29.x_ref), custom_call_target="tpu_custom_call" | custom-call | tf_op jit(solution)/shard_map/gather_line/pallas_call | solution.py:412
  36.6 2.7 pad_maximum_fusion.2
  50.2 3.1 copy.120
  62.5 2.9 copy.150
  67.0 3.0 copy.149
  71.5 2.9 copy.148
  76.5 5.3 fusion.84
  89.8 69.0 %scatter_line.2 = f32[128,2048]{1,0:T(8,128)S(1)} custom-call(bf16[4,128,2048]{2,1,0:T(8,128)(2,1)S(1)} %bitcast.191), custom_call_target="tpu_custom_call" | custom-call | tf_op jit(solution)/shard_map/scatter_line/pallas_call | solution.py:485
  159.3 2.8 slice.187
  169.3 61.4 %gather_plane.2 = bf16[32,128,2176]{2,1,0:T(8,128)(2,1)} custom-call(bf16[128,2176]{1,0:T(8,128)(2,1)} %concatenate.76.x_ref), custom_call_target="tpu_custom_call" | custom-call | tf_op jit(solution)/shard_map/gather_plane/pallas_call | solution.py:206
  237.2 6.1 copy-done.1
  243.3 8.3 select_rows.3
  254.5 6.1 copy-done.2
  260.6 8.4 select_rows.2
  273.4 30.7 %expert_layer.2 = (bf16[640,2048]{1,0:T(8,128)(2,1)}, bf16[640,2176]{1,0:T(8,128)(2,1)}, bf16[3,768,2048]{2,1,0:T(8,128)(2,1)}) custom-call(s32[1]{0:T(128)} %bitcast.19.first_ref.expert_ref, bf16[3,192,2048]{2,1,0:T(8,128)(2,1)} %get-tuple-element.30.own_ref, bf16[3,192,2048]{2,1,0:T(8,128)(2,1)} %collective-permute-done.left_ref, ...), custom_call_target="tpu_custom_call" | custom-call | flops 18119393280 | bytes 31981568 | tf_op jit(solution)/shard_map/expert_layer/pallas_call | solution.py:689
  304.2 31.1 %expert_layer.3 = (bf16[640,2048]{1,0:T(8,128)(2,1)}, bf16[640,2176]{1,0:T(8,128)(2,1)}, bf16[3,768,2048]{2,1,0:T(8,128)(2,1)}) custom-call(s32[1]{0:T(128)S(6)} %add.158.expert_ref, bf16[3,192,2048]{2,1,0:T(8,128)(2,1)} %get-tuple-element.35.own_ref, bf16[3,192,2048]{2,1,0:T(8,128)(2,1)} %collective-permute-done.4.left_ref, ...), custom_call_target="tpu_custom_call" | custom-call | flops 18119393280 | bytes 31981568 | tf_op jit(solution)/shard_map/expert_layer/pallas_call | solution.py:689
  337.2 8.1 combine_rows.3
  345.3 6.1 copy-done.3
  351.3 54.3 %scatter_plane.2 = f32[128,2176]{1,0:T(8,128)S(1)} custom-call(bf16[32,128,2176]{2,1,0:T(8,128)(2,1)} %bitcast.188), custom_call_target="tpu_custom_call" | custom-call | tf_op jit(solution)/shard_map/scatter_plane/pallas_call | solution.py:349
  409.4 19.9 %gather_line.3 = bf16[4,128,2048]{2,1,0:T(8,128)(2,1)} custom-call(bf16[128,2048]{1,0:T(8,128)(2,1)} %fusion.70.x_ref), custom_call_target="tpu_custom_call" | custom-call | tf_op jit(solution)/shard_map/gather_line/pallas_call | solution.py:412
  429.3 5.9 convolution_convert_fusion
  438.7 7.8 combine_rows.2
  446.6 5.8 copy-done.4
  452.5 5.0 fusion.75
  460.2 5.1 fusion.76
  471.1 4.7 fusion.5
  475.9 8.1 copy.138
  485.2 3.0 bitcast_multiply_fusion.2
  492.1 2.9 copy.152
  497.0 6.0 fusion.55
  513.4 7.5 pad_maximum_fusion
  521.0 8.0 copy.139
  531.6 27.8 %scatter_plane.3 = f32[64,1280]{1,0:T(8,128)S(1)} custom-call(bf16[32,64,1280]{2,1,0:T(8,128)(2,1)S(1)} %bitcast.189), custom_call_target="tpu_custom_call" | custom-call | tf_op jit(solution)/shard_map/scatter_plane/pallas_call | solution.py:349
  560.1 26.3 %gather_plane.3 = bf16[32,64,1280]{2,1,0:T(8,128)(2,1)} custom-call(bf16[64,1280]{1,0:T(8,128)(2,1)} %convert_element_type.230.x_ref), custom_call_target="tpu_custom_call" | custom-call | tf_op jit(solution)/shard_map/gather_plane/pallas_call | solution.py:206
  587.2 5.9 fusion.87
  595.2 5.1 bitcast_convert_fusion
  600.3 3.3 add_convert_fusion.4
  605.2 2.8 collective-permute-start.9
  610.9 3.4 add_convert_fusion.2
  620.3 4.7 slice.195
  625.1 106.1 %scatter_line.3 = f32[128,2048]{1,0:T(8,128)S(1)} custom-call(bf16[4,128,2048]{2,1,0:T(8,128)(2,1)S(1)} %bitcast.190), custom_call_target="tpu_custom_call" | custom-call | tf_op jit(solution)/shard_map/scatter_line/pallas_call | solution.py:485
  731.6 66.0 %all-reduce.1 = (f32[2048]{0:T(1024)}, f32[128]{0:T(128)}, f32[128]{0:T(128)}, f32[2048]{0:T(1024)}) all-reduce(f32[2048]{0:T(1024)S(1)} %get-tuple-element.46, f32[128]{0:T(128)S(1)} %bitcast_reduce_fusion, f32[128]{0:T(128)S(1)} %get-tuple-element.48, ...), channel_id=1, replica_groups=mesh['expert'=32,'tensor'=4] {'expert','tensor'}, use_global_device_ids=true, to_apply=%region_19.20 | all-reduce | flops 4352 | bytes 34816 | tf_op jit(solution)/shard_map/psum | solution.py:983
  797.6 3.0 fusion.74
  800.6 6.7 convert_element_type.234
  807.3 4.5 convert_add_fusion.1
  812.4 4.5 convert_add_fusion
  823.1 3.1 fusion.34
  826.2 50.5 %all-reduce.7.cloned.1.call-done = f32[2048,64]{0,1:T(8,128)} async-done(((f32[2048,64]{0,1:T(8,128)}), f32[2048,64]{0,1:T(8,128)}) %all-reduce.7.cloned.1.call-update) | async-done | bytes 524304 | tf_op jit(solution)/shard_map/psum | solution.py:927
  (331 shorter events, 122.0 us)
Async XLA Ops:
  7.2 48.4 %copy-start = (bf16[2048,128]{1,0:T(8,128)(2,1)S(1)}, bf16[2048,128]{1,0:T(8,128)(2,1)}, u32[]{:S(2)}) copy-start(bf16[2048,128]{1,0:T(8,128)(2,1)} %param.18) | copy-start | bytes 1572868
  7.2 230.0 %all-gather.2.cloned.1.call-start = ((), (), s32[]{:S(2)}) async-start(), calls=%async_computation.1 | async-start | bytes 18382848 | tf_op jit(solution)/shard_map/all_gather | solution.py:833
  10.2 24.3 %copy-start.52 = (bf16[2,2048,192]{1,2,0:T(8,128)(2,1)S(1)}, bf16[2,2048,192]{1,2,0:T(8,128)(2,1)}, u32[]{:S(2)}) copy-start(bf16[2,2048,192]{1,2,0:T(8,128)(2,1)} %param.25) | copy-start | bytes 4718596
  10.3 790.4 %all-reduce.5.cloned.1.call-start = ((), (), s32[]{:S(2)}) async-start(), calls=%async_computation.3 | async-start | bytes 8388608 | tf_op jit(solution)/shard_map/psum | solution.py:932
  11.7 23.0 %copy-start.86 = (f32[128]{0:T(128)}, f32[128]{0:T(128)S(1)}, u32[]{:S(2)}) copy-start(f32[128]{0:T(128)S(1)} %add_rsqrt_fusion.3) | copy-start | bytes 1540
  36.6 8.1 copy-start.18
  36.6 8.1 copy-start.92
  39.3 119.9 %collective-permute-start = (bf16[3,192,2048]{2,1,0:T(8,128)(2,1)}, bf16[3,192,2048]{2,1,0:T(8,128)(2,1)}, u32[]{:S(2)}, u32[]{:S(2)}) collective-permute-start(bf16[3,192,2048]{2,1,0:T(8,128)(2,1)} %get-tuple-element.30.own_ref), channel_id=1, source_target_pairs={{0,1},{1,2},{2,3},{3,0},{4,5},{5,6},{6,7},{7,4},{8,9},{9,10},{10,1... | collective-permute-start | bytes 7077896 | tf_op jit(solution)/shard_map/ppermute | solution.py:766
  39.9 122.6 %collective-permute-start.1 = (bf16[3,192,2048]{2,1,0:T(8,128)(2,1)}, bf16[3,192,2048]{2,1,0:T(8,128)(2,1)}, u32[]{:S(2)}, u32[]{:S(2)}) collective-permute-start(bf16[3,192,2048]{2,1,0:T(8,128)(2,1)} %get-tuple-element.30.own_ref), channel_id=1, source_target_pairs={{0,3},{1,0},{2,1},{3,2},{4,7},{5,4},{6,5},{7,6},{8,11},{9,8},{10,9... | collective-permute-start | bytes 7077896 | tf_op jit(solution)/shard_map/ppermute | solution.py:766
  42.0 188.7 %collective-permute-start.4 = (bf16[3,192,2048]{2,1,0:T(8,128)(2,1)}, bf16[3,192,2048]{2,1,0:T(8,128)(2,1)}, u32[]{:S(2)}, u32[]{:S(2)}) collective-permute-start(bf16[3,192,2048]{2,1,0:T(8,128)(2,1)} %get-tuple-element.35.own_ref), channel_id=1, source_target_pairs={{0,1},{1,2},{2,3},{3,0},{4,5},{5,6},{6,7},{7,4},{8,9},{9,10},{10,1... | collective-permute-start | bytes 7077896 | tf_op jit(solution)/shard_map/ppermute | solution.py:766
  42.0 190.1 %collective-permute-start.5 = (bf16[3,192,2048]{2,1,0:T(8,128)(2,1)}, bf16[3,192,2048]{2,1,0:T(8,128)(2,1)}, u32[]{:S(2)}, u32[]{:S(2)}) collective-permute-start(bf16[3,192,2048]{2,1,0:T(8,128)(2,1)} %get-tuple-element.35.own_ref), channel_id=1, source_target_pairs={{0,3},{1,0},{2,1},{3,2},{4,7},{5,4},{6,5},{7,6},{8,11},{9,8},{10,9... | collective-permute-start | bytes 7077896 | tf_op jit(solution)/shard_map/ppermute | solution.py:766
  89.8 69.3 %copy-start.63 = (f32[2048]{0:T(1024)S(1)}, f32[2048]{0:T(1024)}, u32[]{:S(2)}) copy-start(f32[2048]{0:T(1024)} %param.23) | copy-start | bytes 24580
  159.0 248.2 %copy-start.20 = (f32[128,2048]{1,0:T(8,128)}, f32[128,2048]{1,0:T(8,128)S(1)}, u32[]{:S(2)}) copy-start(f32[128,2048]{1,0:T(8,128)S(1)} %get-tuple-element.60) | copy-start | bytes 3145732
  159.0 248.2 %copy-start.79 = (f32[128]{0:T(128)}, f32[128]{0:T(128)S(1)}, u32[]{:S(2)}) copy-start(f32[128]{0:T(128)S(1)} %add_rsqrt_fusion.2) | copy-start | bytes 1540
  159.2 9.1 %copy-start.34 = (bf16[128,2048]{1,0:T(8,128)(2,1)}, bf16[128,2048]{1,0:T(8,128)(2,1)S(1)}, u32[]{:S(2)}) copy-start(bf16[128,2048]{1,0:T(8,128)(2,1)S(1)} %multiply_convert_fusion) | copy-start | bytes 1572868
  159.2 8.1 copy-start.58
  159.2 8.7 copy-start.57
  162.1 111.4 %collective-permute-start.2 = (bf16[3,96,2048]{2,1,0:T(8,128)(2,1)}, bf16[3,96,2048]{2,1,0:T(8,128)(2,1)}, u32[]{:S(2)}, u32[]{:S(2)}) collective-permute-start(bf16[3,96,2048]{2,1,0:T(8,128)(2,1)} %slice.187), channel_id=1, source_target_pairs={{0,1},{1,2},{2,3},{3,0},{4,5},{5,6},{6,7},{7,4},{8,9},{9,10},{10,1... | collective-permute-start | bytes 3538952 | tf_op jit(solution)/shard_map/ppermute | solution.py:766
  164.9 108.5 %collective-permute-start.3 = (bf16[3,96,2048]{2,1,0:T(8,128)(2,1)}, bf16[3,96,2048]{2,1,0:T(8,128)(2,1)}, u32[]{:S(2)}, u32[]{:S(2)}) collective-permute-start(bf16[3,96,2048]{2,1,0:T(8,128)(2,1)} %slice.188), channel_id=1, source_target_pairs={{0,3},{1,0},{2,1},{3,2},{4,7},{5,4},{6,5},{7,6},{8,11},{9,8},{10,9... | collective-permute-start | bytes 3538952 | tf_op jit(solution)/shard_map/ppermute | solution.py:766
  167.7 238.4 %copy-start.72 = (f32[128]{0:T(128)}, f32[128]{0:T(128)S(1)}, u32[]{:S(2)}) copy-start(f32[128]{0:T(128)S(1)} %get-tuple-element.114) | copy-start | bytes 1540
  168.0 238.1 %copy-start.74 = (f32[128]{0:T(128)}, f32[128]{0:T(128)S(1)}, u32[]{:S(2)}) copy-start(f32[128]{0:T(128)S(1)} %fusion.64) | copy-start | bytes 1540
  232.1 72.1 %collective-permute-start.6 = (bf16[3,96,2048]{2,1,0:T(8,128)(2,1)S(1)}, bf16[3,96,2048]{2,1,0:T(8,128)(2,1)}, u32[]{:S(2)}, u32[]{:S(2)}) collective-permute-start(bf16[3,96,2048]{2,1,0:T(8,128)(2,1)S(1)} %slice.189), channel_id=1, source_target_pairs={{0,1},{1,2},{2,3},{3,0},{4,5},{5,6},{6,7},{7,4},{8,9},{9,10},{10,1... | collective-permute-start | bytes 3538952 | tf_op jit(solution)/shard_map/ppermute | solution.py:766
  234.6 69.6 %collective-permute-start.7 = (bf16[3,96,2048]{2,1,0:T(8,128)(2,1)}, bf16[3,96,2048]{2,1,0:T(8,128)(2,1)}, u32[]{:S(2)}, u32[]{:S(2)}) collective-permute-start(bf16[3,96,2048]{2,1,0:T(8,128)(2,1)} %slice.190), channel_id=1, source_target_pairs={{0,3},{1,0},{2,1},{3,2},{4,7},{5,4},{6,5},{7,6},{8,11},{9,8},{10,9... | collective-permute-start | bytes 3538952 | tf_op jit(solution)/shard_map/ppermute | solution.py:766
  304.2 31.1 %copy-start.7 = (bf16[640,2176]{1,0:T(8,128)(2,1)S(1)}, bf16[640,2176]{1,0:T(8,128)(2,1)}, u32[]{:S(2)}) copy-start(bf16[640,2176]{1,0:T(8,128)(2,1)} %get-tuple-element.40.a_ref) | copy-start | bytes 8355844
  407.2 22.1 %copy-start.88 = (f32[128]{0:T(128)}, f32[128]{0:T(128)S(1)}, u32[]{:S(2)}) copy-start(f32[128]{0:T(128)S(1)} %broadcast_multiply_fusion.3) | copy-start | bytes 1540
  408.2 21.1 %copy-start.94 = (bf16[128,8,512]{2,0,1:T(8,128)(2,1)S(1)}, bf16[128,8,512]{2,0,1:T(8,128)(2,1)}, u32[]{:S(2)}) copy-start(bf16[128,8,512]{2,0,1:T(8,128)(2,1)} %copy-done.93) | copy-start | bytes 3145732
  435.3 387.8 %reduce-scatter.2.cloned.1.call-start = ((), (), s32[]{:S(2)}) async-start(), calls=%async_computation.2 | async-start | bytes 17301504 | tf_op jit(solution)/shard_map/reduce_scatter | solution.py:905
  452.5 424.3 %all-reduce.7.cloned.1.call-start = ((), (), s32[]{:S(2)}) async-start(), calls=%async_computation.4 | async-start | bytes 1048576 | tf_op jit(solution)/shard_map/psum | solution.py:927
  452.5 14.2 %copy-start.91 = (bf16[1024,2048]{1,0:T(8,128)(2,1)S(1)}, bf16[1024,2048]{1,0:T(8,128)(2,1)}, u32[]{:S(2)}) copy-start(bf16[1024,2048]{1,0:T(8,128)(2,1)} %param.22) | copy-start | bytes 12582916
  457.5 142.8 %collective-permute-start.10 = (bf16[3,96,2048]{2,1,0:T(8,128)(2,1)}, bf16[3,96,2048]{2,1,0:T(8,128)(2,1)}, u32[]{:S(2)}, u32[]{:S(2)}) collective-permute-start(bf16[3,96,2048]{2,1,0:T(8,128)(2,1)} %get-tuple-element.68), channel_id=1, source_target_pairs={{0,1},{1,2},{2,3},{3,0},{4,5},{5,6},{6,7},{7,4},{8,9},{9,10},{10,1... | collective-permute-start | bytes 3538952 | tf_op jit(solution)/shard_map/ppermute | solution.py:766
  457.8 142.5 %collective-permute-start.8 = (bf16[3,96,2048]{2,1,0:T(8,128)(2,1)}, bf16[3,96,2048]{2,1,0:T(8,128)(2,1)}, u32[]{:S(2)}, u32[]{:S(2)}) collective-permute-start(bf16[3,96,2048]{2,1,0:T(8,128)(2,1)} %get-tuple-element.67), channel_id=1, source_target_pairs={{0,3},{1,0},{2,1},{3,2},{4,7},{5,4},{6,5},{7,6},{8,11},{9,8},{10,9... | collective-permute-start | bytes 3538952 | tf_op jit(solution)/shard_map/ppermute | solution.py:766
  460.2 8.9 %slice-start = ((s8[8388608]{0:T(1024)(128)(4,1)}), s8[4194304]{0:T(1024)(128)(4,1)S(1)}, s32[]{:S(2)}) async-start(s8[8388608]{0:T(1024)(128)(4,1)} %bitcast.192), calls=%async_computation.5 | async-start | bytes 8388608
  465.3 145.6 %collective-permute-start.12 = (bf16[3,96,2048]{2,1,0:T(8,128)(2,1)}, bf16[3,96,2048]{2,1,0:T(8,128)(2,1)}, u32[]{:S(2)}, u32[]{:S(2)}) collective-permute-start(bf16[3,96,2048]{2,1,0:T(8,128)(2,1)} %get-tuple-element.73), channel_id=1, source_target_pairs={{0,3},{1,0},{2,1},{3,2},{4,7},{5,4},{6,5},{7,6},{8,11},{9,8},{10,9... | collective-permute-start | bytes 3538952 | tf_op jit(solution)/shard_map/ppermute | solution.py:766
  465.5 145.4 %collective-permute-start.14 = (bf16[3,96,2048]{2,1,0:T(8,128)(2,1)}, bf16[3,96,2048]{2,1,0:T(8,128)(2,1)}, u32[]{:S(2)}, u32[]{:S(2)}) collective-permute-start(bf16[3,96,2048]{2,1,0:T(8,128)(2,1)} %get-tuple-element.74), channel_id=1, source_target_pairs={{0,1},{1,2},{2,3},{3,0},{4,5},{5,6},{6,7},{7,4},{8,9},{9,10},{10,1... | collective-permute-start | bytes 3538952 | tf_op jit(solution)/shard_map/ppermute | solution.py:766
  475.8 9.4 %copy-start.49 = (f32[512,128]{0,1:T(8,128)S(1)}, f32[512,128]{0,1:T(8,128)}, u32[]{:S(2)}) copy-start(f32[512,128]{0,1:T(8,128)} %copy-done.48) | copy-start | bytes 786436
  586.4 8.8 slice-start.5
  587.2 8.0 slice-start.6
  605.2 202.1 %collective-permute-start.9 = (bf16[3,192,2048]{2,1,0:T(8,128)(2,1)}, bf16[3,192,2048]{2,1,0:T(8,128)(2,1)}, u32[]{:S(2)}, u32[]{:S(2)}) collective-permute-start(bf16[3,192,2048]{2,1,0:T(8,128)(2,1)} %pad_maximum_fusion.4), channel_id=1, source_target_pairs={{0,3},{1,0},{2,1},{3,2},{4,7},{5,4},{6,5},{7,6},{8,11},{9,8},{10,9... | collective-permute-start | bytes 7077896 | tf_op jit(solution)/shard_map/ppermute | solution.py:766
  608.1 12.2 %slice-start.2 = ((s8[10485760]{0:T(1024)(128)(4,1)}), s8[2097152]{0:T(1024)(128)(4,1)S(1)}, s32[]{:S(2)}) async-start(s8[10485760]{0:T(1024)(128)(4,1)} %bitcast.200), calls=%async_computation.7 | async-start | bytes 4194304
  609.7 197.6 %collective-permute-start.11 = (bf16[3,192,2048]{2,1,0:T(8,128)(2,1)}, bf16[3,192,2048]{2,1,0:T(8,128)(2,1)}, u32[]{:S(2)}, u32[]{:S(2)}) collective-permute-start(bf16[3,192,2048]{2,1,0:T(8,128)(2,1)} %pad_maximum_fusion.5), channel_id=1, source_target_pairs={{0,1},{1,2},{2,3},{3,0},{4,5},{5,6},{6,7},{7,4},{8,9},{9,10},{10,1... | collective-permute-start | bytes 7077896 | tf_op jit(solution)/shard_map/ppermute | solution.py:766
  610.9 9.4 %slice-start.3 = ((s8[10485760]{0:T(1024)(128)(4,1)}), s8[4194304]{0:T(1024)(128)(4,1)S(1)}, s32[]{:S(2)}) async-start(s8[10485760]{0:T(1024)(128)(4,1)} %bitcast.200), calls=%async_computation.8 | async-start | bytes 8388608
  610.9 7.7 copy-start.40
  615.9 196.5 %collective-permute-start.13 = (bf16[3,192,2048]{2,1,0:T(8,128)(2,1)}, bf16[3,192,2048]{2,1,0:T(8,128)(2,1)}, u32[]{:S(2)}, u32[]{:S(2)}) collective-permute-start(bf16[3,192,2048]{2,1,0:T(8,128)(2,1)} %pad_maximum_fusion.6), channel_id=1, source_target_pairs={{0,3},{1,0},{2,1},{3,2},{4,7},{5,4},{6,5},{7,6},{8,11},{9,8},{10,9... | collective-permute-start | bytes 7077896 | tf_op jit(solution)/shard_map/ppermute | solution.py:766
  620.1 192.3 %collective-permute-start.15 = (bf16[3,192,2048]{2,1,0:T(8,128)(2,1)}, bf16[3,192,2048]{2,1,0:T(8,128)(2,1)}, u32[]{:S(2)}, u32[]{:S(2)}) collective-permute-start(bf16[3,192,2048]{2,1,0:T(8,128)(2,1)} %pad_maximum_fusion.7), channel_id=1, source_target_pairs={{0,1},{1,2},{2,3},{3,0},{4,5},{5,6},{6,7},{7,4},{8,9},{9,10},{10,1... | collective-permute-start | bytes 7077896 | tf_op jit(solution)/shard_map/ppermute | solution.py:766
  625.1 106.2 %copy-start.32 = (bf16[128,2048]{1,0:T(8,128)(2,1)S(1)}, bf16[128,2048]{1,0:T(8,128)(2,1)}, u32[]{:S(2)}) copy-start(bf16[128,2048]{1,0:T(8,128)(2,1)} %param.15) | copy-start | bytes 1572868
  625.1 106.2 %copy-start.66 = (f32[2048]{0:T(1024)S(1)}, f32[2048]{0:T(1024)}, u32[]{:S(2)}) copy-start(f32[2048]{0:T(1024)} %param.16) | copy-start | bytes 24580
  625.1 106.2 %copy-start.87 = (f32[128]{0:T(128)S(1)}, f32[128]{0:T(128)}, u32[]{:S(2)}) copy-start(f32[128]{0:T(128)} %copy-done.86) | copy-start | bytes 1540
  625.1 106.5 %copy-start.71 = (f32[2048]{0:T(1024)S(1)}, f32[2048]{0:T(1024)}, u32[]{:S(2)}) copy-start(f32[2048]{0:T(1024)} %get-tuple-element.44) | copy-start | bytes 24580
  (74 other events, 225.2 us)
Sparse Core Ops, SparseCore 0:
  10.9 78.6 all-gather.1
  435.4 114.4 all-reduce.4
  553.8 114.2 reduce-scatter.1
  731.4 145.3 all-reduce.6

commit v2 on v0

v2 whole, which is shorter than its diff:
```python
import functools

import jax
import jax.numpy as jnp
from jax import lax
from jax.experimental import pallas as pl
from jax.experimental.pallas import tpu as pltpu
from jax.sharding import PartitionSpec as P

MESH = pl.DeviceIdType.MESH
F32 = jnp.float32
BF16 = jnp.bfloat16
EPSILON = 1e-06
ROPE_BASE = 1000000.0
MASK_VALUE = -1e30
NT = (((1,), (1,)), ((), ()))
TN = (((0,), (0,)), ((), ()))
NN = (((1,), (0,)), ((), ()))
OTHER = {"z": "y", "y": "z"}
ANY = pl.BlockSpec(memory_space=pl.ANY)
VMEM = pl.BlockSpec(memory_space=pltpu.VMEM)
SMEM = pl.BlockSpec(memory_space=pltpu.SMEM)


def dot(left, right, dims):
    return lax.dot_general(left, right, dims, preferred_element_type=F32)


def shape(dims, dtype=BF16):
    return jax.ShapeDtypeStruct(tuple(dims), dtype)


def dma_sems(*counts):
    return [pltpu.SemaphoreType.DMA((count,)) for count in counts]


class Place:
    def __init__(self):
        e = lax.axis_index("expert")
        self.x = lax.axis_index("tensor")
        self.z = e // 8
        self.y = (e // 2) % 4
        self.core = e % 2

    def block(self, axis="z", a=0, b=0, other=0):
        dz, dy = (a, b) if axis == "z" else (b, a)
        core = (self.core + other) % 2
        return ((self.z + dz) % 4) * 8 + ((self.y + dy) % 4) * 2 + core

    def device(self, axis="z", a=0, b=0, other=0):
        return (self.block(axis, a, b, other), self.x)

    def on_line(self, step):
        return (self.block(), (self.x + step) % 4)


def greet(devices):
    barrier = pltpu.get_barrier_semaphore()
    for device in devices:
        pl.semaphore_signal(barrier, inc=1, device_id=device, device_id_type=MESH)
    pl.semaphore_wait(barrier, len(devices))


def plane_neighbours(place):
    return [
        place.device("z", 1),
        place.device("z", -1),
        place.device("y", 1),
        place.device("y", -1),
        place.device(other=1),
    ]


def run(steps):
    for _ in steps:
        pass


def remote(source, target, send_sem, recv_sem, device):
    return pltpu.make_async_remote_copy(
        src_ref=source, dst_ref=target, send_sem=send_sem, recv_sem=recv_sem,
        device_id=device, device_id_type=MESH,
    )


def gather_plan():
    stages = [[], [], [], []]
    for half, first in ((0, "y"), (1, "z")):
        for side in (-1, 1):
            stages[0].append((first, half, side, 0, None, ("f", side)))
            stages[0].append((first, half, 0, side, None, ("s", side)))
    for half, first in ((0, "y"), (1, "z")):
        for quarter, side in ((0, -1), (1, 1)):
            stages[1].append((first, half, 2, 0, quarter, ("f", side)))
        for f in (-1, 1):
            for side in (-1, 1):
                stages[1].append((first, half, f, side, None, ("s", side)))
        for quarter, side in ((0, -1), (1, 1)):
            stages[1].append((first, half, 0, 2, quarter, ("s", side)))
    for half, first in ((0, "y"), (1, "z")):
        for quarter in (0, 1):
            for side in (-1, 1):
                stages[2].append((first, half, 2, side, quarter, ("s", side)))
        for f in (-1, 1):
            for quarter, side in ((0, -1), (1, 1)):
                stages[2].append((first, half, f, 2, quarter, ("s", side)))
    for half, first in ((0, "y"), (1, "z")):
        for quarter, side in ((0, -1), (1, 1)):
            stages[3].append((first, half, 2, 2, quarter, ("s", side)))
    return stages


STAGES = gather_plan()
PIECES = [piece for stage in STAGES for piece in stage]
PIECE_AT = {piece: at for at, piece in enumerate(PIECES)}


def onward(piece):
    first, half, f, s, quarter, (leg, side) = piece
    found = []
    for target in PIECES:
        _, t_half, t_f, t_s, t_quarter, (t_leg, t_side) = target
        if t_half != half or (quarter is not None and t_quarter != quarter):
            continue
        if t_leg == "f":
            take = t_f == 2 and leg == "f" and f == t_side and s == 0
        elif t_s == 2:
            take = leg == "s" and s == t_side and f == t_f
        else:
            take = leg == "f" and s == 0 and f == t_f
        if take:
            found.append(target)
    return found


def plane_gather_steps(place, x_ref, blocks, sems):
    send_sems, recv_sems, core_send, core_recv = sems
    rows = x_ref.shape[0]
    sibling = place.device(other=1)

    def span(half, quarter):
        if quarter is None:
            return pl.ds(half * (rows // 2), rows // 2)
        return pl.ds(half * (rows // 2) + quarter * (rows // 4), rows // 4)

    def send(target, source, f, s):
        first, half, _, _, quarter, (leg, side) = target
        at = PIECE_AT[target]
        copy = remote(
            source.at[span(half, quarter)],
            blocks(place.block(first, f, s)).at[span(half, quarter)],
            send_sems.at[at], recv_sems.at[at],
            place.device(first if leg == "f" else OTHER[first], -side),
        )
        copy.start()
        return copy

    started = [send(piece, x_ref, 0, 0) for piece in STAGES[0]]
    last = len(PIECES)
    core_copies = [
        remote(x_ref, blocks(place.block()), core_send.at[last], core_recv.at[last], sibling)
    ]
    core_copies[0].start()
    yield -1
    for number, stage in enumerate(STAGES):
        for piece in stage:
            first, half, f, s, quarter, _ = piece
            at = PIECE_AT[piece]
            block = blocks(place.block(first, f, s))
            view = block.at[span(half, quarter)]
            remote(view, view, send_sems.at[at], recv_sems.at[at], sibling).wait_recv()
            for target in onward(piece):
                started.append(send(target, block, f, s))
            copy = remote(view, view, core_send.at[at], core_recv.at[at], sibling)
            copy.start()
            core_copies.append(copy)
            yield number
        if number == 0:
            other = blocks(place.block(other=1))
            remote(other, other, core_send.at[last], core_recv.at[last], sibling).wait_recv()
        for piece in stage:
            first, half, f, s, quarter, _ = piece
            at = PIECE_AT[piece]
            view = blocks(place.block(first, f, s, 1)).at[span(half, quarter)]
            remote(view, view, core_send.at[at], core_recv.at[at], sibling).wait_recv()
        yield number + 100
    for copy in started + core_copies:
        copy.wait_send()


def gather_sems():
    count = len(PIECES)
    return dma_sems(count, count, count + 1, count + 1)


def scatter_scratch(rows, width):
    return [
        pltpu.VMEM((16, rows, width), BF16),
        pltpu.VMEM((2, 4, 2, rows // 4, width), BF16),
        pltpu.VMEM((2, 4, 2, rows // 2, width), BF16),
        pltpu.VMEM((2, 2, rows // 4, width), BF16),
        pltpu.VMEM((2, 2, rows // 2, width), BF16),
        *dma_sems(16, 16, 40, 40),
    ]


def plane_scatter_steps(place, rows, make, block, scratch, finish):
    other, in_a, in_b, in_c, in_d, core_send, core_recv, send_sems, recv_sems = scratch
    half_rows, quarter_rows = rows // 2, rows // 4
    exchanged, ready, sent = {}, set(), []

    def exchange(dz, dy):
        at = dz * 4 + dy
        if at in exchanged:
            return
        make(dz, dy)
        exchanged[at] = remote(
            block(dz, dy, 1), other.at[at], core_send.at[at], core_recv.at[at],
            place.device(other=1),
        )
        exchanged[at].start()

    def add_rows(into, start, count, source):
        @pl.loop(0, count, step=16)
        def _(row):
            here = pl.ds(start + row, 16)
            total = into[here].astype(F32) + source[pl.ds(row, 16)].astype(F32)
            into[here] = total.astype(BF16)

    def where(axis, a, b):
        dz, dy = (a, b) if axis == "z" else (b, a)
        return dz % 4, dy % 4

    def ready_block(axis, a, b):
        dz, dy = where(axis, a, b)
        at = dz * 4 + dy
        if at not in ready:
            ready.add(at)
            exchange(dz, dy)
            exchanged[at].wait_recv()
            add_rows(block(dz, dy, 0), 0, rows, other.at[at])
        return block(dz, dy, 0)

    def send(source, target, number, device):
        copy = remote(source, target, send_sems.at[number], recv_sems.at[number], device)
        copy.start()
        sent.append(copy)

    def arrive(target, number):
        remote(
            target, target, send_sems.at[number], recv_sems.at[number], place.device("z", 1)
        ).wait_recv()

    axes = (("z", "y"), ("y", "z"))
    sides = ((0, 1), (1, -1))
    lines = (2, 1, 3, 0)
    first_needs = []
    for line in lines:
        for first, _ in axes:
            if where(first, 2, line) not in first_needs:
                first_needs.append(where(first, 2, line))
    for dz, dy in first_needs[:4]:
        exchange(dz, dy)
    yield
    for line in lines:
        for half, (first, second) in enumerate(axes):
            for dz, dy in first_needs:
                if (dz, dy) not in [where(first, 2, line)] and dz * 4 + dy not in exchanged:
                    exchange(dz, dy)
                    break
            held = ready_block(first, 2, line)
            for quarter, side in sides:
                rows_here = pl.ds(half * half_rows + quarter * quarter_rows, quarter_rows)
                send(held.at[rows_here], in_a.at[half, line, quarter],
                     (half * 4 + line) * 2 + quarter, place.device(first, side))
        yield
    for dz in (1, 3, 0, 2):
        for dy in (1, 3, 0, 2):
            exchange(dz, dy)
    yield
    for line in lines:
        for half, (first, second) in enumerate(axes):
            for quarter, side in sides:
                held = ready_block(first, side, line)
                number = (half * 4 + line) * 2 + quarter
                arrive(in_a.at[half, line, quarter], number)
                add_rows(held, half * half_rows + quarter * quarter_rows, quarter_rows,
                         in_a.at[half, line, quarter])
                send(held.at[pl.ds(half * half_rows, half_rows)],
                     in_b.at[half, line, quarter], 16 + number, place.device(first, side))
        yield
    for line in lines:
        for half, (first, second) in enumerate(axes):
            held = ready_block(first, 0, line)
            for quarter in (0, 1):
                number = (half * 4 + line) * 2 + quarter
                arrive(in_b.at[half, line, quarter], 16 + number)
                add_rows(held, half * half_rows, half_rows, in_b.at[half, line, quarter])
            if line == 2:
                for quarter, side in sides:
                    rows_here = pl.ds(half * half_rows + quarter * quarter_rows, quarter_rows)
                    send(held.at[rows_here], in_c.at[half, quarter],
                         32 + half * 2 + quarter, place.device(second, side))
            if line in (1, 3):
                quarter, side = sides[0] if line == 1 else sides[1]
                number = 32 + half * 2 + quarter
                arrive(in_c.at[half, quarter], number)
                add_rows(held, half * half_rows + quarter * quarter_rows, quarter_rows,
                         in_c.at[half, quarter])
                send(held.at[pl.ds(half * half_rows, half_rows)], in_d.at[half, quarter],
                     36 + half * 2 + quarter, place.device(second, side))
        yield
    held = block(0, 0, 0)
    for half in (0, 1):
        for quarter in (0, 1):
            arrive(in_d.at[half, quarter], 36 + half * 2 + quarter)

        @pl.loop(0, half_rows, step=16)
        def _(row):
            here = pl.ds(half * half_rows + row, 16)
            total = held[here].astype(F32)
            for quarter in (0, 1):
                total = total + in_d[half, quarter, pl.ds(row, 16)].astype(F32)
            finish(half * half_rows + row, total)

    for copy in sent:
        copy.wait_send()
    for at in exchanged:
        exchanged[at].wait_send()


def line_gather_steps(place, out_ref, rows, sems):
    send_sems, recv_sems = sems
    half = rows // 2

    def part(step, start, count):
        return out_ref.at[pl.ds(((place.x + step) % 4) * rows + start, count)]

    def copy(view, number, side):
        return remote(view, view, send_sems.at[number], recv_sems.at[number], place.on_line(side))

    copies = [copy(part(0, 0, rows), 0, 1), copy(part(0, 0, rows), 1, -1)]
    for c in copies:
        c.start()
    yield
    copy(part(-1, 0, rows), 0, 1).wait_recv()
    copies.append(copy(part(-1, 0, half), 2, 1))
    copies[2].start()
    copy(part(1, 0, rows), 1, -1).wait_recv()
    copies.append(copy(part(1, half, half), 3, -1))
    copies[3].start()
    yield
    copy(part(2, 0, half), 2, 1).wait_recv()
    copy(part(2, half, half), 3, -1).wait_recv()
    for c in copies:
        c.wait_send()


def line_scatter_scratch(rows, width):
    return [
        pltpu.VMEM((2, rows // 2, width), BF16),
        pltpu.VMEM((2, rows, width), BF16),
        *dma_sems(4, 4),
    ]


def line_scatter_steps(place, c_ref, rows, scratch):
    in_a, in_b, send_sems, recv_sems = scratch
    half = rows // 2

    def part(step, start, count):
        return c_ref.at[pl.ds(((place.x + step) % 4) * rows + start, count)]

    def copy(source, target, number, side):
        return remote(
            source, target, send_sems.at[number], recv_sems.at[number], place.on_line(side)
        )

    copies = [
        copy(part(2, 0, half), in_a.at[0], 0, 1),
        copy(part(2, half, half), in_a.at[1], 1, -1),
    ]
    for c in copies:
        c.start()
    yield

    def add(view, source):
        @pl.loop(0, half, step=16)
        def _(row):
            here = pl.ds(row, 16)
            view[here] = (view[here].astype(F32) + source[here].astype(F32)).astype(BF16)

    copies[0].wait_recv()
    add(part(1, 0, half), in_a.at[0])
    copies.append(copy(part(1, 0, rows), in_b.at[0], 2, 1))
    copies[2].start()
    copies[1].wait_recv()
    add(part(-1, half, half), in_a.at[1])
    copies.append(copy(part(-1, 0, rows), in_b.at[1], 3, -1))
    copies[3].start()
    yield
    copies[2].wait_recv()
    copies[3].wait_recv()
    for c in copies:
        c.wait_send()


SLOTS = 80
GROUPS = [(dz, dy) for dz in (0, 1, 3, 2) for dy in (0, 1)]


def chosen_rows(slots, first):
    value = slots.astype(F32)
    lane = lax.broadcasted_iota(jnp.int32, value.shape, 1)
    slot = lax.broadcasted_iota(jnp.int32, (value.shape[0], 2 * SLOTS), 1).astype(F32)
    found = []
    for j in range(2):
        mine = jnp.sum(jnp.where(lane == first + j, value, 0.0), axis=1, keepdims=True)
        found.append(jnp.where(mine >= 0.0, mine + float(j * SLOTS), -1.0))
    return jnp.where((slot == found[0]) | (slot == found[1]), 1.0, 0.0).astype(BF16)


def group_blocks(place, dz, dy):
    z = (place.z + dz) % 4
    return [z * 8 + ((place.y + dy + two) % 4) * 2 for two in (0, 2)]


def gather_select_kernel(
    x_ref, grads_ref, all_ref, grad_a_ref, grad_b_ref, row_a_ref, row_b_ref, gate_a_ref, gate_b_ref,
    tokens, slots, rows_a, rows_b, grads_a, grads_b, gates_a, gates_b,
    own_sem, load_sems, slot_sems, save_sems, *sems,
):
    place = Place()
    first = 2 * lax.axis_index("expert")
    width = rows_a.shape[1]
    greet(plane_neighbours(place))
    own = pltpu.make_async_copy(x_ref, all_ref.at[place.block()], own_sem.at[0])
    own.start()
    steps = plane_gather_steps(place, x_ref, lambda at: all_ref.at[at], sems)
    next(steps)

    def loads_of(source, number, slot):
        dz, dy = GROUPS[number]
        return [
            pltpu.make_async_copy(
                source.at[pl.ds(at, 2)], tokens.at[slot, pl.ds(2 * i, 2)], load_sems.at[2 * slot + i]
            )
            for i, at in enumerate(group_blocks(place, dz, dy))
        ]

    saves = []

    def save(value_ref, target, number, slot):
        here = pl.ds(number * SLOTS, SLOTS)
        copy = pltpu.make_async_copy(value_ref.at[here], target.at[here], save_sems.at[slot])
        copy.start()
        saves.append(copy)

    def select(number, slot, is_grad):
        for load in loads_of(grads_ref if is_grad else all_ref, number, slot):
            load.wait()
        here = pl.ds(number * SLOTS, SLOTS)
        block = tokens[slot].reshape(512, width + 128)
        if is_grad:
            slots[number] = block[:, width:]
        rows = dot(chosen_rows(slots[number], first), block, TN)
        a, b = (grads_a, grads_b) if is_grad else (rows_a, rows_b)
        a[here] = rows[:SLOTS, :width].astype(BF16)
        b[here] = rows[SLOTS:, :width].astype(BF16)
        base = number * 2 + (16 if is_grad else 0)
        save(a, grad_a_ref if is_grad else row_a_ref, number, base)
        save(b, grad_b_ref if is_grad else row_b_ref, number, base + 1)
        if not is_grad:
            lane = lax.broadcasted_iota(jnp.int32, (SLOTS, 128), 1) % 64
            for j, (gates, target) in enumerate(((gates_a, gate_a_ref), (gates_b, gate_b_ref))):
                part = rows[j * SLOTS : (j + 1) * SLOTS, width:]
                gate = jnp.sum(jnp.where(lane == first + j, part, 0.0), axis=1, keepdims=True)
                gates[here] = jnp.broadcast_to(gate, (SLOTS, 128))
                save(gates, target, number, 32 + number * 2 + j)

    def start(is_grad, number, slot):
        for load in loads_of(grads_ref if is_grad else all_ref, number, slot):
            load.start()

    start(True, 0, 0)
    grad_turn = 0
    pieces = 0
    for stage in steps:
        if stage < 100:
            pieces += 1
            if pieces % 2 == 0 and grad_turn < 8:
                if grad_turn + 1 < 8:
                    start(True, grad_turn + 1, (grad_turn + 1) % 2)
                select(grad_turn, grad_turn % 2, True)
                grad_turn += 1
        elif stage == 101:
            assert grad_turn == 8
            own.wait()
            start(False, 0, 0)
            start(False, 1, 1)
            select(0, 0, False)
            select(1, 1, False)
        elif stage == 102:
            start(False, 2, 0)
            for number in range(2, 6):
                if number + 1 < 6:
                    start(False, number + 1, (number + 1) % 2)
                select(number, number % 2, False)
        elif stage == 103:
            start(False, 6, 0)
            start(False, 7, 1)
            select(6, 0, False)
            select(7, 1, False)
    for copy in saves:
        copy.wait()


def gather_select(x, grads, collective_id):
    count, full = x.shape
    width = full - 128
    total = len(GROUPS) * SLOTS
    rows = shape((total, width))
    gate = shape((total, 128), F32)
    return pl.pallas_call(
        gather_select_kernel,
        out_shape=(shape((32, count, full)), rows, rows, rows, rows, gate, gate),
        in_specs=[ANY, ANY],
        out_specs=(ANY,) * 7,
        scratch_shapes=[
            pltpu.VMEM((2, 4, count, full), BF16),
            pltpu.VMEM((8, 512, 128), BF16),
            *[pltpu.VMEM((total, width), BF16)] * 4,
            *[pltpu.VMEM((total, 128), F32)] * 2,
            *dma_sems(1, 4, 1, 48),
            *gather_sems(),
        ],
        compiler_params=pltpu.CompilerParams(
            collective_id=collective_id, has_side_effects=True, vmem_limit_bytes=60 * 2**20
        ),
        cost_estimate=pl.CostEstimate(flops=6 * 10**10, bytes_accessed=10**8, transcendentals=0),
        name="gather_select",
    )(x, grads)[1:]


def combine_scatter_kernel(
    back_a_ref, back_b_ref, out_a_ref, out_b_ref, slots_ref, gw_ref, sum_left_ref, sum_right_ref,
    grad_out_ref, hidden_ref, mixed_ref, state_ref, picks_ref, mlp_gain_ref, router_ref,
    shares_ref, from_right_ref, from_left_ref,
    grad_hidden_ref, grad_att_ref, grad_router_ref, gain_ref,
    rows, slots, blocks, out_rows, share, total, load_sems, row_sems, share_sems,
    line_send, line_recv, *scratch,
):
    place = Place()
    first = 2 * lax.axis_index("expert")
    count = hidden_ref.shape[0]
    width = hidden_ref.shape[1]
    for number, (dz, dy) in enumerate(GROUPS):
        for i, at in enumerate(group_blocks(place, dz, dy)):
            pltpu.make_async_copy(
                slots_ref.at[pl.ds(at, 2), :, pl.ds(width, 128)], slots.at[number, pl.ds(2 * i, 2)],
                load_sems.at[2 * number + i],
            ).start()
        for j, ref in enumerate((back_a_ref, back_b_ref)):
            pltpu.make_async_copy(
                ref.at[pl.ds(number * SLOTS, SLOTS)], rows.at[number, j],
                load_sems.at[16 + 2 * number + j],
            ).start()
    greet(plane_neighbours(place) + [place.on_line(1), place.on_line(-1)])
    line = second_sends(
        place, gw_ref, sum_left_ref, sum_right_ref, from_right_ref, from_left_ref, line_send,
        line_recv,
    )
    for copy in line:
        copy.start()
    made = set()

    def loaded(number):
        dz, dy = GROUPS[number]
        for i, at in enumerate(group_blocks(place, dz, dy)):
            pltpu.make_async_copy(
                slots_ref.at[pl.ds(at, 2), :, pl.ds(width, 128)], slots.at[number, pl.ds(2 * i, 2)],
                load_sems.at[2 * number + i],
            ).wait()
        for j, ref in enumerate((back_a_ref, back_b_ref)):
            pltpu.make_async_copy(
                ref.at[pl.ds(number * SLOTS, SLOTS)], rows.at[number, j],
                load_sems.at[16 + 2 * number + j],
            ).wait()

    def table_of(number):
        return chosen_rows(slots[number].reshape(512, 128), first)

    def make(dz, dy):
        number = GROUPS.index((dz, dy % 2))
        if number in made:
            return
        made.add(number)
        loaded(number)
        both = rows[number].reshape(2 * SLOTS, width + 128)
        sums = dot(table_of(number), both, NN).astype(BF16).reshape(2, 2, count, width + 128)
        low = dy % 2
        blocks[dz * 4 + low] = sums[0]
        blocks[dz * 4 + low + 2] = sums[1]

    def block(dz, dy, other):
        return blocks.at[dz * 4 + dy, (place.core + other) % 2]

    def finish(row, value):
        total[pl.ds(row, 16)] = value

    def out_loads(number):
        return [
            pltpu.make_async_copy(
                ref.at[pl.ds(number * SLOTS, SLOTS)], out_rows.at[number % 2, j],
                row_sems.at[2 * (number % 2) + j],
            )
            for j, ref in enumerate((out_a_ref, out_b_ref))
        ]

    def share_saves(number):
        dz, dy = GROUPS[number]
        return [
            pltpu.make_async_copy(
                share.at[number % 2, pl.ds(2 * i, 2)], shares_ref.at[pl.ds(at, 2)],
                share_sems.at[2 * (number % 2) + i],
            )
            for i, at in enumerate(group_blocks(place, dz, dy))
        ]

    def make_share(number):
        if number + 1 < len(GROUPS):
            for load in out_loads(number + 1):
                load.start()
        for load in out_loads(number):
            load.wait()
        if number >= 2:
            for save in share_saves(number - 2):
                save.wait()
        both = out_rows[number % 2].reshape(2 * SLOTS, width)
        sums = dot(table_of(number), both, NN).astype(BF16)
        share[number % 2] = sums.reshape(4, count, width)
        for save in share_saves(number):
            save.start()

    for load in out_loads(0):
        load.start()
    turn = 0
    for at, _ in enumerate(plane_scatter_steps(place, count, make, block, scratch, finish)):
        if at >= 5:
            for _ in range(2):
                if turn < len(GROUPS):
                    make_share(turn)
                    turn += 1
    while turn < len(GROUPS):
        make_share(turn)
        turn += 1

    experts = picks_ref.shape[1]
    probs, gates = state_ref[:, :experts], state_ref[:, experts : 2 * experts]
    picked_total = state_ref[:, 2 * experts : 2 * experts + 1]
    second_scale = state_ref[:, 2 * experts + 1 : 2 * experts + 2]
    tail = total[:, pl.ds(width, 128)]
    gate_grad = tail[:, :experts] + tail[:, experts:]
    mean = jnp.sum(gate_grad * gates, axis=1, keepdims=True)
    prob_grad = picks_ref[...] * (gate_grad - mean) / picked_total
    logit_grad = probs * (prob_grad - jnp.sum(prob_grad * probs, axis=1, keepdims=True))
    logit_grad = logit_grad.astype(BF16)
    grad_router_ref[...] = dot(logit_grad, mixed_ref[:, :width], TN)
    grad_mixed = total[:, :width] + dot(logit_grad, router_ref[...], NN)
    hidden = hidden_ref[...]
    gain_ref[...] = jnp.sum(grad_mixed * hidden * second_scale, axis=0, keepdims=True)
    grad_hidden = grad_out_ref[...].astype(F32) + norm_back(
        hidden, second_scale, mlp_gain_ref[...], grad_mixed
    )
    grad_hidden_ref[...] = grad_hidden
    grad_att_ref[...] = grad_hidden.astype(BF16)
    for number in (len(GROUPS) - 2, len(GROUPS) - 1):
        for save in share_saves(number):
            save.wait()
    for copy in line:
        copy.wait()


def combine_scatter(
    back, out, slots, line, grad_out, hidden, mixed, state, picks, mlp_gain, router_t, collective_id
):
    count, width = hidden.shape
    groups = len(GROUPS)
    return pl.pallas_call(
        combine_scatter_kernel,
        out_shape=(
            shape((32, count, width)),
            *[shape((3, line[0].shape[1] // 4, width))] * 2,
            shape((count, width), F32),
            shape((count, width)),
            shape(router_t.shape, F32),
            shape((1, width), F32),
        ),
        in_specs=[ANY] * 8 + [VMEM] * 7,
        out_specs=(ANY, ANY, ANY, VMEM, VMEM, VMEM, VMEM),
        scratch_shapes=[
            pltpu.VMEM((groups, 2, SLOTS, width + 128), BF16),
            pltpu.VMEM((groups, 4, count, 128), BF16),
            pltpu.VMEM((16, 2, count, width + 128), BF16),
            pltpu.VMEM((2, 2, SLOTS, width), BF16),
            pltpu.VMEM((2, 4, count, width), BF16),
            pltpu.VMEM((count, width + 128), F32),
            *dma_sems(32, 4, 4, 4, 4),
            *scatter_scratch(count, width + 128),
        ],
        compiler_params=pltpu.CompilerParams(
            collective_id=collective_id, has_side_effects=True, vmem_limit_bytes=62 * 2**20
        ),
        cost_estimate=pl.CostEstimate(flops=6 * 10**10, bytes_accessed=10**8, transcendentals=0),
        name="combine_scatter",
    )(*back, *out, slots, *line, grad_out, hidden, mixed, state, picks, mlp_gain, router_t)


def expert_kernel(
    expert_ref, own_ref, left_ref, right_ref, far0_ref, far1_ref, x_hbm, d_hbm, gate_hbm,
    *rest,
):
    expert_steps(
        None, expert_ref, (own_ref, left_ref, right_ref, far0_ref, far1_ref), x_hbm, d_hbm, gate_hbm,
        *rest,
    )


def expert_sending_kernel(
    expert_ref, own_ref, left_ref, right_ref, far0_ref, far1_ref, x_hbm, d_hbm, gate_hbm, other_hbm,
    p_hbm, rb_hbm, gw_hbm, sum_left_hbm, sum_right_hbm, *scratch,
):
    *scratch, come, mine, load_sems, send_sems, recv_sems, save_sems = scratch
    payload = first_sums_steps(
        Place(), other_hbm, sum_left_hbm, sum_right_hbm, come, mine, load_sems, send_sems,
        recv_sems, save_sems,
    )
    expert_steps(
        payload, expert_ref, (own_ref, left_ref, right_ref, far0_ref, far1_ref), x_hbm, d_hbm,
        gate_hbm, p_hbm, rb_hbm, gw_hbm, *scratch,
    )


def expert_steps(
    payload, expert_ref, parts, x_hbm, d_hbm, gate_hbm, p_hbm, rb_hbm, gw_hbm,
    w, x, d, gate, rg, middle, ggp, gup, p, rb, dots, turned, gw, in_sems, out_sems, gw_sems,
):
    f32, bf16 = jnp.float32, jnp.bfloat16
    rows, width = x.shape
    hidden = middle.shape[1]
    chunk = 256
    loads = [
        pltpu.make_async_copy(x_hbm, x, in_sems.at[0]),
        pltpu.make_async_copy(d_hbm, d, in_sems.at[1]),
        pltpu.make_async_copy(gate_hbm, gate, in_sems.at[2]),
    ]
    at = 0
    for i, ref in enumerate(parts):
        size = ref.shape[1]
        loads.append(pltpu.make_async_copy(ref, w.at[:, pl.ds(at, size)], in_sems.at[3 + i]))
        at += size
    for load in loads:
        load.start()
    if payload is not None:
        greet([Place().on_line(1), Place().on_line(-1)])
        next(payload)
    for load in loads:
        load.wait()

    @pl.loop(0, rows, step=16)
    def _(r):
        here = pl.ds(r, 16)
        scaled = d[here].astype(f32) * gate[here, 0:1]
        rg[here] = scaled.astype(bf16)

    for c in range(0, hidden, chunk):
        here = pl.ds(c, chunk)
        gate_pre = dot(x[...], w[0, here], NT)
        up_pre = dot(x[...], w[1, here], NT)
        grad_mid = dot(rg[...], w[2, here], NT)
        sig = 1.0 / (1.0 + jnp.exp(-gate_pre))
        act = gate_pre * sig
        middle[:, here] = (act * up_pre).astype(bf16)
        ggp[:, here] = (grad_mid * up_pre * sig * (1.0 + gate_pre * (1.0 - sig))).astype(bf16)
        gup[:, here] = (grad_mid * act).astype(bf16)

    dots[...] = jnp.zeros_like(dots)

    for n in range(0, width, chunk):
        here = pl.ds(n, chunk)
        out = dot(middle[...], w[2, :, here], NN).astype(bf16).astype(f32)
        p[:, here] = (out * gate[:, 0:1]).astype(bf16)
        along = out * d[:, here].astype(f32)
        dots[...] += along[:, :128] + along[:, 128:]
        back = dot(ggp[...], w[0, :, here], NN) + dot(gup[...], w[1, :, here], NN)
        rb[:, here] = back.astype(bf16)

    expert = expert_ref[0]
    total = jnp.sum(dots[...], axis=1, keepdims=True)
    high = total.astype(bf16).astype(f32)
    lane = lax.broadcasted_iota(jnp.int32, (rows, 128), 1)
    tail = jnp.where(lane == expert, high, jnp.where(lane == expert + 64, total - high, 0.0))
    rb[:, pl.ds(width, 128)] = tail.astype(bf16)
    outs = [
        pltpu.make_async_copy(rb, rb_hbm, out_sems.at[0]),
        pltpu.make_async_copy(p, p_hbm, out_sems.at[1]),
    ]
    for out in outs:
        out.start()

    for i, (left, right) in enumerate(((ggp, x), (gup, x), (middle, rg))):
        turned[...] = left[...].T

        for c in range(0, hidden, chunk):
            here = pl.ds(c, chunk)
            for n in range(0, width, 512):
                there = pl.ds(n, 512)
                gw[i, here, there] = dot(turned[here], right[:, there], NN).astype(bf16)

        save = pltpu.make_async_copy(gw.at[i], gw_hbm.at[i], gw_sems.at[i])
        save.start()
        outs.append(save)
    if payload is not None:
        run(payload)
    for out in outs:
        out.wait()


def first_sums_steps(
    place, gw_hbm, sum_left, sum_right, come, mine, load_sems, send_sems, recv_sems, save_sems
):
    shard = gw_hbm.shape[1] // 4
    half = shard // 2
    sends = [
        remote(gw_hbm.at[:, pl.ds(3 * shard + i * half, half)], come.at[i], send_sems.at[i],
               recv_sems.at[i], place.on_line(side))
        for i, side in ((0, -1), (1, 1))
    ]
    loads = [
        pltpu.make_async_copy(gw_hbm.at[:, pl.ds(at, half)], mine.at[i], load_sems.at[i])
        for i, at in ((0, shard), (1, 2 * shard + half))
    ]
    for copy in sends + loads:
        copy.start()
    yield
    saves = []
    for i, target in ((0, sum_left), (1, sum_right)):
        loads[i].wait()
        sends[i].wait()

        @pl.loop(0, half, step=16)
        def _(row):
            for j in range(3):
                here = (i, j, pl.ds(row, 16))
                mine[here] = (mine[here].astype(F32) + come[here].astype(F32)).astype(BF16)

        saves.append(pltpu.make_async_copy(mine.at[i], target, save_sems.at[i]))
        saves[i].start()
    for save in saves:
        save.wait()


def first_sums_scratch(half, width):
    return [
        pltpu.VMEM((2, 3, half, width), BF16),
        pltpu.VMEM((2, 3, half, width), BF16),
        *dma_sems(2, 2, 2, 2),
    ]


def second_sends(place, gw_hbm, sum_left, sum_right, from_right, from_left, send_sems, recv_sems):
    shard = gw_hbm.shape[1] // 4
    half = shard // 2
    low, high = pl.ds(0, half), pl.ds(half, half)
    plan = [
        (gw_hbm.at[:, pl.ds(shard + half, half)], from_right.at[:, high], -1),
        (gw_hbm.at[:, pl.ds(2 * shard, half)], from_left.at[:, low], 1),
        (sum_left, from_right.at[:, low], -1),
        (sum_right, from_left.at[:, high], 1),
    ]
    return [
        remote(source, target, send_sems.at[i], recv_sems.at[i], place.on_line(side))
        for i, (source, target, side) in enumerate(plan)
    ]


def expert_layer(expert, weights, x, d, gate, other=None, collective_id=None):
    bf16 = jnp.bfloat16
    rows, width = x.shape
    hidden = sum(part.shape[1] for part in weights)
    half = hidden // 8
    sending = other is not None
    more = [shape((3, half, width))] * 2 if sending else []
    extra = first_sums_scratch(half, width) if sending else []
    return pl.pallas_call(
        expert_sending_kernel if sending else expert_kernel,
        out_shape=(
            jax.ShapeDtypeStruct((rows, width), bf16),
            jax.ShapeDtypeStruct((rows, width + 128), bf16),
            jax.ShapeDtypeStruct((3, hidden, width), bf16),
            *more,
        ),
        in_specs=[SMEM] + [ANY] * (9 if sending else 8),
        out_specs=(ANY,) * (5 if sending else 3),
        scratch_shapes=[
            pltpu.VMEM((3, hidden, width), bf16),
            pltpu.VMEM((rows, width), bf16),
            pltpu.VMEM((rows, width), bf16),
            pltpu.VMEM((rows, 128), jnp.float32),
            pltpu.VMEM((rows, width), bf16),
            pltpu.VMEM((rows, hidden), bf16),
            pltpu.VMEM((rows, hidden), bf16),
            pltpu.VMEM((rows, hidden), bf16),
            pltpu.VMEM((rows, width), bf16),
            pltpu.VMEM((rows, width + 128), bf16),
            pltpu.VMEM((rows, 128), jnp.float32),
            pltpu.VMEM((hidden, rows), bf16),
            pltpu.VMEM((3, hidden, width), bf16),
            *dma_sems(8, 2, 3),
            *extra,
        ],
        compiler_params=pltpu.CompilerParams(
            vmem_limit_bytes=60 * 2**20, collective_id=collective_id, has_side_effects=sending
        ),
        cost_estimate=pl.CostEstimate(
            flops=18 * rows * hidden * width,
            bytes_accessed=12 * hidden * width + 10 * rows * width,
            transcendentals=rows * hidden,
        ),
        name="expert_sending" if sending else "expert_layer",
    )(expert, *weights, x, d, gate, *([other] if sending else []))


def rope_tables(length, head_size):
    position = jnp.arange(length, dtype=jnp.float32)[:, None]
    index_half = jnp.arange(head_size // 2, dtype=jnp.float32)[None, :]
    frequency = jnp.exp(index_half * (-2.0 / head_size) * jnp.log(ROPE_BASE))
    turned = position * frequency
    sine = jnp.sin(turned)
    return (
        jnp.concatenate([jnp.cos(turned)] * 2, axis=1),
        jnp.concatenate([-sine, sine], axis=1),
    )


def inverse_rms(values):
    return lax.rsqrt(jnp.mean(values * values, axis=-1, keepdims=True) + EPSILON)


def norm_back(values, scales, gain, grads):
    weighted = grads * gain
    return scales * weighted - values * scales * scales * scales * jnp.mean(
        weighted * values, axis=-1, keepdims=True
    )


def attend(seq, w_query, w_key, w_value, q_gain, k_gain, cosine, sine,
           query_rot, key_rot, values, query_unit, key_unit, stats, context):
    length = seq.shape[0]
    head = cosine.shape[1]
    heads = w_query.shape[1] // head
    scale = head ** (-0.5)
    cos, sin = cosine[...], sine[...]
    lane = lax.broadcasted_iota(jnp.int32, (length, head), 1)
    kept = jnp.zeros((length, head), F32)

    def unit_and_rot(raw, gain):
        scales = inverse_rms(raw)
        unit = raw * scales
        normed = unit * gain
        rot = normed * cos + pltpu.roll(normed, head // 2, 1) * sin
        return scales, unit, rot.astype(BF16)

    raw = dot(seq[...], w_key[...], NN)
    scales, unit, rot = unit_and_rot(raw, k_gain[...])
    key_unit[...] = unit
    key_rot[...] = rot
    kept = jnp.where(lane == 8, scales, kept)
    values[...] = dot(seq[...], w_value[...], NN).astype(BF16)
    half = length // 2
    for pair in range(0, heads, 2):
        raws = dot(seq[...], w_query[:, pl.ds(pair * head, 2 * head)], NN)
        for h in (pair, pair + 1):
            here = pl.ds(h * head, head)
            raw = raws[:, (h - pair) * head : (h - pair + 1) * head]
            scales, unit, rot = unit_and_rot(raw, q_gain[...])
            query_unit[:, here] = unit
            query_rot[:, here] = rot
            kept = jnp.where(lane == h, scales, kept)
            logs = []
            for part in range(2):
                until = (part + 1) * half
                scores = dot(rot[part * half : until], key_rot[:until], NT) * scale
                row = lax.broadcasted_iota(jnp.int32, scores.shape, 0) + part * half
                column = lax.broadcasted_iota(jnp.int32, scores.shape, 1)
                scores = jnp.where(row >= column, scores, MASK_VALUE)
                peak = jnp.max(scores, axis=1, keepdims=True)
                raised = jnp.exp(scores - peak)
                total = jnp.sum(raised, axis=1, keepdims=True)
                probs = (raised * (1.0 / total)).astype(BF16)
                mixed = dot(probs, values[:until], NN)
                context[pl.ds(part * half, half), here] = mixed.astype(BF16)
                logs.append(peak + jnp.log(total))
            kept = jnp.where(lane == 16 + h, jnp.concatenate(logs, axis=0), kept)
    stats[...] = kept


def attend_back(grad_rows, seq, w_query, w_key, w_value, w_out, q_gain, k_gain, cosine, sine,
                query_rot, key_rot, values, query_unit, key_unit, stats,
                grad_context, grad_qkv, gains):
    length = seq.shape[0]
    head = cosine.shape[1]
    heads = query_rot.shape[1] // head
    scale = head ** (-0.5)
    cos, sin = cosine[...], sine[...]
    half = length // 2

    def rotate_back(grads):
        return grads * cos - pltpu.roll(grads, head // 2, 1) * sin

    def unit_back(scales, unit, gain, grads):
        z = grads * gain
        return scales * (z - unit * jnp.mean(z * unit, axis=1, keepdims=True))

    for n in range(0, heads * head, 256):
        here = pl.ds(n, 256)
        grad_context[:, here] = dot(grad_rows[...], w_out[here], NT).astype(BF16)
    yield
    key_grads = [jnp.zeros((half, head), F32)] * 2
    value_grads = [jnp.zeros((half, head), F32)] * 2
    q_gain_grad = jnp.zeros((1, head), F32)
    for h in range(heads):
        here = pl.ds(h * head, head)
        query_grads = []
        for part in range(2):
            until = (part + 1) * half
            rows = pl.ds(part * half, half)
            rot = query_rot[rows, here]
            scores = dot(rot, key_rot[:until], NT) * scale
            row = lax.broadcasted_iota(jnp.int32, scores.shape, 0) + part * half
            column = lax.broadcasted_iota(jnp.int32, scores.shape, 1)
            scores = jnp.where(row >= column, scores, MASK_VALUE)
            probs = jnp.exp(scores - stats[rows, 16 + h : 17 + h])
            from_context = grad_context[rows, here]
            grad_probs = dot(from_context, values[:until], NT)
            low = probs.astype(BF16)
            value_part = dot(low, from_context, TN)
            mean = jnp.sum(grad_probs * probs, axis=1, keepdims=True)
            grad_scores = (probs * (grad_probs - mean)).astype(BF16)
            query_grads.append(dot(grad_scores, key_rot[:until], NN) * scale)
            key_part = dot(grad_scores, rot, TN) * scale
            for other in range(part + 1):
                cut = slice(other * half, (other + 1) * half)
                value_grads[other] = value_grads[other] + value_part[cut]
                key_grads[other] = key_grads[other] + key_part[cut]
        grads = rotate_back(jnp.concatenate(query_grads, axis=0))
        unit = query_unit[:, here]
        q_gain_grad = q_gain_grad + jnp.sum(grads * unit, axis=0, keepdims=True)
        grad_qkv[:, here] = unit_back(stats[:, h : h + 1], unit, q_gain[...], grads).astype(BF16)
        yield
    grads = rotate_back(jnp.concatenate(key_grads, axis=0))
    unit = key_unit[...]
    gains[0:1, :] = q_gain_grad
    gains[1:2, :] = jnp.sum(grads * unit, axis=0, keepdims=True)
    grad_qkv[:, pl.ds(heads * head, head)] = unit_back(
        stats[:, 8:9], unit, k_gain[...], grads
    ).astype(BF16)
    grad_qkv[:, pl.ds((heads + 1) * head, head)] = jnp.concatenate(value_grads, axis=0).astype(BF16)
    yield


def forward_kernel(
    inputs_ref, attn_gain_ref, q_gain_ref, k_gain_ref, cos_ref, sin_ref, mlp_gain_ref, router_ref,
    picks_ref, w_query_ref, w_key_ref, w_value_ref, w_out_ref,
    mixed_ref, hidden_ref, state_ref, seq_ref,
    query_rot_ref, key_rot_ref, values_ref, query_unit_ref, key_unit_ref, stats_ref, context_ref,
    seq, w_query, w_key, w_value, w_out, partial, query_rot, key_rot, values, query_unit, key_unit,
    stats, context, load_sems, save_sems, gather_send, gather_recv, *scratch,
):
    place = Place()
    count, width = inputs_ref.shape
    experts = picks_ref.shape[1]
    loads = [
        pltpu.make_async_copy(source, target, load_sems.at[i])
        for i, (source, target) in enumerate(
            (
                (w_key_ref, w_key), (w_value_ref, w_value),
                (w_query_ref, w_query), (w_out_ref, w_out),
            )
        )
    ]
    for load in loads:
        load.start()
    float_in = inputs_ref[...].astype(F32)
    first_scale = inverse_rms(float_in)
    own = pl.ds(place.x * count, count)
    seq[own] = (float_in * first_scale * attn_gain_ref[...]).astype(BF16)
    greet([place.on_line(1), place.on_line(-1)])
    run(line_gather_steps(place, seq, count, (gather_send, gather_recv)))
    for load in loads:
        load.wait()
    attend(seq, w_query, w_key, w_value, q_gain_ref, k_gain_ref, cos_ref, sin_ref,
           query_rot, key_rot, values, query_unit, key_unit, stats, context)
    for n in range(0, width, 512):
        here = pl.ds(n, 512)
        partial[:, here] = dot(context[...], w_out[:, here], NN).astype(BF16)
    steps = line_scatter_steps(place, partial, count, scratch)
    next(steps)
    saves = [
        pltpu.make_async_copy(source, target, save_sems.at[i])
        for i, (source, target) in enumerate(
            (
                (seq, seq_ref), (query_rot, query_rot_ref), (key_rot, key_rot_ref),
                (values, values_ref), (query_unit, query_unit_ref), (key_unit, key_unit_ref),
                (stats, stats_ref), (context, context_ref),
            )
        )
    ]
    for save in saves:
        save.start()
    run(steps)
    in_b = scratch[1]
    attended = partial[own].astype(F32) + in_b[0].astype(F32) + in_b[1].astype(F32)
    hidden = float_in + attended
    hidden_ref[...] = hidden
    second_scale = inverse_rms(hidden)
    mixed = (hidden * second_scale * mlp_gain_ref[...]).astype(BF16)
    mixed_ref[:, :width] = mixed
    logits = dot(mixed, router_ref[...], NT)
    raised = jnp.exp(logits - jnp.max(logits, axis=1, keepdims=True))
    probs = raised / jnp.sum(raised, axis=1, keepdims=True)
    picked = picks_ref[...] * probs
    picked_total = jnp.sum(picked, axis=1, keepdims=True)
    gates = picked / picked_total
    high = gates.astype(BF16)
    low = (gates - high.astype(F32)).astype(BF16)
    mixed_ref[:, width:] = jnp.concatenate([high, low], axis=1)
    state_ref[:, : 2 * experts] = jnp.concatenate([probs, gates], axis=1)
    lane = lax.broadcasted_iota(jnp.int32, (count, 2 * experts), 1)
    extra = jnp.where(lane == 0, picked_total, jnp.where(lane == 1, second_scale, first_scale))
    state_ref[:, 2 * experts :] = extra
    for save in saves:
        save.wait()


def forward(inputs, attn_gain, q_gain, k_gain, cosine, sine, mlp_gain, router_t, picks,
            w_query, w_key, w_value, w_out, collective_id):
    count, width = inputs.shape
    head = cosine.shape[1]
    length = 4 * count
    wide = w_query.shape[1]
    saved = [
        ((length, width), BF16), ((length, wide), BF16), ((length, head), BF16),
        ((length, head), BF16), ((length, wide), F32), ((length, head), F32),
        ((length, head), F32), ((length, wide), BF16),
    ]
    kept = [pltpu.VMEM(dims, dtype) for dims, dtype in saved]
    return pl.pallas_call(
        forward_kernel,
        out_shape=(
            shape((count, width + 128)),
            shape((count, width), F32),
            shape((count, 256), F32),
            *[shape(dims, dtype) for dims, dtype in saved],
        ),
        in_specs=[VMEM] * 9 + [ANY] * 4,
        out_specs=(VMEM, VMEM, VMEM, *[ANY] * 8),
        scratch_shapes=[
            kept[0],
            *[pltpu.VMEM(w.shape, BF16) for w in (w_query, w_key, w_value, w_out)],
            pltpu.VMEM((length, width), BF16),
            *kept[1:],
            *dma_sems(4, 8, 4, 4),
            *line_scatter_scratch(count, width),
        ],
        compiler_params=pltpu.CompilerParams(
            collective_id=collective_id, has_side_effects=True, vmem_limit_bytes=60 * 2**20
        ),
        cost_estimate=pl.CostEstimate(flops=7 * 10**10, bytes_accessed=10**8, transcendentals=0),
        name="forward",
    )(inputs, attn_gain, q_gain, k_gain, cosine, sine, mlp_gain, router_t, picks,
      w_query, w_key, w_value, w_out)


def backward_kernel(
    grad_att_ref, inputs_ref, attn_gain_ref, q_gain_ref, k_gain_ref, cos_ref, sin_ref, state_ref,
    grad_hidden_ref, router_grad_ref, mlp_grad_ref,
    gw_b_ref, seq_ref, w_query_ref, w_key_ref, w_value_ref, w_out_ref,
    query_rot_ref, key_rot_ref, values_ref, query_unit_ref, key_unit_ref, stats_ref, context_ref,
    grad_inputs_ref, router_out_ref, gains_out_ref, all_w_ref, right_b_ref, left_b_ref,
    sum_left_ref, sum_right_ref,
    grad_rows, seq, w_query, w_key, w_value, w_out,
    query_rot, key_rot, values, query_unit, key_unit, stats, context,
    grad_context, grad_qkv, summed, out_w, qkv_w, gains,
    late, late_in, router_all, both_sum, load_sems, line_send, line_recv, second_send, second_recv,
    *scratch,
):
    place = Place()
    count, width = inputs_ref.shape
    experts = router_grad_ref.shape[0]
    head = cos_ref.shape[1]
    pairs = (
        (context_ref, context), (w_out_ref, w_out), (query_rot_ref, query_rot),
        (key_rot_ref, key_rot), (values_ref, values), (stats_ref, stats),
        (query_unit_ref, query_unit), (key_unit_ref, key_unit), (w_query_ref, w_query),
        (w_key_ref, w_key), (w_value_ref, w_value), (seq_ref, seq),
    )
    loads = [
        pltpu.make_async_copy(source, target, load_sems.at[i])
        for i, (source, target) in enumerate(pairs)
    ]
    for load in loads:
        load.start()
    own = pl.ds(place.x * count, count)
    grad_rows[own] = grad_att_ref[...]
    far = {
        "x": [place.on_line(step) for step in (1, -1, 2)],
        "z": [place.device("z", step) for step in (1, -1, 2)],
        "y": [place.device("y", step) for step in (1, -1, 2)],
        "core": [place.device(other=1)],
    }
    greet([device for axis in ("x", "z", "y", "core") for device in far[axis]])
    line = line_gather_steps(place, grad_rows, count, (line_send, line_recv))
    next(line)

    run(line)

    half = width // 2
    for load in loads[:2]:
        load.wait()
    for n in range(0, width, 512):
        where = (pl.ds((n // half) * context.shape[1], context.shape[1]), pl.ds(n % half, 512))
        out_w[where] = dot(context[...], grad_rows[:, pl.ds(n, 512)], TN).astype(BF16)

    def scattered(weights, columns, scratch):
        rows = weights.shape[0] // 32

        def block(dz, dy, other):
            return weights.at[pl.ds(place.block("z", dz, dy, other) * rows, rows)]

        def finish(row, value):
            both_sum[pl.ds(row, 16), columns] = value.astype(BF16)

        return plane_scatter_steps(place, rows, lambda dz, dy: None, block, scratch, finish)

    out_width = out_w.shape[1]
    scatter_out, scratch = scratch[:9], scratch[9:]
    scatter_qkv, scratch = scratch[:9], scratch[9:]
    gather_both, scratch = scratch[:4], scratch[4:]
    late_send, late_recv, keep_sem, *scratch = scratch
    sums_scratch, scratch = scratch[:6], scratch[6:]

    def out_total():
        return scattered(out_w, pl.ds(0, out_width), scatter_out)

    outs = out_total()
    next(outs)
    sums = first_sums_steps(place, gw_b_ref, sum_left_ref, sum_right_ref, *sums_scratch)
    next(sums)
    for load in loads[2:]:
        load.wait()
    back = attend_back(grad_rows, seq, w_query, w_key, w_value, w_out, q_gain_ref, k_gain_ref,
                       cos_ref, sin_ref, query_rot, key_rot, values, query_unit, key_unit, stats,
                       grad_context, grad_qkv, gains)
    gains[...] = jnp.zeros_like(gains)
    for _ in back:
        next(outs, None)
    heads = query_rot.shape[1]
    block_rows = summed.shape[0] // 4
    part = experts // 4
    for i in range(4):
        router = router_grad_ref[pl.ds(i * part, part)]
        high = router.astype(BF16)
        summed[pl.ds(i * block_rows + count, part)] = high
        summed[pl.ds(i * block_rows + count + part, part)] = (router - high.astype(F32)).astype(BF16)
    for n in range(0, width, 512):
        here = pl.ds(n, 512)
        value = dot(grad_qkv[:, :heads], w_query[here], NT)
        value = value + dot(grad_qkv[:, heads : heads + head], w_key[here], NT)
        value = value + dot(grad_qkv[:, heads + head :], w_value[here], NT)
        for i in range(4):
            summed[pl.ds(i * block_rows, count), here] = value[i * count : (i + 1) * count].astype(BF16)
    line_scatter = scratch
    line = line_scatter_steps(place, summed, block_rows, line_scatter)
    next(line)
    for n in range(0, grad_qkv.shape[1], 256):
        here = pl.ds(n, 256)
        qkv_w[:, here] = dot(seq[...], grad_qkv[:, here], TN).astype(BF16)

    rows = both_sum.shape[0]

    def qkv_total():
        yield from scattered(qkv_w, pl.ds(out_width, qkv_w.shape[1]), scatter_qkv)
        for _ in outs:
            pass
        keep = pltpu.make_async_copy(
            both_sum, all_w_ref.at[pl.ds(place.block() * rows, rows)], keep_sem.at[0]
        )
        keep.start()
        yield from plane_gather_steps(
            place, both_sum, lambda at: all_w_ref.at[pl.ds(at * rows, rows)], gather_both
        )
        keep.wait()

    second = second_sends(
        place, gw_b_ref, sum_left_ref, sum_right_ref, right_b_ref, left_b_ref, second_send, second_recv
    )
    for copy in second[:2]:
        copy.start()
    run(sums)
    for copy in second[2:]:
        copy.start()
    qkvs = qkv_total()
    next(qkvs)
    next(line)
    for _ in range(4):
        next(qkvs, None)
    run(line)
    in_b = line_scatter[1]

    def line_total(start, size):
        here = pl.ds(start, size)
        total = summed[pl.ds(place.x * block_rows + start, size)].astype(F32)
        return total + in_b[0, here].astype(F32) + in_b[1, here].astype(F32)

    grad_normed = line_total(0, count)
    late[...] = jnp.zeros_like(late)
    late[:part] = line_total(count, part) + line_total(count + part, part)
    float_in = inputs_ref[...].astype(F32)
    first_scale = state_ref[:, 2 * experts + 2 : 2 * experts + 3]
    grad_inputs_ref[...] = (
        grad_hidden_ref[...] + norm_back(float_in, first_scale, attn_gain_ref[...], grad_normed)
    ).astype(BF16)
    late[part : part + 1, :] = jnp.sum(grad_normed * float_in * first_scale, axis=0, keepdims=True)
    late[part + 1 : part + 2, :head] = gains[0:1, :]
    late[part + 1 : part + 2, head : 2 * head] = gains[1:2, :]
    late[part + 2 : part + 3, :] = mlp_grad_ref[...]

    def late_total():
        base = 0
        for axis in ("x", "z", "y", "core"):
            peers = far[axis]
            span = pl.ds(part, 8) if axis == "x" else pl.ds(0, part + 8)
            copies = [
                remote(late.at[span], late_in.at[base + i, span], late_send.at[base + i],
                       late_recv.at[base + i], device)
                for i, device in enumerate(peers)
            ]
            for copy in copies:
                copy.start()
            yield
            for copy in copies:
                copy.wait()
            total = late[span]
            for i in range(len(peers)):
                total = total + late_in[base + i, span]
            late[span] = total
            base += len(peers)
        router_all[place.x] = late[:part]
        mine = router_all.at[place.x]
        copies = [
            remote(mine, mine, late_send.at[base + i], late_recv.at[base + i], device)
            for i, device in enumerate(far["x"])
        ]
        for copy in copies:
            copy.start()
        yield
        for copy in copies:
            copy.wait_send()
        for i, step in enumerate((-1, 1, 2)):
            there = router_all.at[(place.x + step) % 4]
            remote(
                there, there, late_send.at[base + i], late_recv.at[base + i], far["x"][0]
            ).wait_recv()

    lates = late_total()
    running = [qkvs, lates]
    while running:
        for steps in list(running):
            if next(steps, "end") == "end":
                running.remove(steps)
    gains_out_ref[...] = late[part : part + 8]
    for i in range(4):
        router_out_ref[i * part : (i + 1) * part] = router_all[i]
    for copy in second:
        copy.wait()


def backward(grad_att, inputs, attn_gain, q_gain, k_gain, cosine, sine, state, grad_hidden,
             router_grad, mlp_grad, gw_b, weights, saved, collective_id):
    count, width = inputs.shape
    length = 4 * count
    head = cosine.shape[1]
    seq, query_rot, key_rot, values, query_unit, key_unit, stats, context = saved
    w_query, w_key, w_value, w_out = weights
    wide = w_query.shape[1]
    total = wide + 2 * head
    experts = router_grad.shape[0]
    part = experts // 4
    block_rows = count + 2 * part
    rows = width // 32
    shard = gw_b.shape[1] // 4
    like = lambda array: pltpu.VMEM(array.shape, array.dtype)
    return pl.pallas_call(
        backward_kernel,
        out_shape=(
            shape((count, width)),
            shape((experts, width), F32),
            shape((8, width), F32),
            shape((width, width // 2 + total)),
            *[shape((3, shard, width))] * 2,
            *[shape((3, shard // 2, width))] * 2,
        ),
        in_specs=[VMEM] * 11 + [ANY] * 13,
        out_specs=(VMEM, VMEM, VMEM) + (ANY,) * 5,
        scratch_shapes=[
            pltpu.VMEM((length, width), BF16),
            *[like(a) for a in (seq, w_query, w_key, w_value, w_out)],
            *[like(a) for a in saved[1:]],
            pltpu.VMEM((length, wide), BF16),
            pltpu.VMEM((length, total), BF16),
            pltpu.VMEM((4 * block_rows, width), BF16),
            pltpu.VMEM((2 * wide, width // 2), BF16),
            pltpu.VMEM((width, total), BF16),
            pltpu.VMEM((8, head), F32),
            pltpu.VMEM((part + 8, width), F32),
            pltpu.VMEM((10, part + 8, width), F32),
            pltpu.VMEM((4, part, width), F32),
            pltpu.VMEM((rows, width // 2 + total), BF16),
            *dma_sems(12, 4, 4, 4, 4),
            *scatter_scratch(2 * wide // 32, width // 2),
            *scatter_scratch(rows, total),
            *gather_sems(),
            *dma_sems(13, 13, 1),
            *first_sums_scratch(shard // 2, width),
            *line_scatter_scratch(block_rows, width),
        ],
        compiler_params=pltpu.CompilerParams(
            collective_id=collective_id, has_side_effects=True, vmem_limit_bytes=62 * 2**20
        ),
        cost_estimate=pl.CostEstimate(flops=10**11, bytes_accessed=10**8, transcendentals=0),
        name="backward",
    )(grad_att, inputs, attn_gain, q_gain, k_gain, cosine, sine, state, grad_hidden, router_grad,
      mlp_grad, gw_b, seq, w_query, w_key, w_value, w_out, *saved[1:])


def along_line(value, step):
    return lax.ppermute(value, "tensor", [(i, (i + step) % 4) for i in range(4)])


def per_device(
    inputs,
    attn_gain,
    w_query,
    w_key,
    w_value,
    q_gain,
    k_gain,
    w_out,
    mlp_gain,
    w_router,
    w_gate,
    w_up,
    w_down,
    routes,
    grad_out,
):
    row_count, model_width = inputs.shape
    head_size = q_gain.shape[0]
    expert_count = w_router.shape[1]
    place = lax.axis_index("expert")
    first = (2 * place).astype(jnp.int32).reshape(1)

    chosen = routes[:, :, None] == jnp.arange(expert_count, dtype=jnp.int32)[None, None, :]
    picks = jnp.sum(chosen.astype(F32), axis=1)
    before = (jnp.arange(row_count)[:, None] > jnp.arange(row_count)[None, :]).astype(BF16)
    rank = jnp.dot(before, picks.astype(BF16), preferred_element_type=F32)
    base = 20 * ((place // 4) % 2 * 2 + place % 2)
    slots = jnp.where(picks > 0.0, rank + base.astype(F32), -1.0)
    slots = jnp.concatenate([slots, jnp.full_like(slots, -1.0)], axis=1).astype(BF16)
    dout_all = lax.all_gather(jnp.concatenate([grad_out, slots], axis=1), "expert", axis=0)

    gate_t = jnp.swapaxes(w_gate, 1, 2)
    up_t = jnp.swapaxes(w_up, 1, 2)
    own = [jnp.stack([gate_t[j], up_t[j], w_down[j]]) for j in range(2)]
    half = own[0].shape[1] // 2
    cosine, sine = rope_tables(4 * row_count, head_size)
    router_t = w_router.T
    q_gain, k_gain = q_gain[None], k_gain[None]
    attn_gain, mlp_gain = attn_gain[None], mlp_gain[None]
    left_a, right_a = along_line(own[0], 1), along_line(own[0], -1)
    mixed, hidden, state, *saved = forward(
        inputs, attn_gain, q_gain, k_gain, cosine, sine, mlp_gain, router_t, picks,
        w_query, w_key, w_value, w_out, 0,
    )

    mixed, left_a, right_a, own[1] = lax.optimization_barrier((mixed, left_a, right_a, own[1]))
    low_a, high_a = along_line(left_a[:, :half], 1), along_line(right_a[:, half:], -1)
    left_b, right_b = along_line(own[1], 1), along_line(own[1], -1)
    grad_a, grad_b, rows_a, rows_b, gate_a, gate_b = gather_select(mixed, dout_all, 1)
    rows_a, left_b, right_b, low_a, high_a = lax.optimization_barrier(
        (rows_a, left_b, right_b, low_a, high_a)
    )
    low_b, high_b = along_line(left_b[:, :half], 1), along_line(right_b[:, half:], -1)
    out_a, back_a, gw_a = expert_layer(
        first, (own[0], left_a, right_a, low_a, high_a), rows_a, grad_a, gate_a
    )
    rows_b, back_a = lax.optimization_barrier((rows_b, back_a))
    out_b, back_b, gw_b, sum_left_a, sum_right_a = expert_layer(
        first + 1, (own[1], left_b, right_b, low_b, high_b), rows_b, grad_b, gate_b, gw_a, 4
    )
    shares, right_a, left_a, grad_hidden, grad_att, router_grad, mlp_grad = combine_scatter(
        (back_a, back_b), (out_a, out_b), dout_all, (gw_a, sum_left_a, sum_right_a), grad_out,
        hidden, mixed, state, picks, mlp_gain, router_t, 2,
    )
    expert_mix = lax.psum_scatter(
        shares.reshape(-1, model_width), "expert", scatter_dimension=0, tiled=True
    )
    output = (hidden + expert_mix.astype(F32)).astype(BF16)

    results = backward(
        grad_att, inputs, attn_gain, q_gain, k_gain, cosine, sine, state, grad_hidden,
        router_grad, mlp_grad, gw_b, (w_query, w_key, w_value, w_out), saved, 3,
    )
    grad_inputs, router_grad, gains, all_w, right_b, left_b, _, _ = results
    wide, narrow = w_query.shape[1], w_key.shape[1]
    start = model_width // 2
    out_w = jnp.concatenate([all_w[:wide, :start], all_w[wide:, :start]], axis=1).astype(F32)
    query_w = all_w[:, start : start + wide].astype(F32)
    key_w = all_w[:, start + wide : start + wide + narrow].astype(F32)
    value_w = all_w[:, start + wide + narrow :].astype(F32)

    def line_total(i):
        shard = w_down.shape[1]
        return jnp.stack([
            gw[i, :shard].astype(F32) + right[i].astype(F32) + left[i].astype(F32)
            for gw, right, left in ((gw_a, right_a, left_a), (gw_b, right_b, left_b))
        ])

    return (
        output,
        grad_inputs,
        gains[0],
        query_w,
        key_w,
        value_w,
        gains[1, :head_size],
        gains[1, head_size : 2 * head_size],
        out_w,
        gains[2],
        router_grad.T,
        jnp.swapaxes(line_total(0), 1, 2),
        jnp.swapaxes(line_total(1), 1, 2),
        line_total(2),
    )


def solution(mesh):
    placed = (
        P(("expert", "tensor"), None),
        P(),
        P(None, "tensor"),
        P(None, "tensor"),
        P(None, "tensor"),
        P(),
        P(),
        P("tensor", None),
        P(),
        P(),
        P("expert", None, "tensor"),
        P("expert", None, "tensor"),
        P("expert", "tensor", None),
        P(("expert", "tensor"), None),
        P(("expert", "tensor"), None),
    )
    return jax.shard_map(
        per_device,
        mesh=mesh,
        in_specs=placed,
        out_specs=(
            P(("expert", "tensor"), None),
            P(("expert", "tensor"), None),
            P(),
            P(None, "tensor"),
            P(None, "tensor"),
            P(None, "tensor"),
            P(),
            P(),
            P("tensor", None),
            P(),
            P(),
            P("expert", None, "tensor"),
            P("expert", None, "tensor"),
            P("expert", "tensor", None),
        ),
        check_vma=False,
    )
```

time: 1100 us -> 594 us (0.54)
  Pallas kernels: 0 us -> 516 us
  waiting for transfers between devices: 436 us -> 0.06 us
  local copies, waits for them, and re-layouts: 217 us -> 15 us
  matrix products: 184 us -> 0.14 us
  blocking collectives: 77.1 us -> 0 us
  other arithmetic: 102 us -> 34 us
  starting transfers between devices: 59.6 us -> 9.8 us
    pallas_call x0 -> x6, Pallas kernels: none -> 516 us  [the longest x1 202 us: backward(): pl.pallas_call(backward_kernel, out_shape=(shape((count, width)), shape((...]
    dot_general x30 -> x1, matrix products: 184 us -> 0.14 us  [per_device(): rank = jnp.dot(before, picks.astype(BF16), preferred_element_type=F32)]
    all_to_all x8 -> x0, waiting for transfers between devices: 163 us -> none  [the longest x2 48.6 us: sent_to_all(): lax.all_to_all(jnp.broadcast_to(x[None], (peers, *x.shape)), axis, 0, 0,...]
    psum x2 -> x0, waiting for transfers between devices: 147 us -> none  [the longest x1 147 us: per_device(): lax.psum((grad_router, attn_gain_grad, q_gain_grad, k_gain_grad, mlp_gain...]
    reduce_scatter x3 -> x1, waiting for transfers between devices: 125 us -> 0.01 us  [per_device(): lax.psum_scatter(shares.reshape(-1, model_width), 'expert', scatter_dimen...]
    psum x1 -> x0, blocking collectives: 77.1 us -> none  [per_device(): lax.psum((grad_router, attn_gain_grad, q_gain_grad, k_gain_grad, mlp_gain...]
    reshape x10 -> x0, local copies, waits for them, and re-layouts: 68.8 us -> none  [the longest x2 20.1 us: per_device(): send_buffer.reshape(group_count, local_experts, capacity, model_width)]
    all_to_all x8 -> x0, starting transfers between devices: 59.4 us -> none  [the longest x1 16 us: per_device(): lax.all_to_all(send_buffer, 'expert', split_axis=0, concat_axis=0, tiled=...]
  transfers between devices with their start and end apart: 14 -> 10, of which waited for: 11 -> 0; matrix products, arithmetic and copies ran while one was open for 33% -> 6% of each run, Pallas kernels for 0% -> 71%
where the time goes in v2:
time: 594 us; the launch traced here: 589 us
  Pallas kernels  516 us (87%)
  other arithmetic  34 us (6%)
  local copies, waits for them, and re-layouts  15 us (3%)
  between operations  14.6 us (2%)
  starting transfers between devices  9.8 us (2%)
    pallas_call x1, Pallas kernels, backward(): pl.pallas_call(backward_kernel, out_shape=(shape((count, width)), shape((...  202 us
    pallas_call x1, Pallas kernels, forward(): pl.pallas_call(forward_kernel, out_shape=(shape((count, width + 128)), sh...  115 us
    pallas_call x1, Pallas kernels, gather_select(): pl.pallas_call(gather_select_kernel, out_shape=(shape((32, count, full)),...  69.9 us
    pallas_call x1, Pallas kernels, combine_scatter(): pl.pallas_call(combine_scatter_kernel, out_shape=(shape((32, count, width...  66.1 us
    pallas_call x2, Pallas kernels, expert_layer(): pl.pallas_call(expert_sending_kernel if sending else expert_kernel, out_s...  62.6 us
  transfers between devices with their start and end apart: 10, of which 0 were waited for; matrix products, arithmetic and copies ran while one was open for 6% of the time, Pallas kernels for 71%

profile of v2, /device:TPU:1, one launch (start us, length us, event | category | flops | bytes accessed | tf_op | source)
XLA Modules:
  0.0 589.2 jit_solution(6075949344708445612)
XLA Ops:
  7.2 0.0 all-gather.3.cloned.1.call-start
  7.3 0.8 convert_reduce_fusion
  8.1 0.1 fusion.2
  8.2 0.1 copy.34
  8.4 1.9 fusion.3
  10.3 0.0 all-gather.3.cloned.1.call-update
  10.3 0.0 reduce-scatter.2.cloned.1.call-start
  10.4 0.2 fusion.11
  10.5 2.1 fusion.9
  12.7 1.7 pad_maximum_fusion.1.own_ref
  14.3 3.3 collective-permute-start.1
  17.6 0.7 copy.31.picks_ref
  18.4 1.0 fusion.6
  19.4 1.0 pad_maximum_fusion.3
  20.4 114.9 %forward.1 = (bf16[128,2176]{1,0:T(8,128)(2,1)}, f32[128,2048]{1,0:T(8,128)}, f32[128,256]{1,0:T(8,128)}, bf16[512,2048]{1,0:T(8,128)(2,1)}, bf16[512,1024]{1,0:...) custom-call(bf16[128,2048]{1,0:T(8,128)(2,1)} %inputs_ref.3, ...), custom_call_target="tpu_custom_call" | custom-call | flops 70000001024 | bytes 100000000 | tf_op jit(solution)/shard_map/forward/pallas_call | solution.py:1158
  135.3 1.7 pad_maximum_fusion.2.own_ref
  136.9 1.5 collective-permute-start.2
  138.4 1.3 slice.117
  139.7 1.4 slice.118
  141.1 1.4 collective-permute-start.5
  142.5 0.2 collective-permute-start.4
  142.6 69.9 %gather_select.1 = (bf16[32,128,2176]{2,1,0:T(8,128)(2,1)}, bf16[640,2048]{1,0:T(8,128)(2,1)}, bf16[640,2048]{1,0:T(8,128)(2,1)}, bf16[640,2048]{1,0:T(8,128)(2,...) custom-call(bf16[128,2176]{1,0:T(8,128)(2,1)} %get-tuple-element.65.x_ref.mixed_ref, ...), custom_call_target="tpu_custom_call" | custom-call | flops 60000002048 | bytes 100000000 | tf_op jit(solution)/shard_map/gather_select/pallas_call | solution.py:524
  212.6 0.0 copy-start.6
  212.6 1.8 slice.119
  214.4 1.4 slice.120
  215.8 3.0 collective-permute-start.7
  218.8 0.4 collective-permute-start.6
  219.2 30.8 %expert_layer.1 = (bf16[640,2048]{1,0:T(8,128)(2,1)}, bf16[640,2176]{1,0:T(8,128)(2,1)}, bf16[3,768,2048]{2,1,0:T(8,128)(2,1)}) custom-call(s32[1]{0:T(128)} %bitcast.8.expert_ref, bf16[3,192,2048]{2,1,0:T(8,128)(2,1)} %pad_maximum_fusion.1.own_ref, bf16[3,192,2048]{2,1,0:T(8,128)(2,1)} %collective-permute-done.left_ref, ...), custom_call_target="tpu_custom_call" | custom-call | flops 18119393280 | bytes 31981568 | tf_op jit(solution)/shard_map/expert_layer/pallas_call | solution.py:895
  250.0 0.0 copy-start.7
  250.0 1.0 copy-done.7
  251.0 31.8 %expert_sending.1 = (bf16[640,2048]{1,0:T(8,128)(2,1)}, bf16[640,2176]{1,0:T(8,128)(2,1)}, bf16[3,768,2048]{2,1,0:T(8,128)(2,1)}, bf16[3,96,2048]{2,1,0:T(8,128)(2,1)}, bf16[3,96,2048]{2,1,0:T(8,128)(2,1)}) custom-call(s32[1]{0:T(128)S(6)} %add.80.expert_ref, bf16[3,192,2048]{2,1,0:T(8,128)(2,1)} %pad_maximum_fusion.2.own_ref, ...), custom_call_target="tpu_custom_call" | custom-call | flops 18119393280 | bytes 31981568 | tf_op jit(solution)/shard_map/expert_sending/pallas_call | solution.py:895
  282.9 66.1 %combine_scatter.1 = (bf16[32,128,2048]{2,1,0:T(8,128)(2,1)}, bf16[3,192,2048]{2,1,0:T(8,128)(2,1)}, bf16[3,192,2048]{2,1,0:T(8,128)(2,1)}, f32[128,2048]{1,0:T(...) custom-call(bf16[640,2176]{1,0:T(8,128)(2,1)} %get-tuple-element.77.back_a_ref, ...), custom_call_target="tpu_custom_call" | custom-call | flops 60000002048 | bytes 100000000 | tf_op jit(solution)/shard_map/combine_scatter/pallas_call | solution.py:689
  349.0 0.0 reduce-scatter.2.cloned.1.call-update
  349.0 202.2 %backward.1 = (bf16[128,2048]{1,0:T(8,128)(2,1)}, f32[64,2048]{1,0:T(8,128)}, f32[8,2048]{1,0:T(8,128)}, bf16[2048,2304]{1,0:T(8,128)(2,1)}, bf16[3,192,2048]{2,...) custom-call(bf16[128,2048]{1,0:T(8,128)(2,1)} %get-tuple-element.91.gra, ...), custom_call_target="tpu_custom_call" | custom-call | flops 99999997952 | bytes 100000000 | tf_op jit(solution)/shard_map/backward/pallas_call | solution.py:1404
  551.3 1.2 slice_bitcast_fusion
  552.5 4.6 convert_add_fusion.1
  557.1 3.1 convert_add_fusion
  560.2 1.9 pad_maximum_fusion
  562.2 1.9 maximum_bitcast_fusion.1
  564.1 1.9 maximum_bitcast_fusion
  566.0 0.6 fusion.8
  566.6 4.4 maximum_convert_fusion
  571.0 1.5 fusion.12
  572.5 1.5 slice_convert_fusion.1
  574.0 4.6 slice_convert_fusion
  578.6 2.0 add_convert_fusion
  580.6 0.8 copy.37
  581.4 0.8 copy.38
  (33 shorter events, 0.1 us)
Async XLA Ops:
  7.2 3.2 copy-start.2
  7.2 135.5 %all-gather.3.cloned.1.call-start = ((), (), s32[]{:S(2)}) async-start(), calls=%async_computation.2 | async-start | bytes 18382848 | tf_op jit(solution)/shard_map/all_gather | solution.py:1481
  10.3 568.3 %reduce-scatter.2.cloned.1.call-start = ((), (), s32[]{:S(2)}) async-start(), calls=%async_computation.1 | async-start | bytes 17301504 | tf_op jit(solution)/shard_map/reduce_scatter | solution.py:1516
  14.3 122.6 %collective-permute-start.1 = (bf16[3,192,2048]{2,1,0:T(8,128)(2,1)}, bf16[3,192,2048]{2,1,0:T(8,128)(2,1)}, u32[]{:S(2)}, u32[]{:S(2)}) collective-permute-start(bf16[3,192,2048]{2,1,0:T(8,128)(2,1)} %pad_maximum_fusion.1.own_ref), channel_id=1, source_target_pairs={{0,3},{1,0},{2,1},{3,2},{4,7},{5,4},{6,5},{7,6},{8,11},{9,8},{10,9... | collective-permute-start | bytes 7077896 | tf_op jit(solution)/shard_map/ppermute | solution.py:1448
  17.6 119.3 %collective-permute-start = (bf16[3,192,2048]{2,1,0:T(8,128)(2,1)}, bf16[3,192,2048]{2,1,0:T(8,128)(2,1)}, u32[]{:S(2)}, u32[]{:S(2)}) collective-permute-start(bf16[3,192,2048]{2,1,0:T(8,128)(2,1)} %pad_maximum_fusion.1.own_ref), channel_id=1, source_target_pairs={{0,1},{1,2},{2,3},{3,0},{4,5},{5,6},{6,7},{7,4},{8,9},{9,10},{10,1... | collective-permute-start | bytes 7077896 | tf_op jit(solution)/shard_map/ppermute | solution.py:1448
  136.9 75.7 %collective-permute-start.3 = (bf16[3,192,2048]{2,1,0:T(8,128)(2,1)}, bf16[3,192,2048]{2,1,0:T(8,128)(2,1)}, u32[]{:S(2)}, u32[]{:S(2)}) collective-permute-start(bf16[3,192,2048]{2,1,0:T(8,128)(2,1)} %pad_maximum_fusion.2.own_ref), channel_id=1, source_target_pairs={{0,3},{1,0},{2,1},{3,2},{4,7},{5,4},{6,5},{7,6},{8,11},{9,8},{10,9... | collective-permute-start | bytes 7077896 | tf_op jit(solution)/shard_map/ppermute | solution.py:1448
  136.9 75.7 %collective-permute-start.2 = (bf16[3,192,2048]{2,1,0:T(8,128)(2,1)}, bf16[3,192,2048]{2,1,0:T(8,128)(2,1)}, u32[]{:S(2)}, u32[]{:S(2)}) collective-permute-start(bf16[3,192,2048]{2,1,0:T(8,128)(2,1)} %pad_maximum_fusion.2.own_ref), channel_id=1, source_target_pairs={{0,1},{1,2},{2,3},{3,0},{4,5},{5,6},{6,7},{7,4},{8,9},{9,10},{10,1... | collective-permute-start | bytes 7077896 | tf_op jit(solution)/shard_map/ppermute | solution.py:1448
  141.1 71.5 %collective-permute-start.5 = (bf16[3,96,2048]{2,1,0:T(8,128)(2,1)S(1)}, bf16[3,96,2048]{2,1,0:T(8,128)(2,1)S(1)}, u32[]{:S(2)}, u32[]{:S(2)}) collective-permute-start(bf16[3,96,2048]{2,1,0:T(8,128)(2,1)S(1)} %slice.118), channel_id=1, source_target_pairs={{0,3},{1,0},{2,1},{3,2},{4,7},{5,4},{6,5},{7,6},{8,11},{9,8},{10,9... | collective-permute-start | bytes 3538952 | tf_op jit(solution)/shard_map/ppermute | solution.py:1448
  142.5 70.1 %collective-permute-start.4 = (bf16[3,96,2048]{2,1,0:T(8,128)(2,1)S(1)}, bf16[3,96,2048]{2,1,0:T(8,128)(2,1)}, u32[]{:S(2)}, u32[]{:S(2)}) collective-permute-start(bf16[3,96,2048]{2,1,0:T(8,128)(2,1)S(1)} %slice.117), channel_id=1, source_target_pairs={{0,1},{1,2},{2,3},{3,0},{4,5},{5,6},{6,7},{7,4},{8,9},{9,10},{10,1... | collective-permute-start | bytes 3538952 | tf_op jit(solution)/shard_map/ppermute | solution.py:1448
  212.6 3.2 copy-start.6
  215.8 34.2 %collective-permute-start.7 = (bf16[3,96,2048]{2,1,0:T(8,128)(2,1)S(1)}, bf16[3,96,2048]{2,1,0:T(8,128)(2,1)}, u32[]{:S(2)}, u32[]{:S(2)}) collective-permute-start(bf16[3,96,2048]{2,1,0:T(8,128)(2,1)S(1)} %slice.120), channel_id=1, source_target_pairs={{0,3},{1,0},{2,1},{3,2},{4,7},{5,4},{6,5},{7,6},{8,11},{9,8},{10,9... | collective-permute-start | bytes 3538952 | tf_op jit(solution)/shard_map/ppermute | solution.py:1448
  218.8 31.2 %collective-permute-start.6 = (bf16[3,96,2048]{2,1,0:T(8,128)(2,1)S(1)}, bf16[3,96,2048]{2,1,0:T(8,128)(2,1)S(1)}, u32[]{:S(2)}, u32[]{:S(2)}) collective-permute-start(bf16[3,96,2048]{2,1,0:T(8,128)(2,1)S(1)} %slice.119), channel_id=1, source_target_pairs={{0,1},{1,2},{2,3},{3,0},{4,5},{5,6},{6,7},{7,4},{8,9},{9,10},{10,1... | collective-permute-start | bytes 3538952 | tf_op jit(solution)/shard_map/ppermute | solution.py:1448
  250.0 1.0 copy-start.7
  552.5 4.6 copy-start
  552.5 4.6 copy-start.1
  557.1 8.9 %slice-start = ((s8[9437184]{0:T(1024)(128)(4,1)}), s8[4194304]{0:T(1024)(128)(4,1)S(1)}, s32[]{:S(2)}) async-start(s8[9437184]{0:T(1024)(128)(4,1)} %bitcast.22), calls=%async_computation.3 | async-start | bytes 8388608
  557.1 8.9 %slice-start.1 = ((s8[9437184]{0:T(1024)(128)(4,1)}), s8[4194304]{0:T(1024)(128)(4,1)S(1)}, s32[]{:S(2)}) async-start(s8[9437184]{0:T(1024)(128)(4,1)} %bitcast.22), calls=%async_computation.4 | async-start | bytes 8388608
  562.2 3.8 slice-start.2
  574.0 4.6 copy-start.3
  578.6 2.0 copy-start.5
  578.6 2.8 copy-start.4
Sparse Core Ops, SparseCore 0:
  10.8 78.6 all-gather.2
  349.1 116.6 reduce-scatter.1

commit v3 on v2

--- a/solution.py
+++ b/solution.py
@@ -426,14 +426,21 @@
 
 
 def gather_select_kernel(
-    x_ref, grads_ref, all_ref, grad_a_ref, grad_b_ref, row_a_ref, row_b_ref, gate_a_ref, gate_b_ref,
+    x_ref, grads_ref, gate_w_ref, up_w_ref, down_w_ref, left_gate_ref, right_gate_ref,
+    left_two_ref, right_two_ref, low_ref, high_ref, left_next_ref, right_next_ref,
+    all_ref, grad_a_ref, grad_b_ref, row_a_ref, row_b_ref, gate_a_ref, gate_b_ref,
     tokens, slots, rows_a, rows_b, grads_a, grads_b, gates_a, gates_b,
-    own_sem, load_sems, slot_sems, save_sems, *sems,
+    own_sem, load_sems, save_sems, line_send, line_recv, *sems,
 ):
     place = Place()
     first = 2 * lax.axis_index("expert")
     width = rows_a.shape[1]
-    greet(plane_neighbours(place))
+    greet(plane_neighbours(place) + [place.on_line(1), place.on_line(-1)])
+    line = line_weights_steps(
+        place, gate_w_ref, up_w_ref, down_w_ref, left_gate_ref, right_gate_ref, left_two_ref,
+        right_two_ref, low_ref, high_ref, left_next_ref, right_next_ref, line_send, line_recv,
+    )
+    next(line)
     own = pltpu.make_async_copy(x_ref, all_ref.at[place.block()], own_sem.at[0])
     own.start()
     steps = plane_gather_steps(place, x_ref, lambda at: all_ref.at[at], sems)
@@ -495,6 +502,7 @@
                 grad_turn += 1
         elif stage == 101:
             assert grad_turn == 8
+            next(line)
             own.wait()
             start(False, 0, 0)
             start(False, 1, 1)
@@ -502,6 +510,7 @@
             select(1, 1, False)
         elif stage == 102:
             start(False, 2, 0)
+            next(line)
             for number in range(2, 6):
                 if number + 1 < 6:
                     start(False, number + 1, (number + 1) % 2)
@@ -511,27 +520,76 @@
             start(False, 7, 1)
             select(6, 0, False)
             select(7, 1, False)
+    run(line)
     for copy in saves:
         copy.wait()
 
 
-def gather_select(x, grads, collective_id):
+def line_weights_steps(
+    place, gate_w, up_w, down_w, left_gate, right_gate, left_two, right_two, low, high,
+    left_next, right_next, send_sems, recv_sems,
+):
+    half = gate_w.shape[1] // 2
+    first, second = pl.ds(0, half), pl.ds(half, half)
+    numbers = iter(range(12))
+    started = []
+
+    def send(source, target, side):
+        number = next(numbers)
+        copy = remote(
+            source, target, send_sems.at[number], recv_sems.at[number], place.on_line(side)
+        )
+        copy.start()
+        started.append(copy)
+        return copy
+
+    def onward(left, right, matrix):
+        send(left.at[first], low.at[matrix], 1)
+        send(right.at[second], high.at[matrix], -1)
+
+    near = []
+    for i, w in enumerate((up_w, down_w)):
+        near.append((send(w.at[0], left_two.at[i], 1), send(w.at[0], right_two.at[i], -1)))
+        if i == 0:
+            onward(left_gate, right_gate, 0)
+    send(gate_w.at[1], left_next, 1)
+    send(gate_w.at[1], right_next, -1)
+    yield
+    for i in range(2):
+        for copy in near[i]:
+            copy.wait_recv()
+        onward(left_two.at[i], right_two.at[i], i + 1)
+        yield
+    come = [id(copy) for pair in near for copy in pair]
+    for copy in started:
+        copy.wait_send()
+        if id(copy) not in come:
+            copy.wait_recv()
+
+
+def gather_select(x, grads, gate_w, up_w, down_w, left_gate, right_gate, collective_id):
     count, full = x.shape
     width = full - 128
     total = len(GROUPS) * SLOTS
     rows = shape((total, width))
     gate = shape((total, 128), F32)
+    shard = gate_w.shape[1]
+    two = shape((2, shard, width))
+    far = shape((3, shard // 2, width))
+    one = shape((shard, width))
     return pl.pallas_call(
         gather_select_kernel,
-        out_shape=(shape((32, count, full)), rows, rows, rows, rows, gate, gate),
-        in_specs=[ANY, ANY],
-        out_specs=(ANY,) * 7,
+        out_shape=(
+            two, two, far, far, one, one, shape((32, count, full)), rows, rows, rows, rows, gate, gate
+        ),
+        in_specs=[ANY] * 7,
+        out_specs=(ANY,) * 13,
         scratch_shapes=[
             pltpu.VMEM((2, 4, count, full), BF16),
             pltpu.VMEM((8, 512, 128), BF16),
             *[pltpu.VMEM((total, width), BF16)] * 4,
             *[pltpu.VMEM((total, 128), F32)] * 2,
-            *dma_sems(1, 4, 1, 48),
+            *dma_sems(1, 4, 48, 12, 12),
             *gather_sems(),
         ],
         compiler_params=pltpu.CompilerParams(
@@ -539,13 +597,13 @@
         ),
         cost_estimate=pl.CostEstimate(flops=6 * 10**10, bytes_accessed=10**8, transcendentals=0),
         name="gather_select",
-    )(x, grads)[1:]
+    )(x, grads, gate_w, up_w, down_w, left_gate, right_gate)
 
 
 def combine_scatter_kernel(
-    back_a_ref, back_b_ref, out_a_ref, out_b_ref, slots_ref, gw_ref, sum_left_ref, sum_right_ref,
+    back_a_ref, back_b_ref, out_a_ref, out_b_ref, slots_ref, gw_ref,
     grad_out_ref, hidden_ref, mixed_ref, state_ref, picks_ref, mlp_gain_ref, router_ref,
-    shares_ref, from_right_ref, from_left_ref,
+    shares_ref, from_right_ref, from_left_ref, sum_left_ref, sum_right_ref,
     grad_hidden_ref, grad_att_ref, grad_router_ref, gain_ref,
     rows, slots, blocks, out_rows, share, total, load_sems, row_sems, share_sems,
     line_send, line_recv, *scratch,
@@ -570,7 +628,10 @@
         place, gw_ref, sum_left_ref, sum_right_ref, from_right_ref, from_left_ref, line_send,
         line_recv,
     )
-    for copy in line:
+    sums = first_sums_steps(place, gw_ref, sum_left_ref, sum_right_ref, *scratch[:6])
+    scratch = scratch[6:]
+    next(sums)
+    for copy in line[:2]:
         copy.start()
     made = set()
 
@@ -646,6 +707,10 @@
         load.start()
     turn = 0
     for at, _ in enumerate(plane_scatter_steps(place, count, make, block, scratch, finish)):
+        if at == 6:
+            run(sums)
+            for copy in line[2:]:
+                copy.start()
         if at >= 5:
             for _ in range(2):
                 if turn < len(GROUPS):
@@ -682,7 +747,7 @@
 
 
 def combine_scatter(
-    back, out, slots, line, grad_out, hidden, mixed, state, picks, mlp_gain, router_t, collective_id
+    back, out, slots, gw, grad_out, hidden, mixed, state, picks, mlp_gain, router_t, collective_id
 ):
     count, width = hidden.shape
     groups = len(GROUPS)
@@ -690,14 +755,15 @@
         combine_scatter_kernel,
         out_shape=(
             shape((32, count, width)),
-            *[shape((3, line[0].shape[1] // 4, width))] * 2,
+            *[shape((3, gw.shape[1] // 4, width))] * 2,
+            *[shape((3, gw.shape[1] // 8, width))] * 2,
             shape((count, width), F32),
             shape((count, width)),
             shape(router_t.shape, F32),
             shape((1, width), F32),
         ),
-        in_specs=[ANY] * 8 + [VMEM] * 7,
-        out_specs=(ANY, ANY, ANY, VMEM, VMEM, VMEM, VMEM),
+        in_specs=[ANY] * 6 + [VMEM] * 7,
+        out_specs=(ANY, ANY, ANY, ANY, ANY, VMEM, VMEM, VMEM, VMEM),
         scratch_shapes=[
             pltpu.VMEM((groups, 2, SLOTS, width + 128), BF16),
             pltpu.VMEM((groups, 4, count, 128), BF16),
@@ -706,6 +772,7 @@
             pltpu.VMEM((2, 4, count, width), BF16),
             pltpu.VMEM((count, width + 128), F32),
             *dma_sems(32, 4, 4, 4, 4),
+            *first_sums_scratch(gw.shape[1] // 8, width),
             *scatter_scratch(count, width + 128),
         ],
         compiler_params=pltpu.CompilerParams(
@@ -713,37 +780,12 @@
         ),
         cost_estimate=pl.CostEstimate(flops=6 * 10**10, bytes_accessed=10**8, transcendentals=0),
         name="combine_scatter",
-    )(*back, *out, slots, *line, grad_out, hidden, mixed, state, picks, mlp_gain, router_t)
-
-
-def expert_kernel(
-    expert_ref, own_ref, left_ref, right_ref, far0_ref, far1_ref, x_hbm, d_hbm, gate_hbm,
-    *rest,
-):
-    expert_steps(
-        None, expert_ref, (own_ref, left_ref, right_ref, far0_ref, far1_ref), x_hbm, d_hbm, gate_hbm,
-        *rest,
-    )
-
-
-def expert_sending_kernel(
-    expert_ref, own_ref, left_ref, right_ref, far0_ref, far1_ref, x_hbm, d_hbm, gate_hbm, other_hbm,
-    p_hbm, rb_hbm, gw_hbm, sum_left_hbm, sum_right_hbm, *scratch,
-):
-    *scratch, come, mine, load_sems, send_sems, recv_sems, save_sems = scratch
-    payload = first_sums_steps(
-        Place(), other_hbm, sum_left_hbm, sum_right_hbm, come, mine, load_sems, send_sems,
-        recv_sems, save_sems,
-    )
-    expert_steps(
-        payload, expert_ref, (own_ref, left_ref, right_ref, far0_ref, far1_ref), x_hbm, d_hbm,
-        gate_hbm, p_hbm, rb_hbm, gw_hbm, *scratch,
-    )
+    )(*back, *out, slots, gw, grad_out, hidden, mixed, state, picks, mlp_gain, router_t)
 
 
 def expert_steps(
-    payload, expert_ref, parts, x_hbm, d_hbm, gate_hbm, p_hbm, rb_hbm, gw_hbm,
-    w, x, d, gate, rg, middle, ggp, gup, p, rb, dots, turned, gw, in_sems, out_sems, gw_sems,
+    expert_ref, parts, receive, x_hbm, d_hbm, gate_hbm, p_hbm, rb_hbm, gw_hbm,
+    w, x, d, gate, rg, middle, ggp, gup, p, rb, dots, gw, in_sems, out_sems, gw_sems,
 ):
     f32, bf16 = jnp.float32, jnp.bfloat16
     rows, width = x.shape
@@ -754,16 +796,12 @@
         pltpu.make_async_copy(d_hbm, d, in_sems.at[1]),
         pltpu.make_async_copy(gate_hbm, gate, in_sems.at[2]),
     ]
-    at = 0
-    for i, ref in enumerate(parts):
-        size = ref.shape[1]
-        loads.append(pltpu.make_async_copy(ref, w.at[:, pl.ds(at, size)], in_sems.at[3 + i]))
-        at += size
+    for i, (ref, where) in enumerate(parts):
+        loads.append(pltpu.make_async_copy(ref, w.at[where], in_sems.at[3 + i]))
     for load in loads:
         load.start()
-    if payload is not None:
-        greet([Place().on_line(1), Place().on_line(-1)])
-        next(payload)
+    if receive is not None:
+        next(receive)
     for load in loads:
         load.wait()
 
@@ -773,7 +811,7 @@
         scaled = d[here].astype(f32) * gate[here, 0:1]
         rg[here] = scaled.astype(bf16)
 
-    for c in range(0, hidden, chunk):
+    def hidden_chunk(c):
         here = pl.ds(c, chunk)
         gate_pre = dot(x[...], w[0, here], NT)
         up_pre = dot(x[...], w[1, here], NT)
@@ -784,6 +822,29 @@
         ggp[:, here] = (grad_mid * up_pre * sig * (1.0 + gate_pre * (1.0 - sig))).astype(bf16)
         gup[:, here] = (grad_mid * act).astype(bf16)
 
+    outs = []
+
+    def weight_chunk(c):
+        here = pl.ds(c, chunk)
+        for i, (left, right) in enumerate(((ggp, x), (gup, x), (middle, rg))):
+            turned = left[:, here].T
+            for n in range(0, width, 512):
+                there = pl.ds(n, 512)
+                gw[i, here, there] = dot(turned, right[:, there], NN).astype(bf16)
+            save = pltpu.make_async_copy(
+                gw.at[i, here], gw_hbm.at[i, here], gw_sems.at[c // chunk * 3 + i]
+            )
+            save.start()
+            outs.append(save)
+
+    chunks = list(range(0, hidden, chunk))
+    for c in chunks[:-1]:
+        hidden_chunk(c)
+    if receive is not None:
+        for c in chunks[:-1]:
+            weight_chunk(c)
+        run(receive)
+    hidden_chunk(chunks[-1])
     dots[...] = jnp.zeros_like(dots)
 
     for n in range(0, width, chunk):
@@ -801,29 +862,67 @@
     lane = lax.broadcasted_iota(jnp.int32, (rows, 128), 1)
     tail = jnp.where(lane == expert, high, jnp.where(lane == expert + 64, total - high, 0.0))
     rb[:, pl.ds(width, 128)] = tail.astype(bf16)
-    outs = [
-        pltpu.make_async_copy(rb, rb_hbm, out_sems.at[0]),
-        pltpu.make_async_copy(p, p_hbm, out_sems.at[1]),
-    ]
-    for out in outs:
-        out.start()
-
-    for i, (left, right) in enumerate(((ggp, x), (gup, x), (middle, rg))):
-        turned[...] = left[...].T
-
-        for c in range(0, hidden, chunk):
-            here = pl.ds(c, chunk)
-            for n in range(0, width, 512):
-                there = pl.ds(n, 512)
-                gw[i, here, there] = dot(turned[here], right[:, there], NN).astype(bf16)
-
-        save = pltpu.make_async_copy(gw.at[i], gw_hbm.at[i], gw_sems.at[i])
-        save.start()
-        outs.append(save)
-    if payload is not None:
-        run(payload)
+    outs.append(pltpu.make_async_copy(rb, rb_hbm, out_sems.at[0]))
+    outs.append(pltpu.make_async_copy(p, p_hbm, out_sems.at[1]))
+    outs[-2].start()
+    outs[-1].start()
+    for c in chunks[-1:] if receive is not None else chunks:
+        weight_chunk(c)
     for out in outs:
         out.wait()
+
+
+def near_parts(number, gate_ref, up_ref, down_ref, left_gate, left_two, right_gate, right_two):
+    shard = gate_ref.shape[1]
+    own, left, right = pl.ds(0, shard), pl.ds(shard, shard), pl.ds(2 * shard, shard)
+    return [
+        (gate_ref.at[number], (0, own)), (up_ref.at[number], (1, own)),
+        (down_ref.at[number], (2, own)), (left_gate, (0, left)),
+        (left_two, (pl.ds(1, 2), left)), (right_gate, (0, right)), (right_two, (pl.ds(1, 2), right)),
+    ]
+
+
+def first_expert_kernel(expert_ref, x, d, gate, *refs):
+    weights, low, high, rest = refs[:7], refs[7], refs[8], refs[9:]
+    half = low.shape[1]
+    parts = near_parts(0, *weights)
+    for i, ref in enumerate((low, high)):
+        parts.append((ref, (slice(None), pl.ds((6 + i) * half, half))))
+    expert_steps(expert_ref, parts, None, x, d, gate, *rest)
+
+
+def second_expert_kernel(expert_ref, x, d, gate, *refs):
+    weights, rest = refs[:7], refs[7:]
+    *rest, send_sems, recv_sems = rest
+    w = rest[3]
+    shard = weights[0].shape[1]
+    half = shard // 2
+    _, _, _, left_gate, left_two, right_gate, right_two = weights
+    place = Place()
+
+    def receive():
+        greet([place.on_line(1), place.on_line(-1)])
+        copies = []
+        for i, (one, two, side) in enumerate(
+            ((left_gate, left_two, 1), (right_gate, right_two, -1))
+        ):
+            cut = pl.ds(i * half, half)
+            there = pl.ds((6 + i) * half, half)
+            copies.append(
+                remote(one.at[cut], w.at[0, there], send_sems.at[2 * i], recv_sems.at[2 * i],
+                       place.on_line(side))
+            )
+            copies.append(
+                remote(two.at[:, cut], w.at[pl.ds(1, 2), there], send_sems.at[2 * i + 1],
+                       recv_sems.at[2 * i + 1], place.on_line(side))
+            )
+        for copy in copies:
+            copy.start()
+        yield
+        for copy in copies:
+            copy.wait()
+
+    expert_steps(expert_ref, near_parts(1, *weights), receive(), x, d, gate, *rest)
 
 
 def first_sums_steps(
@@ -884,24 +983,21 @@
     ]
 
 
-def expert_layer(expert, weights, x, d, gate, other=None, collective_id=None):
+def expert_layer(expert, weights, x, d, gate, collective_id=None):
     bf16 = jnp.bfloat16
     rows, width = x.shape
-    hidden = sum(part.shape[1] for part in weights)
-    half = hidden // 8
-    sending = other is not None
-    more = [shape((3, half, width))] * 2 if sending else []
-    extra = first_sums_scratch(half, width) if sending else []
+    hidden = 4 * weights[0].shape[1]
+    second = collective_id is not None
+    extra = dma_sems(4, 4) if second else []
     return pl.pallas_call(
-        expert_sending_kernel if sending else expert_kernel,
+        second_expert_kernel if second else first_expert_kernel,
         out_shape=(
-            jax.ShapeDtypeStruct((rows, width), bf16),
-            jax.ShapeDtypeStruct((rows, width + 128), bf16),
-            jax.ShapeDtypeStruct((3, hidden, width), bf16),
-            *more,
+            shape((rows, width)),
+            shape((rows, width + 128)),
+            shape((3, hidden, width)),
         ),
-        in_specs=[SMEM] + [ANY] * (9 if sending else 8),
-        out_specs=(ANY,) * (5 if sending else 3),
+        in_specs=[SMEM] + [ANY] * (3 + len(weights)),
+        out_specs=(ANY,) * 3,
         scratch_shapes=[
             pltpu.VMEM((3, hidden, width), bf16),
             pltpu.VMEM((rows, width), bf16),
@@ -914,21 +1010,20 @@
             pltpu.VMEM((rows, width), bf16),
             pltpu.VMEM((rows, width + 128), bf16),
             pltpu.VMEM((rows, 128), jnp.float32),
-            pltpu.VMEM((hidden, rows), bf16),
             pltpu.VMEM((3, hidden, width), bf16),
-            *dma_sems(8, 2, 3),
+            *dma_sems(12, 2, 9),
             *extra,
         ],
         compiler_params=pltpu.CompilerParams(
-            vmem_limit_bytes=60 * 2**20, collective_id=collective_id, has_side_effects=sending
+            vmem_limit_bytes=60 * 2**20, collective_id=collective_id, has_side_effects=second
         ),
         cost_estimate=pl.CostEstimate(
             flops=18 * rows * hidden * width,
             bytes_accessed=12 * hidden * width + 10 * rows * width,
             transcendentals=rows * hidden,
         ),
-        name="expert_sending" if sending else "expert_layer",
-    )(expert, *weights, x, d, gate, *([other] if sending else []))
+        name="second_expert" if second else "first_expert",
+    )(expert, x, d, gate, *weights)
 
 
 def rope_tables(length, head_size):
@@ -1002,6 +1097,7 @@
                 context[pl.ds(part * half, half), here] = mixed.astype(BF16)
                 logs.append(peak + jnp.log(total))
             kept = jnp.where(lane == 16 + h, jnp.concatenate(logs, axis=0), kept)
+        yield
     stats[...] = kept
 
 
@@ -1071,11 +1167,12 @@
 
 def forward_kernel(
     inputs_ref, attn_gain_ref, q_gain_ref, k_gain_ref, cos_ref, sin_ref, mlp_gain_ref, router_ref,
-    picks_ref, w_query_ref, w_key_ref, w_value_ref, w_out_ref,
-    mixed_ref, hidden_ref, state_ref, seq_ref,
+    picks_ref, w_query_ref, w_key_ref, w_value_ref, w_out_ref, gate_w_ref, dout_ref,
+    mixed_ref, hidden_ref, state_ref, left_gate_ref, right_gate_ref, dout_all_ref, seq_ref,
     query_rot_ref, key_rot_ref, values_ref, query_unit_ref, key_unit_ref, stats_ref, context_ref,
     seq, w_query, w_key, w_value, w_out, partial, query_rot, key_rot, values, query_unit, key_unit,
-    stats, context, load_sems, save_sems, gather_send, gather_recv, *scratch,
+    stats, context, load_sems, save_sems, gather_send, gather_recv, gate_send, gate_recv, dout_sem,
+    *scratch,
 ):
     place = Place()
     count, width = inputs_ref.shape
@@ -1095,17 +1192,44 @@
     first_scale = inverse_rms(float_in)
     own = pl.ds(place.x * count, count)
     seq[own] = (float_in * first_scale * attn_gain_ref[...]).astype(BF16)
-    greet([place.on_line(1), place.on_line(-1)])
-    run(line_gather_steps(place, seq, count, (gather_send, gather_recv)))
+    greet(plane_neighbours(place) + [place.on_line(1), place.on_line(-1)])
+    scratch, dout_sems = scratch[:4], scratch[4:]
+    keep = pltpu.make_async_copy(dout_ref, dout_all_ref.at[place.block()], dout_sem.at[0])
+    douts = plane_gather_steps(place, dout_ref, lambda at: dout_all_ref.at[at], dout_sems)
+
+    def gather_until(last):
+        for stage in douts:
+            if stage == last:
+                break
+
+    line = line_gather_steps(place, seq, count, (gather_send, gather_recv))
+    next(line)
+    keep.start()
+    for _ in range(9):
+        next(douts)
+    run(line)
+    gates_sent = [
+        remote(gate_w_ref.at[0], target, gate_send.at[i], gate_recv.at[i], place.on_line(side))
+        for i, (target, side) in enumerate(((left_gate_ref, 1), (right_gate_ref, -1)))
+    ]
+    for copy in gates_sent:
+        copy.start()
     for load in loads:
         load.wait()
-    attend(seq, w_query, w_key, w_value, q_gain_ref, k_gain_ref, cos_ref, sin_ref,
-           query_rot, key_rot, values, query_unit, key_unit, stats, context)
+    heads_done = attend(
+        seq, w_query, w_key, w_value, q_gain_ref, k_gain_ref, cos_ref, sin_ref,
+        query_rot, key_rot, values, query_unit, key_unit, stats, context,
+    )
+    next(heads_done)
+    next(heads_done)
+    gather_until(101)
+    run(heads_done)
     for n in range(0, width, 512):
         here = pl.ds(n, 512)
         partial[:, here] = dot(context[...], w_out[:, here], NN).astype(BF16)
     steps = line_scatter_steps(place, partial, count, scratch)
     next(steps)
+    gather_until(102)
     saves = [
         pltpu.make_async_copy(source, target, save_sems.at[i])
         for i, (source, target) in enumerate(
@@ -1118,6 +1242,8 @@
     ]
     for save in saves:
         save.start()
+    next(steps)
+    run(douts)
     run(steps)
     in_b = scratch[1]
     attended = partial[own].astype(F32) + in_b[0].astype(F32) + in_b[1].astype(F32)
@@ -1139,12 +1265,12 @@
     lane = lax.broadcasted_iota(jnp.int32, (count, 2 * experts), 1)
     extra = jnp.where(lane == 0, picked_total, jnp.where(lane == 1, second_scale, first_scale))
     state_ref[:, 2 * experts :] = extra
-    for save in saves:
-        save.wait()
+    for copy in saves + gates_sent + [keep]:
+        copy.wait()
 
 
 def forward(inputs, attn_gain, q_gain, k_gain, cosine, sine, mlp_gain, router_t, picks,
-            w_query, w_key, w_value, w_out, collective_id):
+            w_query, w_key, w_value, w_out, gate_w, dout, collective_id):
     count, width = inputs.shape
     head = cosine.shape[1]
     length = 4 * count
@@ -1161,17 +1287,20 @@
             shape((count, width + 128)),
             shape((count, width), F32),
             shape((count, 256), F32),
+            *[shape(gate_w.shape[1:])] * 2,
+            shape((32, *dout.shape)),
             *[shape(dims, dtype) for dims, dtype in saved],
         ),
-        in_specs=[VMEM] * 9 + [ANY] * 4,
-        out_specs=(VMEM, VMEM, VMEM, *[ANY] * 8),
+        in_specs=[VMEM] * 9 + [ANY] * 6,
+        out_specs=(VMEM, VMEM, VMEM, *[ANY] * 11),
         scratch_shapes=[
             kept[0],
             *[pltpu.VMEM(w.shape, BF16) for w in (w_query, w_key, w_value, w_out)],
             pltpu.VMEM((length, width), BF16),
             *kept[1:],
-            *dma_sems(4, 8, 4, 4),
+            *dma_sems(4, 8, 4, 4, 2, 2, 1),
             *line_scatter_scratch(count, width),
+            *gather_sems(),
         ],
         compiler_params=pltpu.CompilerParams(
             collective_id=collective_id, has_side_effects=True, vmem_limit_bytes=60 * 2**20
@@ -1179,7 +1308,23 @@
         cost_estimate=pl.CostEstimate(flops=7 * 10**10, bytes_accessed=10**8, transcendentals=0),
         name="forward",
     )(inputs, attn_gain, q_gain, k_gain, cosine, sine, mlp_gain, router_t, picks,
-      w_query, w_key, w_value, w_out)
+      w_query, w_key, w_value, w_out, gate_w, dout)
+
+
+LATE_EVERY = 12
+
+
+def exchange_steps(buffer, inbox, peers, sems):
+    send_sems, recv_sems, base = sems
+    copies = [
+        remote(buffer, inbox.at[base + i], send_sems.at[base + i], recv_sems.at[base + i], device)
+        for i, device in enumerate(peers)
+    ]
+    for copy in copies:
+        copy.start()
+    yield
+    for copy in copies:
+        copy.wait()
 
 
 def backward_kernel(
@@ -1192,8 +1337,8 @@
     grad_rows, seq, w_query, w_key, w_value, w_out,
     query_rot, key_rot, values, query_unit, key_unit, stats, context,
     grad_context, grad_qkv, summed, out_w, qkv_w, gains,
-    late, late_in, router_all, both_sum, load_sems, line_send, line_recv, second_send, second_recv,
-    *scratch,
+    small, small_in, small_out, late, late_in, both_sum, load_sems, line_send, line_recv, small_send,
+    small_recv, second_send, second_recv, *scratch,
 ):
     place = Place()
     count, width = inputs_ref.shape
@@ -1223,6 +1368,58 @@
     line = line_gather_steps(place, grad_rows, count, (line_send, line_recv))
     next(line)
 
+    part = small.shape[1]
+    small[...] = jnp.zeros_like(small)
+    for i in range(4):
+        used = min(part, experts + 1 - i * part)
+        from_router = min(used, experts - i * part)
+        if from_router > 0:
+            small[i, :from_router] = router_grad_ref[i * part : i * part + from_router]
+    at_gain = experts // part
+    small[at_gain, experts - at_gain * part : experts - at_gain * part + 1] = mlp_grad_ref[...]
+
+    def small_total():
+        def send(step, number):
+            return remote(
+                small.at[(place.x + step) % 4], small_in.at[number], small_send.at[number],
+                small_recv.at[number], place.on_line(step),
+            )
+
+        copies = [send(step, i) for i, step in enumerate((1, -1, 2))]
+        for copy in copies:
+            copy.start()
+        yield
+        for copy in copies:
+            copy.wait()
+        mine = small.at[place.x]
+        mine[...] = mine[...] + small_in[0] + small_in[1] + small_in[2]
+        base = 3
+        for axis in ("z", "y", "core"):
+            peers = far[axis]
+            yield from exchange_steps(mine, small_in, peers, (small_send, small_recv, base))
+            total = mine[...]
+            for i in range(len(peers)):
+                total = total + small_in[base + i]
+            mine[...] = total
+            base += len(peers)
+        done = small_out.at[place.x]
+        done[...] = mine[...]
+        copies = [
+            remote(done, done, small_send.at[base + i], small_recv.at[base + i], device)
+            for i, device in enumerate(far["x"])
+        ]
+        for copy in copies:
+            copy.start()
+        yield
+        for i, step in enumerate((-1, 1, 2)):
+            copies[i].wait_send()
+            there = small_out.at[(place.x + step) % 4]
+            remote(
+                there, there, small_send.at[base + i], small_recv.at[base + i], far["x"][0]
+            ).wait_recv()
+
+    smalls = small_total()
+    next(smalls)
     run(line)
 
     half = width // 2
@@ -1257,31 +1454,29 @@
     next(outs)
     sums = first_sums_steps(place, gw_b_ref, sum_left_ref, sum_right_ref, *sums_scratch)
     next(sums)
+    next(smalls)
+    second = second_sends(
+        place, gw_b_ref, sum_left_ref, sum_right_ref, right_b_ref, left_b_ref, second_send, second_recv
+    )
     for load in loads[2:]:
         load.wait()
     back = attend_back(grad_rows, seq, w_query, w_key, w_value, w_out, q_gain_ref, k_gain_ref,
                        cos_ref, sin_ref, query_rot, key_rot, values, query_unit, key_unit, stats,
                        grad_context, grad_qkv, gains)
     gains[...] = jnp.zeros_like(gains)
-    for _ in back:
+    for at, _ in enumerate(back):
         next(outs, None)
+        if at in (4, 9):
+            next(smalls)
     heads = query_rot.shape[1]
-    block_rows = summed.shape[0] // 4
-    part = experts // 4
-    for i in range(4):
-        router = router_grad_ref[pl.ds(i * part, part)]
-        high = router.astype(BF16)
-        summed[pl.ds(i * block_rows + count, part)] = high
-        summed[pl.ds(i * block_rows + count + part, part)] = (router - high.astype(F32)).astype(BF16)
     for n in range(0, width, 512):
         here = pl.ds(n, 512)
         value = dot(grad_qkv[:, :heads], w_query[here], NT)
         value = value + dot(grad_qkv[:, heads : heads + head], w_key[here], NT)
         value = value + dot(grad_qkv[:, heads + head :], w_value[here], NT)
-        for i in range(4):
-            summed[pl.ds(i * block_rows, count), here] = value[i * count : (i + 1) * count].astype(BF16)
+        summed[:, here] = value.astype(BF16)
     line_scatter = scratch
-    line = line_scatter_steps(place, summed, block_rows, line_scatter)
+    line = line_scatter_steps(place, summed, count, line_scatter)
     next(line)
     for n in range(0, grad_qkv.shape[1], 256):
         here = pl.ds(n, 256)
@@ -1302,86 +1497,60 @@
         )
         keep.wait()
 
-    second = second_sends(
-        place, gw_b_ref, sum_left_ref, sum_right_ref, right_b_ref, left_b_ref, second_send, second_recv
-    )
-    for copy in second[:2]:
-        copy.start()
-    run(sums)
-    for copy in second[2:]:
-        copy.start()
     qkvs = qkv_total()
-    next(qkvs)
-    next(line)
-    for _ in range(4):
-        next(qkvs, None)
+    for step in range(15):
+        next(qkvs)
+        if step == 2:
+            next(line)
+        if step == 6:
+            run(sums)
+        if step == 10:
+            next(smalls)
     run(line)
     in_b = line_scatter[1]
-
-    def line_total(start, size):
-        here = pl.ds(start, size)
-        total = summed[pl.ds(place.x * block_rows + start, size)].astype(F32)
-        return total + in_b[0, here].astype(F32) + in_b[1, here].astype(F32)
-
-    grad_normed = line_total(0, count)
-    late[...] = jnp.zeros_like(late)
-    late[:part] = line_total(count, part) + line_total(count + part, part)
+    grad_normed = summed[own].astype(F32) + in_b[0].astype(F32) + in_b[1].astype(F32)
     float_in = inputs_ref[...].astype(F32)
     first_scale = state_ref[:, 2 * experts + 2 : 2 * experts + 3]
     grad_inputs_ref[...] = (
         grad_hidden_ref[...] + norm_back(float_in, first_scale, attn_gain_ref[...], grad_normed)
     ).astype(BF16)
-    late[part : part + 1, :] = jnp.sum(grad_normed * float_in * first_scale, axis=0, keepdims=True)
-    late[part + 1 : part + 2, :head] = gains[0:1, :]
-    late[part + 1 : part + 2, head : 2 * head] = gains[1:2, :]
-    late[part + 2 : part + 3, :] = mlp_grad_ref[...]
+    late[...] = jnp.zeros_like(late)
+    late[0:1, :] = jnp.sum(grad_normed * float_in * first_scale, axis=0, keepdims=True)
+    late[1:2, :head] = gains[0:1, :]
+    late[1:2, head : 2 * head] = gains[1:2, :]
 
     def late_total():
         base = 0
         for axis in ("x", "z", "y", "core"):
             peers = far[axis]
-            span = pl.ds(part, 8) if axis == "x" else pl.ds(0, part + 8)
-            copies = [
-                remote(late.at[span], late_in.at[base + i, span], late_send.at[base + i],
-                       late_recv.at[base + i], device)
-                for i, device in enumerate(peers)
-            ]
-            for copy in copies:
-                copy.start()
-            yield
-            for copy in copies:
-                copy.wait()
-            total = late[span]
+            yield from exchange_steps(late, late_in, peers, (late_send, late_recv, base))
+            total = late[...]
             for i in range(len(peers)):
-                total = total + late_in[base + i, span]
-            late[span] = total
+                total = total + late_in[base + i]
+            late[...] = total
             base += len(peers)
-        router_all[place.x] = late[:part]
-        mine = router_all.at[place.x]
-        copies = [
-            remote(mine, mine, late_send.at[base + i], late_recv.at[base + i], device)
-            for i, device in enumerate(far["x"])
-        ]
-        for copy in copies:
-            copy.start()
-        yield
-        for copy in copies:
-            copy.wait_send()
-        for i, step in enumerate((-1, 1, 2)):
-            there = router_all.at[(place.x + step) % 4]
-            remote(
-                there, there, late_send.at[base + i], late_recv.at[base + i], far["x"][0]
-            ).wait_recv()
 
     lates = late_total()
-    running = [qkvs, lates]
-    while running:
-        for steps in list(running):
-            if next(steps, "end") == "end":
-                running.remove(steps)
-    gains_out_ref[...] = late[part : part + 8]
+    next(lates)
+    for _ in range(4):
+        next(qkvs)
+    next(lates)
+    for copy in second:
+        copy.start()
+    steps_done = 0
+    for _ in qkvs:
+        steps_done += 1
+        if steps_done % LATE_EVERY == 0:
+            next(lates, None)
+    run(lates)
+    run(smalls)
+    gains_out_ref[0:2] = late[0:2]
+    at_row = experts - at_gain * part
+    gains_out_ref[2:3] = small_out[at_gain, at_row : at_row + 1]
     for i in range(4):
-        router_out_ref[i * part : (i + 1) * part] = router_all[i]
+        from_router = min(part, experts - i * part)
+        if from_router > 0:
+            router_out_ref[i * part : i * part + from_router] = small_out[i, :from_router]
     for copy in second:
         copy.wait()
 
@@ -1396,8 +1565,7 @@
     wide = w_query.shape[1]
     total = wide + 2 * head
     experts = router_grad.shape[0]
-    part = experts // 4
-    block_rows = count + 2 * part
+    part = -(-(experts + 1) // 32) * 8
     rows = width // 32
     shard = gw_b.shape[1] // 4
     like = lambda array: pltpu.VMEM(array.shape, array.dtype)
@@ -1419,21 +1587,23 @@
             *[like(a) for a in saved[1:]],
             pltpu.VMEM((length, wide), BF16),
             pltpu.VMEM((length, total), BF16),
-            pltpu.VMEM((4 * block_rows, width), BF16),
+            pltpu.VMEM((length, width), BF16),
             pltpu.VMEM((2 * wide, width // 2), BF16),
             pltpu.VMEM((width, total), BF16),
             pltpu.VMEM((8, head), F32),
-            pltpu.VMEM((part + 8, width), F32),
-            pltpu.VMEM((10, part + 8, width), F32),
             pltpu.VMEM((4, part, width), F32),
+            pltpu.VMEM((10, part, width), F32),
+            pltpu.VMEM((4, part, width), F32),
+            pltpu.VMEM((8, width), F32),
+            pltpu.VMEM((10, 8, width), F32),
             pltpu.VMEM((rows, width // 2 + total), BF16),
-            *dma_sems(12, 4, 4, 4, 4),
+            *dma_sems(12, 4, 4, 13, 13, 4, 4),
             *scatter_scratch(2 * wide // 32, width // 2),
             *scatter_scratch(rows, total),
             *gather_sems(),
-            *dma_sems(13, 13, 1),
+            *dma_sems(10, 10, 1),
             *first_sums_scratch(shard // 2, width),
-            *line_scatter_scratch(block_rows, width),
+            *line_scatter_scratch(count, width),
         ],
         compiler_params=pltpu.CompilerParams(
             collective_id=collective_id, has_side_effects=True, vmem_limit_bytes=62 * 2**20
@@ -1442,6 +1612,72 @@
         name="backward",
     )(grad_att, inputs, attn_gain, q_gain, k_gain, cosine, sine, state, grad_hidden, router_grad,
       mlp_grad, gw_b, seq, w_query, w_key, w_value, w_out, *saved[1:])
+
+
+def attention_grads_kernel(all_ref, out_ref, query_ref, key_ref, value_ref):
+    value = all_ref[...].astype(F32)
+    at = 0
+    for ref in (out_ref, query_ref, key_ref, value_ref):
+        ref[...] = value[:, at : at + ref.shape[1]]
+        at += ref.shape[1]
+
+
+def attention_grads(total, wide, narrow):
+    rows, full = total.shape
+    half = full - wide - 2 * narrow
+    step = 128
+    steps = rows // step
+    cut = wide // step
+    return pl.pallas_call(
+        attention_grads_kernel,
+        grid=(steps,),
+        out_shape=(
+            shape((wide, half * steps // cut), F32), shape((rows, wide), F32),
+            shape((rows, narrow), F32), shape((rows, narrow), F32),
+        ),
+        in_specs=[pl.BlockSpec((step, full), lambda i: (i, 0))],
+        out_specs=(
+            pl.BlockSpec((step, half), lambda i: (i % cut, i // cut)),
+            pl.BlockSpec((step, wide), lambda i: (i, 0)),
+            pl.BlockSpec((step, narrow), lambda i: (i, 0)),
+            pl.BlockSpec((step, narrow), lambda i: (i, 0)),
+        ),
+        compiler_params=pltpu.CompilerParams(vmem_limit_bytes=32 * 2**20),
+        name="attention_grads",
+    )(total)
+
+
+def expert_grads_kernel(own_a, right_a, left_a, own_b, right_b, left_b, *outs):
+    step = pl.program_id(0)
+
+    def add(own, right, left):
+        for i, out in enumerate(outs):
+            value = own[i].astype(F32) + right[i].astype(F32)
+            out[0] = value + left[i].astype(F32)
+
+    @pl.when(step < 2)
+    def _():
+        add(own_a, right_a, left_a)
+
+    @pl.when(step >= 2)
+    def _():
+        add(own_b, right_b, left_b)
+
+
+def expert_grads(first, second):
+    _, shard, width = first[1].shape
+    half = shard // 2
+    early = pl.BlockSpec((3, half, width), lambda i: (0, jnp.minimum(i, 1), 0))
+    late = pl.BlockSpec((3, half, width), lambda i: (0, jnp.maximum(i - 2, 0), 0))
+    return pl.pallas_call(
+        expert_grads_kernel,
+        grid=(4,),
+        out_shape=(shape((2, shard, width), F32),) * 3,
+        in_specs=[early] * 3 + [late] * 3,
+        out_specs=(pl.BlockSpec((1, half, width), lambda i: (i // 2, i % 2, 0)),) * 3,
+        compiler_params=pltpu.CompilerParams(vmem_limit_bytes=48 * 2**20),
+        name="expert_grads",
+    )(*first, *second)
 
 
 def along_line(value, step):
@@ -1478,40 +1714,39 @@
     base = 20 * ((place // 4) % 2 * 2 + place % 2)
     slots = jnp.where(picks > 0.0, rank + base.astype(F32), -1.0)
     slots = jnp.concatenate([slots, jnp.full_like(slots, -1.0)], axis=1).astype(BF16)
-    dout_all = lax.all_gather(jnp.concatenate([grad_out, slots], axis=1), "expert", axis=0)
+    dout = jnp.concatenate([grad_out, slots], axis=1)
 
     gate_t = jnp.swapaxes(w_gate, 1, 2)
     up_t = jnp.swapaxes(w_up, 1, 2)
-    own = [jnp.stack([gate_t[j], up_t[j], w_down[j]]) for j in range(2)]
-    half = own[0].shape[1] // 2
     cosine, sine = rope_tables(4 * row_count, head_size)
     router_t = w_router.T
     q_gain, k_gain = q_gain[None], k_gain[None]
     attn_gain, mlp_gain = attn_gain[None], mlp_gain[None]
-    left_a, right_a = along_line(own[0], 1), along_line(own[0], -1)
-    mixed, hidden, state, *saved = forward(
+    mixed, hidden, state, left_a, right_a, dout_all, *saved = forward(
         inputs, attn_gain, q_gain, k_gain, cosine, sine, mlp_gain, router_t, picks,
-        w_query, w_key, w_value, w_out, 0,
-    )
-
-    mixed, left_a, right_a, own[1] = lax.optimization_barrier((mixed, left_a, right_a, own[1]))
-    low_a, high_a = along_line(left_a[:, :half], 1), along_line(right_a[:, half:], -1)
-    left_b, right_b = along_line(own[1], 1), along_line(own[1], -1)
-    grad_a, grad_b, rows_a, rows_b, gate_a, gate_b = gather_select(mixed, dout_all, 1)
-    rows_a, left_b, right_b, low_a, high_a = lax.optimization_barrier(
-        (rows_a, left_b, right_b, low_a, high_a)
-    )
-    low_b, high_b = along_line(left_b[:, :half], 1), along_line(right_b[:, half:], -1)
+        w_query, w_key, w_value, w_out, gate_t, dout, 0,
+    )
+
+    left_two_a, right_two_a, low_a, high_a, left_b, right_b, _, *rows = gather_select(
+        mixed, dout_all, gate_t, up_t, w_down, left_a, right_a, 1
+    )
+    grad_a, grad_b, rows_a, rows_b, gate_a, gate_b = rows
+    own_two, rows_a = lax.optimization_barrier((jnp.stack([up_t[1], w_down[1]]), rows_a))
+    left_two_b, right_two_b = along_line(own_two, 1), along_line(own_two, -1)
+    shards = (gate_t, up_t, w_down)
     out_a, back_a, gw_a = expert_layer(
-        first, (own[0], left_a, right_a, low_a, high_a), rows_a, grad_a, gate_a
-    )
-    rows_b, back_a = lax.optimization_barrier((rows_b, back_a))
-    out_b, back_b, gw_b, sum_left_a, sum_right_a = expert_layer(
-        first + 1, (own[1], left_b, right_b, low_b, high_b), rows_b, grad_b, gate_b, gw_a, 4
-    )
-    shares, right_a, left_a, grad_hidden, grad_att, router_grad, mlp_grad = combine_scatter(
-        (back_a, back_b), (out_a, out_b), dout_all, (gw_a, sum_left_a, sum_right_a), grad_out,
-        hidden, mixed, state, picks, mlp_gain, router_t, 2,
+        first, (*shards, left_a, left_two_a, right_a, right_two_a, low_a, high_a),
+        rows_a, grad_a, gate_a,
+    )
+    rows_b, back_a, left_two_b, right_two_b = lax.optimization_barrier(
+        (rows_b, back_a, left_two_b, right_two_b)
+    )
+    out_b, back_b, gw_b = expert_layer(
+        first + 1, (*shards, left_b, left_two_b, right_b, right_two_b), rows_b, grad_b, gate_b, 4
+    )
+    shares, right_a, left_a, _, _, grad_hidden, grad_att, router_grad, mlp_grad = combine_scatter(
+        (back_a, back_b), (out_a, out_b), dout_all, gw_a, grad_out, hidden, mixed, state, picks,
+        mlp_gain, router_t, 2,
     )
     expert_mix = lax.psum_scatter(
         shares.reshape(-1, model_width), "expert", scatter_dimension=0, tiled=True
@@ -1523,20 +1758,8 @@
         router_grad, mlp_grad, gw_b, (w_query, w_key, w_value, w_out), saved, 3,
     )
     grad_inputs, router_grad, gains, all_w, right_b, left_b, _, _ = results
-    wide, narrow = w_query.shape[1], w_key.shape[1]
-    start = model_width // 2
-    out_w = jnp.concatenate([all_w[:wide, :start], all_w[wide:, :start]], axis=1).astype(F32)
-    query_w = all_w[:, start : start + wide].astype(F32)
-    key_w = all_w[:, start + wide : start + wide + narrow].astype(F32)
-    value_w = all_w[:, start + wide + narrow :].astype(F32)
-
-    def line_total(i):
-        shard = w_down.shape[1]
-        return jnp.stack([
-            gw[i, :shard].astype(F32) + right[i].astype(F32) + left[i].astype(F32)
-            for gw, right, left in ((gw_a, right_a, left_a), (gw_b, right_b, left_b))
-        ])
-
+    out_w, query_w, key_w, value_w = attention_grads(all_w, w_query.shape[1], w_key.shape[1])
+    gate_w, up_w, down_w = expert_grads((gw_a, right_a, left_a), (gw_b, right_b, left_b))
     return (
         output,
         grad_inputs,
@@ -1549,9 +1772,9 @@
         out_w,
         gains[2],
         router_grad.T,
-        jnp.swapaxes(line_total(0), 1, 2),
-        jnp.swapaxes(line_total(1), 1, 2),
-        line_total(2),
+        jnp.swapaxes(gate_w, 1, 2),
+        jnp.swapaxes(up_w, 1, 2),
+        down_w,
     )
 
 

time: 594 us -> 547 us (0.921)
  other arithmetic: 34 us -> 5.69 us
  Pallas kernels: 516 us -> 501 us
  starting transfers between devices: 9.8 us -> 1.8 us
    pallas_call x3 -> x5, Pallas kernels: 132 us -> 171 us  [the longest x1 81.8 us: gather_select(): pl.pallas_call(gather_select_kernel, out_shape=(two, two, far, far, one,...]
    pallas_call x1, Pallas kernels: 115 us -> 78.4 us  [forward(): pl.pallas_call(forward_kernel, out_shape=(shape((count, width + 128)), sh...]
    pallas_call x1, Pallas kernels: 202 us -> 169 us  [backward(): pl.pallas_call(backward_kernel, out_shape=(shape((count, width)), shape((...]
    pallas_call x1, Pallas kernels: 66.1 us -> 83.1 us  [combine_scatter(): pl.pallas_call(combine_scatter_kernel, out_shape=(shape((32, count, width...]
    convert_element_type x3 -> x0, other arithmetic: 10.5 us -> none  [the longest x1 4.57 us: per_device(): query_w = all_w[:, start:start + wide].astype(F32)]
    ppermute x8 -> x2, starting transfers between devices: 9.72 us -> 1.76 us  [along_line(): lax.ppermute(value, 'tensor', [(i, (i + step) % 4) for i in range(4)])]
    add x2 -> x0, other arithmetic: 7.72 us -> none  [line_total(): gw[i, :shard].astype(F32) + right[i].astype(F32) + left[i].astype(F32)]
    slice x7 -> x3, local copies, waits for them, and re-layouts: 8.73 us -> 1.27 us  [the longest x1 1.26 us: per_device(): up_t[1]]
  transfers between devices with their start and end apart: 10 -> 3, of which waited for: 0 -> 2; matrix products, arithmetic and copies ran while one was open for 6% -> 1% of each run, Pallas kernels for 71% -> 40%
where the time goes in v3:
time: 547 us; the launch traced here: 538 us
  Pallas kernels  501 us (92%)
  between operations  14.5 us (3%)
  local copies, waits for them, and re-layouts  9.46 us (2%)
  other arithmetic  5.69 us (1%)
    pallas_call x1, Pallas kernels, backward(): pl.pallas_call(backward_kernel, out_shape=(shape((count, width)), shape((...  169 us
    pallas_call x1, Pallas kernels, combine_scatter(): pl.pallas_call(combine_scatter_kernel, out_shape=(shape((32, count, width...  83.1 us
    pallas_call x1, Pallas kernels, gather_select(): pl.pallas_call(gather_select_kernel, out_shape=(two, two, far, far, one,...  81.8 us
    pallas_call x1, Pallas kernels, forward(): pl.pallas_call(forward_kernel, out_shape=(shape((count, width + 128)), sh...  78.4 us
    pallas_call x2, Pallas kernels, expert_layer(): pl.pallas_call(second_expert_kernel if second else first_expert_kernel, o...  71 us
  transfers between devices with their start and end apart: 3, of which 2 were waited for; matrix products, arithmetic and copies ran while one was open for 1% of the time, Pallas kernels for 40%

profile of v3, /device:TPU:1, one launch (start us, length us, event | category | flops | bytes accessed | tf_op | source)
XLA Modules:
  0.0 537.6 jit_solution(3529863430496179559)
XLA Ops:
  7.2 0.0 copy-start.4
  7.2 0.0 reduce-scatter.2.cloned.1.call-start
  7.3 0.8 convert_reduce_fusion
  8.1 0.1 copy.33.picks_ref
  8.2 0.0 copy-start.7
  8.2 1.0 fusion.6
  9.2 0.0 slice-start
  9.2 1.3 slice.24
  10.4 0.1 fusion.1
  10.6 0.0 copy-done.4
  10.6 0.8 fusion.3.dout_ref
  11.4 0.0 copy-done.7
  11.4 0.0 slice-done
  11.5 0.1 pad_maximum_fusion
  11.6 1.0 pad_maximum_fusion.1
  12.6 78.4 %forward.1 = (bf16[128,2176]{1,0:T(8,128)(2,1)}, f32[128,2048]{1,0:T(8,128)}, f32[128,256]{1,0:T(8,128)}, bf16[192,2048]{1,0:T(8,128)(2,1)}, bf16[192,2048]{1,0:...) custom-call(bf16[128,2048]{1,0:T(8,128)(2,1)} %inputs_ref.3, ...), custom_call_target="tpu_custom_call" | custom-call | flops 70000001024 | bytes 100000000 | tf_op jit(solution)/shard_map/forward/pallas_call | solution.py:1284
  91.0 81.8 %gather_select.1 = (bf16[2,192,2048]{2,1,0:T(8,128)(2,1)}, bf16[2,192,2048]{2,1,0:T(8,128)(2,1)}, bf16[3,96,2048]{2,1,0:T(8,128)(2,1)}, bf16[3,96,2048]{2,1,0:T(...) custom-call(bf16[128,2176]{1,0:T(8,128)(2,1)} %get-tuple-element.73., ...), custom_call_target="tpu_custom_call" | custom-call | flops 60000002048 | bytes 100000000 | tf_op jit(solution)/shard_map/gather_select/pallas_call | solution.py:580
  172.8 1.8 collective-permute-start.1
  174.5 0.0 collective-permute-start
  174.5 30.9 %first_expert.1 = (bf16[640,2048]{1,0:T(8,128)(2,1)}, bf16[640,2176]{1,0:T(8,128)(2,1)}, bf16[3,768,2048]{2,1,0:T(8,128)(2,1)}) custom-call(s32[1]{0:T(128)} %bitcast.7.expert_ref, bf16[640,2048]{1,0:T(8,128)(2,1)} %get-tuple-element.79.x, bf16[640,2048]{1,0:T(8,128)(2,1)} %get-tuple-element.80.d, f32[640,128]{1,0:T(8,128)} %get-tuple-element.81.gate, ...), custom_call_target="tpu_custom_call" | custom-call | flops 18119393280 | bytes 31981568 | tf_op jit(solution)/shard_map/first_expert/pallas_call | solution.py:992
  205.5 2.1 collective-permute-done.1.refs_6_
  207.6 3.1 collective-permute-done.refs_4_
  210.7 40.1 %second_expert.1 = (bf16[640,2048]{1,0:T(8,128)(2,1)}, bf16[640,2176]{1,0:T(8,128)(2,1)}, bf16[3,768,2048]{2,1,0:T(8,128)(2,1)}) custom-call(s32[1]{0:T(128)S(6)} %add.32.expert_ref, bf16[640,2048]{1,0:T(8,128)(2,1)} %get-tuple-element.89.x, bf16[640,2048]{1,0:T(8,128)(2,1)} %get-tuple-element.90.d, f32[640,128]{1,0:T(8,128)} %get-tuple-element.91.gate, ...), custom_call_target="tpu_custom_call" | custom-call | flops 18119393280 | bytes 31981568 | tf_op jit(solution)/shard_map/second_expert/pallas_call | solution.py:992
  250.8 83.1 %combine_scatter.1 = (bf16[32,128,2048]{2,1,0:T(8,128)(2,1)}, bf16[3,192,2048]{2,1,0:T(8,128)(2,1)}, bf16[3,192,2048]{2,1,0:T(8,128)(2,1)}, bf16[3,96,2048]{2,1,...) custom-call(bf16[640,2176]{1,0:T(8,128)(2,1)} %get-tuple-element.88., ...), custom_call_target="tpu_custom_call" | custom-call | flops 60000002048 | bytes 100000000 | tf_op jit(solution)/shard_map/combine_scatter/pallas_call | solution.py:754
  334.0 0.0 reduce-scatter.2.cloned.1.call-update
  334.0 168.8 %backward.1 = (bf16[128,2048]{1,0:T(8,128)(2,1)}, f32[64,2048]{1,0:T(8,128)}, f32[8,2048]{1,0:T(8,128)}, bf16[2048,2304]{1,0:T(8,128)(2,1)}, bf16[3,192,2048]{2,...) custom-call(bf16[128,2048]{1,0:T(8,128)(2,1)} %get-tuple-element.102.gr, ...), custom_call_target="tpu_custom_call" | custom-call | flops 99999997952 | bytes 100000000 | tf_op jit(solution)/shard_map/backward/pallas_call | solution.py:1572
  502.7 0.0 copy-start
  502.8 3.7 copy-done
  506.4 0.0 copy-start.1
  506.4 0.0 copy-start.2
  506.4 8.7 %attention_grads.1 = (f32[1024,2048]{1,0:T(8,128)}, f32[2048,1024]{1,0:T(8,128)}, f32[2048,128]{1,0:T(8,128)}, f32[2048,128]{1,0:T(8,128)}) custom-call(bf16[2048,2304]{1,0:T(8,128)(2,1)S(1)} %copy-done), custom_call_target="tpu_custom_call" | custom-call | tf_op jit(solution)/shard_map/attention_grads/pallas_call | solution.py:1631
  515.2 0.0 copy-done.1
  515.2 0.0 copy-done.2
  515.2 0.0 copy-start.3
  515.2 9.0 %expert_grads.1 = (f32[2,192,2048]{2,1,0:T(8,128)}, f32[2,192,2048]{2,1,0:T(8,128)}, f32[2,192,2048]{2,1,0:T(8,128)}) custom-call(bf16[3,768,2048]{2,1,0:T(8,128)(2,1)} %get-tuple-element.99.gw_ref.own_a, bf16[3,192,2048]{2,1,0:T(8,128)(2,1)S(1)} %copy-done.1, bf16[3,192,2048]{2,1,0:T(8,128)(2,1)S(1)} %copy-done.2, ...), custom_call_target="tpu_custom_call" | custom-call | tf_op jit(solution)/shard_map/expert_grads/pallas_call | solution.py:1672
  524.2 0.0 copy-start.6
  524.2 0.0 copy-start.5
  524.2 1.3 slice_bitcast_fusion
  525.5 1.5 fusion.8
  527.0 0.0 reduce-scatter.2.cloned.1.call-done
  527.0 0.0 copy-done.3
  527.0 1.9 add_convert_fusion
  529.0 0.0 copy-done.6
  529.0 0.8 copy.38
  529.8 0.0 copy-done.5
  529.8 0.8 copy.39
  (1 shorter events, 0.0 us)
Async XLA Ops:
  7.2 3.4 copy-start.4
  7.2 519.8 %reduce-scatter.2.cloned.1.call-start = ((), (), s32[]{:S(2)}) async-start(), calls=%async_computation.1 | async-start | bytes 17301504 | tf_op jit(solution)/shard_map/reduce_scatter | solution.py:1751
  8.2 3.3 copy-start.7
  9.2 2.3 slice-start
  172.8 34.8 %collective-permute-start.1 = (bf16[2,192,2048]{2,1,0:T(8,128)(2,1)S(1)}, bf16[2,192,2048]{2,1,0:T(8,128)(2,1)}, u32[]{:S(2)}, u32[]{:S(2)}) collective-permute-start(bf16[2,192,2048]{2,1,0:T(8,128)(2,1)S(1)} %pad_maximum_fusion), channel_id=1, source_target_pairs={{0,3},{1,0},{2,1},{3,2},{4,7},{5,4},{6,5},{7,6},{8,11},{9,8},{10,9... | collective-permute-start | bytes 4718600 | tf_op jit(solution)/shard_map/ppermute | solution.py:1684
  174.5 36.2 %collective-permute-start = (bf16[2,192,2048]{2,1,0:T(8,128)(2,1)S(1)}, bf16[2,192,2048]{2,1,0:T(8,128)(2,1)}, u32[]{:S(2)}, u32[]{:S(2)}) collective-permute-start(bf16[2,192,2048]{2,1,0:T(8,128)(2,1)S(1)} %pad_maximum_fusion), channel_id=1, source_target_pairs={{0,1},{1,2},{2,3},{3,0},{4,5},{5,6},{6,7},{7,4},{8,9},{9,10},{10,1... | collective-permute-start | bytes 4718600 | tf_op jit(solution)/shard_map/ppermute | solution.py:1684
  502.7 3.7 copy-start
  506.4 8.7 %copy-start.1 = (bf16[3,192,2048]{2,1,0:T(8,128)(2,1)S(1)}, bf16[3,192,2048]{2,1,0:T(8,128)(2,1)}, u32[]{:S(2)}) copy-start(bf16[3,192,2048]{2,1,0:T(8,128)(2,1)} %get-tuple-element.123.right_a) | copy-start | bytes 7077892
  506.4 8.7 %copy-start.2 = (bf16[3,192,2048]{2,1,0:T(8,128)(2,1)S(1)}, bf16[3,192,2048]{2,1,0:T(8,128)(2,1)}, u32[]{:S(2)}) copy-start(bf16[3,192,2048]{2,1,0:T(8,128)(2,1)} %get-tuple-element.124.left_a) | copy-start | bytes 7077892
  515.2 11.9 %copy-start.3 = (f32[128,2048]{1,0:T(8,128)S(1)}, f32[128,2048]{1,0:T(8,128)}, u32[]{:S(2)}) copy-start(f32[128,2048]{1,0:T(8,128)} %get-tuple-element.72.hidden_ref) | copy-start | bytes 3145732
  524.2 4.8 copy-start.6
  524.2 5.6 %copy-start.5 = (f32[64,2048]{1,0:T(8,128)S(1)}, f32[64,2048]{1,0:T(8,128)}, u32[]{:S(2)}) copy-start(f32[64,2048]{1,0:T(8,128)} %get-tuple-element.122) | copy-start | bytes 1572868
Sparse Core Ops, SparseCore 0:
  334.1 140.9 reduce-scatter.1

commit v4 on v3

--- a/solution.py
+++ b/solution.py
@@ -603,7 +603,8 @@
 def combine_scatter_kernel(
     back_a_ref, back_b_ref, out_a_ref, out_b_ref, slots_ref, gw_ref,
     grad_out_ref, hidden_ref, mixed_ref, state_ref, picks_ref, mlp_gain_ref, router_ref,
-    shares_ref, from_right_ref, from_left_ref, sum_left_ref, sum_right_ref,
+    shares_ref, right_low_ref, left_high_ref, right_last_ref, left_last_ref, sum_left_ref,
+    sum_right_ref,
     grad_hidden_ref, grad_att_ref, grad_router_ref, gain_ref,
     rows, slots, blocks, out_rows, share, total, load_sems, row_sems, share_sems,
     line_send, line_recv, *scratch,
@@ -624,10 +625,16 @@
                 load_sems.at[16 + 2 * number + j],
             ).start()
     greet(plane_neighbours(place) + [place.on_line(1), place.on_line(-1)])
-    line = second_sends(
-        place, gw_ref, sum_left_ref, sum_right_ref, from_right_ref, from_left_ref, line_send,
-        line_recv,
-    )
+    line = raw_sends(
+        place, gw_ref, pl.ds(2, 1), right_last_ref, left_last_ref,
+        [line_send.at[0], line_send.at[1]], [line_recv.at[0], line_recv.at[1]],
+    )
+    for i, (source, target, side) in enumerate(
+        ((sum_left_ref, right_low_ref, -1), (sum_right_ref, left_high_ref, 1))
+    ):
+        line.append(
+            remote(source, target, line_send.at[2 + i], line_recv.at[2 + i], place.on_line(side))
+        )
     sums = first_sums_steps(place, gw_ref, sum_left_ref, sum_right_ref, *scratch[:6])
     scratch = scratch[6:]
     next(sums)
@@ -755,7 +762,8 @@
         combine_scatter_kernel,
         out_shape=(
             shape((32, count, width)),
-            *[shape((3, gw.shape[1] // 4, width))] * 2,
+            *[shape((3, gw.shape[1] // 8, width))] * 2,
+            *[shape((1, gw.shape[1] // 8, width))] * 2,
             *[shape((3, gw.shape[1] // 8, width))] * 2,
             shape((count, width), F32),
             shape((count, width)),
@@ -763,7 +771,7 @@
             shape((1, width), F32),
         ),
         in_specs=[ANY] * 6 + [VMEM] * 7,
-        out_specs=(ANY, ANY, ANY, ANY, ANY, VMEM, VMEM, VMEM, VMEM),
+        out_specs=(ANY, ANY, ANY, ANY, ANY, ANY, ANY, VMEM, VMEM, VMEM, VMEM),
         scratch_shapes=[
             pltpu.VMEM((groups, 2, SLOTS, width + 128), BF16),
             pltpu.VMEM((groups, 4, count, 128), BF16),
@@ -843,7 +851,7 @@
     if receive is not None:
         for c in chunks[:-1]:
             weight_chunk(c)
-        run(receive)
+        next(receive)
     hidden_chunk(chunks[-1])
     dots[...] = jnp.zeros_like(dots)
 
@@ -868,6 +876,8 @@
     outs[-1].start()
     for c in chunks[-1:] if receive is not None else chunks:
         weight_chunk(c)
+    if receive is not None:
+        run(receive)
     for out in outs:
         out.wait()
 
@@ -892,8 +902,10 @@
 
 
 def second_expert_kernel(expert_ref, x, d, gate, *refs):
-    weights, rest = refs[:7], refs[7:]
+    weights, other, rest = refs[:7], refs[7], refs[8:]
     *rest, send_sems, recv_sems = rest
+    raw_right, raw_left = rest[3:5]
+    rest = rest[:3] + rest[5:]
     w = rest[3]
     shard = weights[0].shape[1]
     half = shard // 2
@@ -921,6 +933,15 @@
         yield
         for copy in copies:
             copy.wait()
+        sends = raw_sends(
+            place, other, pl.ds(0, 2), raw_right, raw_left,
+            [send_sems.at[4], send_sems.at[5]], [recv_sems.at[4], recv_sems.at[5]],
+        )
+        for copy in sends:
+            copy.start()
+        yield
+        for copy in sends:
+            copy.wait()
 
     expert_steps(expert_ref, near_parts(1, *weights), receive(), x, d, gate, *rest)
 
@@ -967,6 +988,18 @@
     ]
 
 
+def raw_sends(place, gw_hbm, which, raw_right, raw_left, send_sems, recv_sems):
+    shard = gw_hbm.shape[1] // 4
+    half = shard // 2
+    return [
+        remote(gw_hbm.at[which, pl.ds(start, half)], target, send_sems[i], recv_sems[i],
+               place.on_line(side))
+        for i, (start, target, side) in enumerate(
+            ((shard + half, raw_right, -1), (2 * shard, raw_left, 1))
+        )
+    ]
+
+
 def second_sends(place, gw_hbm, sum_left, sum_right, from_right, from_left, send_sems, recv_sems):
     shard = gw_hbm.shape[1] // 4
     half = shard // 2
@@ -983,21 +1016,24 @@
     ]
 
 
-def expert_layer(expert, weights, x, d, gate, collective_id=None):
+def expert_layer(expert, weights, x, d, gate, other=None, collective_id=None):
     bf16 = jnp.bfloat16
     rows, width = x.shape
     hidden = 4 * weights[0].shape[1]
     second = collective_id is not None
-    extra = dma_sems(4, 4) if second else []
+    extra = dma_sems(6, 6) if second else []
+    raw = [shape((2, hidden // 8, width))] * 2 if second else []
+    more = [other] if second else []
     return pl.pallas_call(
         second_expert_kernel if second else first_expert_kernel,
         out_shape=(
             shape((rows, width)),
             shape((rows, width + 128)),
             shape((3, hidden, width)),
+            *raw,
         ),
-        in_specs=[SMEM] + [ANY] * (3 + len(weights)),
-        out_specs=(ANY,) * 3,
+        in_specs=[SMEM] + [ANY] * (3 + len(weights) + len(more)),
+        out_specs=(ANY,) * (3 + len(raw)),
         scratch_shapes=[
             pltpu.VMEM((3, hidden, width), bf16),
             pltpu.VMEM((rows, width), bf16),
@@ -1023,7 +1059,7 @@
             transcendentals=rows * hidden,
         ),
         name="second_expert" if second else "first_expert",
-    )(expert, x, d, gate, *weights)
+    )(expert, x, d, gate, *weights, *more)
 
 
 def rope_tables(length, head_size):
@@ -1468,6 +1504,9 @@
         next(outs, None)
         if at in (4, 9):
             next(smalls)
+        if at == 9:
+            for copy in second[:2]:
+                copy.start()
     heads = query_rot.shape[1]
     for n in range(0, width, 512):
         here = pl.ds(n, 512)
@@ -1500,10 +1539,10 @@
     qkvs = qkv_total()
     for step in range(15):
         next(qkvs)
-        if step == 2:
+        if step == 4:
+            run(sums)
+        if step == 7:
             next(line)
-        if step == 6:
-            run(sums)
         if step == 10:
             next(smalls)
     run(line)
@@ -1535,7 +1574,7 @@
     for _ in range(4):
         next(qkvs)
     next(lates)
-    for copy in second:
+    for copy in second[2:]:
         copy.start()
     steps_done = 0
     for _ in qkvs:
@@ -1647,17 +1686,23 @@
     )(total)
 
 
-def expert_grads_kernel(own_a, right_a, left_a, own_b, right_b, left_b, *outs):
+def expert_grads_kernel(
+    own_a, right_low, left_high, raw_right, raw_left, right_last, left_last,
+    own_b, right_b, left_b, *outs,
+):
     step = pl.program_id(0)
 
     def add(own, right, left):
         for i, out in enumerate(outs):
-            value = own[i].astype(F32) + right[i].astype(F32)
-            out[0] = value + left[i].astype(F32)
-
-    @pl.when(step < 2)
+            out[0] = own[i].astype(F32) + right[i].astype(F32) + left[i].astype(F32)
+
+    @pl.when(step == 0)
     def _():
-        add(own_a, right_a, left_a)
+        add(own_a, right_low, [raw_left[0], raw_left[1], left_last[0]])
+
+    @pl.when(step == 1)
+    def _():
+        add(own_a, [raw_right[0], raw_right[1], right_last[0]], left_high)
 
     @pl.when(step >= 2)
     def _():
@@ -1665,15 +1710,16 @@
 
 
 def expert_grads(first, second):
-    _, shard, width = first[1].shape
+    _, shard, width = second[1].shape
     half = shard // 2
     early = pl.BlockSpec((3, half, width), lambda i: (0, jnp.minimum(i, 1), 0))
     late = pl.BlockSpec((3, half, width), lambda i: (0, jnp.maximum(i - 2, 0), 0))
+    whole = [pl.BlockSpec(part.shape, lambda i: (0, 0, 0)) for part in first[1:]]
     return pl.pallas_call(
         expert_grads_kernel,
         grid=(4,),
         out_shape=(shape((2, shard, width), F32),) * 3,
-        in_specs=[early] * 3 + [late] * 3,
+        in_specs=[early, *whole] + [late] * 3,
         out_specs=(pl.BlockSpec((1, half, width), lambda i: (i // 2, i % 2, 0)),) * 3,
         compiler_params=pltpu.CompilerParams(vmem_limit_bytes=48 * 2**20),
         name="expert_grads",
@@ -1741,13 +1787,15 @@
     rows_b, back_a, left_two_b, right_two_b = lax.optimization_barrier(
         (rows_b, back_a, left_two_b, right_two_b)
     )
-    out_b, back_b, gw_b = expert_layer(
-        first + 1, (*shards, left_b, left_two_b, right_b, right_two_b), rows_b, grad_b, gate_b, 4
-    )
-    shares, right_a, left_a, _, _, grad_hidden, grad_att, router_grad, mlp_grad = combine_scatter(
+    out_b, back_b, gw_b, raw_right, raw_left = expert_layer(
+        first + 1, (*shards, left_b, left_two_b, right_b, right_two_b), rows_b, grad_b, gate_b,
+        gw_a, 4,
+    )
+    shares, right_low, left_high, right_last, left_last, _, _, *results = combine_scatter(
         (back_a, back_b), (out_a, out_b), dout_all, gw_a, grad_out, hidden, mixed, state, picks,
         mlp_gain, router_t, 2,
     )
+    grad_hidden, grad_att, router_grad, mlp_grad = results
     expert_mix = lax.psum_scatter(
         shares.reshape(-1, model_width), "expert", scatter_dimension=0, tiled=True
     )
@@ -1759,7 +1807,10 @@
     )
     grad_inputs, router_grad, gains, all_w, right_b, left_b, _, _ = results
     out_w, query_w, key_w, value_w = attention_grads(all_w, w_query.shape[1], w_key.shape[1])
-    gate_w, up_w, down_w = expert_grads((gw_a, right_a, left_a), (gw_b, right_b, left_b))
+    gate_w, up_w, down_w = expert_grads(
+        (gw_a, right_low, left_high, raw_right, raw_left, right_last, left_last),
+        (gw_b, right_b, left_b),
+    )
     return (
         output,
         grad_inputs,

time: 547 us -> 527 us (0.963)
  Pallas kernels: 501 us -> 481 us
    pallas_call x1, Pallas kernels: 83.1 us -> 68.3 us  [combine_scatter(): pl.pallas_call(combine_scatter_kernel, out_shape=(shape((32, count, width...]
    pallas_call x1, Pallas kernels: 169 us -> 160 us  [backward(): pl.pallas_call(backward_kernel, out_shape=(shape((count, width)), shape((...]
where the time goes in v4:
time: 527 us; the launch traced here: 518 us
  Pallas kernels  481 us (91%)
  between operations  14.5 us (3%)
  local copies, waits for them, and re-layouts  9.48 us (2%)
  other arithmetic  5.71 us (1%)
  waiting for transfers between devices  5.63 us (1%)
    pallas_call x1, Pallas kernels, backward(): pl.pallas_call(backward_kernel, out_shape=(shape((count, width)), shape((...  160 us
    pallas_call x1, Pallas kernels, gather_select(): pl.pallas_call(gather_select_kernel, out_shape=(two, two, far, far, one,...  81.8 us
    pallas_call x1, Pallas kernels, forward(): pl.pallas_call(forward_kernel, out_shape=(shape((count, width + 128)), sh...  78.3 us
    pallas_call x2, Pallas kernels, expert_layer(): pl.pallas_call(second_expert_kernel if second else first_expert_kernel, o...  74.9 us
    pallas_call x1, Pallas kernels, combine_scatter(): pl.pallas_call(combine_scatter_kernel, out_shape=(shape((32, count, width...  68.3 us
  transfers between devices with their start and end apart: 3, of which 2 were waited for; matrix products, arithmetic and copies ran while one was open for 1% of the time, Pallas kernels for 40%

profile of v4, /device:TPU:1, one launch (start us, length us, event | category | flops | bytes accessed | tf_op | source)
XLA Modules:
  0.0 518.5 jit_solution(4299834905399189639)
XLA Ops:
  7.2 0.0 reduce-scatter.2.cloned.1.call-start
  7.3 0.0 copy-start.8
  7.3 0.8 convert_reduce_fusion
  8.1 0.1 copy.33.picks_ref
  8.2 0.0 copy-start.11
  8.2 1.0 fusion.6
  9.2 0.0 slice-start
  9.2 1.3 slice.24
  10.5 0.1 fusion.1
  10.6 0.0 copy-done.8
  10.6 0.8 fusion.3.dout_ref
  11.5 0.0 copy-done.11
  11.5 0.0 slice-done
  11.5 0.1 pad_maximum_fusion
  11.6 1.0 pad_maximum_fusion.1
  12.6 78.3 %forward.1 = (bf16[128,2176]{1,0:T(8,128)(2,1)}, f32[128,2048]{1,0:T(8,128)}, f32[128,256]{1,0:T(8,128)}, bf16[192,2048]{1,0:T(8,128)(2,1)}, bf16[192,2048]{1,0:...) custom-call(bf16[128,2048]{1,0:T(8,128)(2,1)} %inputs_ref.3, ...), custom_call_target="tpu_custom_call" | custom-call | flops 70000001024 | bytes 100000000 | tf_op jit(solution)/shard_map/forward/pallas_call | solution.py:1320
  91.0 81.8 %gather_select.1 = (bf16[2,192,2048]{2,1,0:T(8,128)(2,1)}, bf16[2,192,2048]{2,1,0:T(8,128)(2,1)}, bf16[3,96,2048]{2,1,0:T(8,128)(2,1)}, bf16[3,96,2048]{2,1,0:T(...) custom-call(bf16[128,2176]{1,0:T(8,128)(2,1)} %get-tuple-element.77., ...), custom_call_target="tpu_custom_call" | custom-call | flops 60000002048 | bytes 100000000 | tf_op jit(solution)/shard_map/gather_select/pallas_call | solution.py:580
  172.7 1.8 collective-permute-start.1
  174.5 0.0 collective-permute-start
  174.5 30.6 %first_expert.1 = (bf16[640,2048]{1,0:T(8,128)(2,1)}, bf16[640,2176]{1,0:T(8,128)(2,1)}, bf16[3,768,2048]{2,1,0:T(8,128)(2,1)}) custom-call(s32[1]{0:T(128)} %bitcast.7.expert_ref, bf16[640,2048]{1,0:T(8,128)(2,1)} %get-tuple-element.83.x, bf16[640,2048]{1,0:T(8,128)(2,1)} %get-tuple-element.84.d, f32[640,128]{1,0:T(8,128)} %get-tuple-element.85.gate, ...), custom_call_target="tpu_custom_call" | custom-call | flops 18119393280 | bytes 31981568 | tf_op jit(solution)/shard_map/first_expert/pallas_call | solution.py:1027
  205.1 2.5 collective-permute-done.1.refs_6_
  207.6 3.1 collective-permute-done.refs_4_
  210.7 44.3 %second_expert.1 = (bf16[640,2048]{1,0:T(8,128)(2,1)}, bf16[640,2176]{1,0:T(8,128)(2,1)}, bf16[3,768,2048]{2,1,0:T(8,128)(2,1)}, bf16[2,96,2048]{2,1,0:T(8,128)(2,1)}, bf16[2,96,2048]{2,1,0:T(8,128)(2,1)}) custom-call(s32[1]{0:T(128)S(6)} %add.32.expert_ref, bf16[640,2048]{1,0:T(8,128)(2,1)} %get-tuple-element.93.x, bf16[640,2048]{1,0:T(8,128)(2,1)} %get-tuple-element.94.d, ...), custom_call_target="tpu_custom_call" | custom-call | flops 18119393280 | bytes 31981568 | tf_op jit(solution)/shard_map/second_expert/pallas_call | solution.py:1027
  255.0 68.3 %combine_scatter.1 = (bf16[32,128,2048]{2,1,0:T(8,128)(2,1)}, bf16[3,96,2048]{2,1,0:T(8,128)(2,1)}, bf16[3,96,2048]{2,1,0:T(8,128)(2,1)}, bf16[1,96,2048]{2,1,0:...) custom-call(bf16[640,2176]{1,0:T(8,128)(2,1)} %get-tuple-element.92., ...), custom_call_target="tpu_custom_call" | custom-call | flops 60000002048 | bytes 100000000 | tf_op jit(solution)/shard_map/combine_scatter/pallas_call | solution.py:761
  323.3 0.0 reduce-scatter.2.cloned.1.call-update
  323.3 160.3 %backward.1 = (bf16[128,2048]{1,0:T(8,128)(2,1)}, f32[64,2048]{1,0:T(8,128)}, f32[8,2048]{1,0:T(8,128)}, bf16[2048,2304]{1,0:T(8,128)(2,1)}, bf16[3,192,2048]{2,...) custom-call(bf16[128,2048]{1,0:T(8,128)(2,1)} %get-tuple-element.106.gr, ...), custom_call_target="tpu_custom_call" | custom-call | flops 99999997952 | bytes 100000000 | tf_op jit(solution)/shard_map/backward/pallas_call | solution.py:1611
  483.6 0.0 copy-start
  483.6 3.7 copy-done
  487.3 0.0 copy-start.2
  487.3 0.0 copy-start.5
  487.3 0.0 copy-start.6
  487.3 8.7 %attention_grads.1 = (f32[1024,2048]{1,0:T(8,128)}, f32[2048,1024]{1,0:T(8,128)}, f32[2048,128]{1,0:T(8,128)}, f32[2048,128]{1,0:T(8,128)}) custom-call(bf16[2048,2304]{1,0:T(8,128)(2,1)S(1)} %copy-done), custom_call_target="tpu_custom_call" | custom-call | tf_op jit(solution)/shard_map/attention_grads/pallas_call | solution.py:1670
  496.0 0.0 copy-done.1
  496.0 0.0 copy-done.2
  496.0 0.0 copy-done.3
  496.0 0.0 copy-done.4
  496.0 0.0 copy-done.5
  496.0 0.0 copy-done.6
  496.0 0.0 copy-start.7
  496.0 9.0 %expert_grads.1 = (f32[2,192,2048]{2,1,0:T(8,128)}, f32[2,192,2048]{2,1,0:T(8,128)}, f32[2,192,2048]{2,1,0:T(8,128)}) custom-call(bf16[3,768,2048]{2,1,0:T(8,128)(2,1)} %get-tuple-element.100.refs_7_.gw_ref.own_a, bf16[3,96,2048]{2,1,0:T(8,128)(2,1)S(1)} %copy-done.1, bf16[3,96,2048]{2,1,0:T(8,128)(2,1)S(1)} %copy-done.2, ...), custom_call_target="tpu_custom_call" | custom-call | tf_op jit(solution)/shard_map/expert_grads/pallas_call | solution.py:1718
  505.0 1.3 slice_bitcast_fusion
  506.3 1.5 fusion.8
  507.9 0.0 copy-done.7
  507.9 1.9 add_convert_fusion
  509.8 0.0 copy-done.10
  509.8 0.8 copy.38
  510.6 0.0 copy-done.9
  510.6 0.8 copy.39
  (7 shorter events, 0.0 us)
Async XLA Ops:
  7.2 500.7 %reduce-scatter.2.cloned.1.call-start = ((), (), s32[]{:S(2)}) async-start(), calls=%async_computation.1 | async-start | bytes 17301504 | tf_op jit(solution)/shard_map/reduce_scatter | solution.py:1799
  7.3 3.3 copy-start.8
  8.2 3.3 copy-start.11
  9.2 2.3 slice-start
  172.7 34.8 %collective-permute-start.1 = (bf16[2,192,2048]{2,1,0:T(8,128)(2,1)S(1)}, bf16[2,192,2048]{2,1,0:T(8,128)(2,1)}, u32[]{:S(2)}, u32[]{:S(2)}) collective-permute-start(bf16[2,192,2048]{2,1,0:T(8,128)(2,1)S(1)} %pad_maximum_fusion), channel_id=1, source_target_pairs={{0,3},{1,0},{2,1},{3,2},{4,7},{5,4},{6,5},{7,6},{8,11},{9,8},{10,9... | collective-permute-start | bytes 4718600 | tf_op jit(solution)/shard_map/ppermute | solution.py:1730
  174.5 36.2 %collective-permute-start = (bf16[2,192,2048]{2,1,0:T(8,128)(2,1)S(1)}, bf16[2,192,2048]{2,1,0:T(8,128)(2,1)}, u32[]{:S(2)}, u32[]{:S(2)}) collective-permute-start(bf16[2,192,2048]{2,1,0:T(8,128)(2,1)S(1)} %pad_maximum_fusion), channel_id=1, source_target_pairs={{0,1},{1,2},{2,3},{3,0},{4,5},{5,6},{6,7},{7,4},{8,9},{9,10},{10,1... | collective-permute-start | bytes 4718600 | tf_op jit(solution)/shard_map/ppermute | solution.py:1730
  483.6 3.7 copy-start
  487.3 8.7 %copy-start.1 = (bf16[3,96,2048]{2,1,0:T(8,128)(2,1)S(1)}, bf16[3,96,2048]{2,1,0:T(8,128)(2,1)}, u32[]{:S(2)}) copy-start(bf16[3,96,2048]{2,1,0:T(8,128)(2,1)} %get-tuple-element.127.right_low) | copy-start | bytes 3538948
  487.3 8.7 %copy-start.2 = (bf16[3,96,2048]{2,1,0:T(8,128)(2,1)S(1)}, bf16[3,96,2048]{2,1,0:T(8,128)(2,1)}, u32[]{:S(2)}) copy-start(bf16[3,96,2048]{2,1,0:T(8,128)(2,1)} %get-tuple-element.128.left_high) | copy-start | bytes 3538948
  487.3 8.7 %copy-start.3 = (bf16[2,96,2048]{2,1,0:T(8,128)(2,1)S(1)}, bf16[2,96,2048]{2,1,0:T(8,128)(2,1)}, u32[]{:S(2)}) copy-start(bf16[2,96,2048]{2,1,0:T(8,128)(2,1)} %get-tuple-element.129.raw_right) | copy-start | bytes 2359300
  487.3 8.7 %copy-start.4 = (bf16[2,96,2048]{2,1,0:T(8,128)(2,1)S(1)}, bf16[2,96,2048]{2,1,0:T(8,128)(2,1)}, u32[]{:S(2)}) copy-start(bf16[2,96,2048]{2,1,0:T(8,128)(2,1)} %get-tuple-element.130.raw_left) | copy-start | bytes 2359300
  487.3 8.7 %copy-start.5 = (bf16[1,96,2048]{2,1,0:T(8,128)(2,1)S(1)}, bf16[1,96,2048]{2,1,0:T(8,128)(2,1)}, u32[]{:S(2)}) copy-start(bf16[1,96,2048]{2,1,0:T(8,128)(2,1)} %get-tuple-element.131.right_last) | copy-start | bytes 1179652
  487.3 8.7 %copy-start.6 = (bf16[1,96,2048]{2,1,0:T(8,128)(2,1)S(1)}, bf16[1,96,2048]{2,1,0:T(8,128)(2,1)}, u32[]{:S(2)}) copy-start(bf16[1,96,2048]{2,1,0:T(8,128)(2,1)} %get-tuple-element.132.left_last) | copy-start | bytes 1179652
  496.0 11.8 %copy-start.7 = (f32[128,2048]{1,0:T(8,128)S(1)}, f32[128,2048]{1,0:T(8,128)}, u32[]{:S(2)}) copy-start(f32[128,2048]{1,0:T(8,128)} %get-tuple-element.76.hidden_ref) | copy-start | bytes 3145732
  505.0 4.8 copy-start.10
  505.0 5.6 %copy-start.9 = (f32[64,2048]{1,0:T(8,128)S(1)}, f32[64,2048]{1,0:T(8,128)}, u32[]{:S(2)}) copy-start(f32[64,2048]{1,0:T(8,128)} %get-tuple-element.126) | copy-start | bytes 1572868
Sparse Core Ops, SparseCore 0:
  323.4 137.2 reduce-scatter.1
